TPU v7x, 32 devices: a whole 2x2x4 slice. The times are simulated.
32 devices in a mesh: chan: 4 (over z), lag: 4 (over x, core), seg: 2 (over y).
Axes of the slice: x: 2, y: 2, z: 4, core: 2. Of those that a mesh axis runs over, the one named last changes fastest.
Arguments:
- records_owned: float32 [512, 2, 1024], P('chan', 'seg', 'lag'), may hold values from -6 to 6
- section_list: int32 [512], replicated, may hold values from 0 to 511, as said below
- ref_index: int32 [64], replicated, may hold values from 0 to 511, as said below
Outputs:
- correlations: float32 [512, 8192], P(('chan', 'seg'), 'lag')
Inputs may be any that keep to these rules, and one draw needn't show every extreme that they name: `section_list`: each value names a channel once. The 128 rows of each owner name exactly 32 channels of every channel block (channels b*128 to (b+1)*128 - 1). `ref_index`: distinct channel numbers.
All inputs are finite; a program needn't handle non-finite values.
Results may differ from a plain program's by a relative error of at most 0.000098.
Values sent between devices are 32-bit elements; how exact they have to be, the bound alone decides.
No kernel may reach another device: no remote copies, remote signals or barrier semaphores. Data moves between devices by JAX's collectives and lax.ppermute only.
A program may use at most 64 MiB of HBM per device.

v0:
```python
import functools
import math

import jax
import jax.numpy as jnp
from jax import lax
from jax.experimental import pallas as pl
from jax.experimental.pallas import tpu as pltpu
from jax.sharding import PartitionSpec as P

LAGS = 128
SAMPLES = 2048
PHASES = 4
GROUPS = 4


def halves(value):
    high = value.astype(jnp.bfloat16)
    low = (value - high.astype(jnp.float32)).astype(jnp.bfloat16)
    return high, low


def product(left, right):
    return jnp.dot(left, right, preferred_element_type=jnp.float32)


def product_nt(left, right):
    return lax.dot_general(
        left, right, (((1,), (1,)), ((), ())), preferred_element_type=jnp.float32
    )


def steps(lags, segments):
    return [(lag, segment) for lag in range(lags) for segment in range(segments)]


def swapped(value, lag_step, segment_step):
    lags, segments = lax.axis_size("lag"), lax.axis_size("seg")
    pairs = [
        (lag * segments + segment, (lag ^ lag_step) * segments + (segment ^ segment_step))
        for lag, segment in steps(lags, segments)
    ]
    return lax.ppermute(value, ("lag", "seg"), pairs)


def across(value, step):
    return lax.ppermute(value, "chan", [(i, i ^ step) for i in range(lax.axis_size("chan"))])


def paired(value, order):
    lags = lax.axis_size("lag")
    pairs = [
        (chan * lags + lag, (chan ^ order[lag % 2]) * lags + lag)
        for chan in range(lax.axis_size("chan"))
        for lag in range(lags)
    ]
    return lax.ppermute(value, ("chan", "lag"), pairs)


def choice(pick, rows):
    high, low = halves(rows)
    return product(pick, high) + product(pick, low)


def counts_before(present):
    rows = present.shape[0]
    line = lax.broadcasted_iota(jnp.int32, (rows, rows), 0)
    lane = lax.broadcasted_iota(jnp.int32, (rows, rows), 1)
    return product((lane < line).astype(jnp.bfloat16), present.astype(jnp.bfloat16))


def columns(refs_ref, width):
    return jnp.broadcast_to(refs_ref[...], (width, refs_ref.shape[1])).T


def choose_four_kernel(
    records_ref,
    lists_ref,
    refs_ref,
    parts_ref,
    pick_ref,
    take_ref,
    held_ref,
    done,
):
    copy = pltpu.make_async_copy(records_ref, held_ref, done)
    copy.start()
    rows = lists_ref.shape[1]
    kept = take_ref.shape[1]
    refs = refs_ref.shape[1]
    me = lax.axis_index("chan")
    odd = lax.rem(lax.axis_index("lag"), 2)
    near, far = 1 + odd, 2 - odd
    line = lax.broadcasted_iota(jnp.int32, (rows, 2 * rows), 0)

    def pool(owner):
        lists = [lists_ref[pl.ds(lax.bitwise_xor(owner, i), 1), :] for i in (0, near)]
        return jnp.concatenate(lists, axis=1)

    def where(owner, block):
        return pool(owner) == line + block * rows

    def ranks(found):
        present = jnp.max(found.astype(jnp.float32), axis=1, keepdims=True)
        return present, counts_before(jnp.broadcast_to(present, (rows, rows)))

    other = lax.bitwise_xor(me, far)
    found = where(me, other)
    _, rank = ranks(found)
    rank = jnp.concatenate([rank, rank], axis=1)
    slot = jnp.sum(jnp.where(found, rank + 1.0, 0.0), axis=0, keepdims=True).astype(jnp.int32)
    send = jnp.concatenate([line[:kept] + 1 == slot, columns(refs_ref, 2 * rows) == pool(me)], axis=0)
    send = send.astype(jnp.bfloat16)
    keep = where(me, me).astype(jnp.bfloat16)
    picks = jnp.concatenate([send, keep], axis=0)
    own, arrived = picks[:, :rows], picks[:, rows:]
    pick_ref[...] = jnp.concatenate([own, own, arrived, arrived], axis=1)
    present, rank = ranks(where(other, me))
    lane = lax.broadcasted_iota(jnp.int32, (rows, kept), 1)
    slot = jnp.where(present > 0.0, rank[:, :kept], -1.0).astype(jnp.int32)
    take_ref[...] = (lane == slot).astype(jnp.bfloat16)
    copy.wait()
    parts_ref[...] = jnp.concatenate(halves(held_ref[:, 0, :]), axis=0)


def pick_kernel(arrived_ref, pick_ref, parts_ref, sent_ref, base_ref):
    parts = jnp.concatenate([parts_ref[...], *halves(arrived_ref[:, 0, :])], axis=0)
    rows = product(pick_ref[...], parts)
    lines = sent_ref.shape[0]
    sent_ref[...] = rows[:lines]
    base_ref[...] = rows[lines:]


def put(series, panel, out_refs):
    segments = len(out_refs)
    kept = series.shape[0] // segments
    own = lax.axis_index("seg")
    for part in range(segments):
        half = lax.bitwise_xor(own, part)
        chosen = series[:kept]
        for other in range(1, segments):
            chosen = jnp.where(half == other, series[other * kept : (other + 1) * kept], chosen)
        out_refs[part][:kept, :] = chosen
        out_refs[part][kept:, :] = panel


def place_four_kernel(base_ref, take_ref, sent_ref, arrived_ref, *out_refs):
    kept = take_ref.shape[1]
    series = base_ref[...] + choice(take_ref[...], arrived_ref[:kept, :])
    put(series, sent_ref[kept:, :] + arrived_ref[kept:, :], out_refs)


def pack_kernel(records_ref, lists_ref, refs_ref, out_ref, panel_ref):
    rows = records_ref.shape[0]
    refs = refs_ref.shape[1]
    own = jnp.broadcast_to(lists_ref[pl.ds(lax.axis_index("chan"), 1), :], (rows, rows))
    rank = jnp.sum((own.T < own).astype(jnp.int32), axis=0, keepdims=True)
    line = lax.broadcasted_iota(jnp.int32, (rows, rows), 0)
    records = records_ref[:, 0, :]
    panel_ref[...] = choice((columns(refs_ref, rows) == own[:refs]).astype(jnp.bfloat16), records)
    out_ref[...] = choice((line == rank).astype(jnp.bfloat16), records)


def choose_kernel(peers, lists_ref, pick_ref):
    rows = lists_ref.shape[1]
    share = rows // peers
    lane = lax.broadcasted_iota(jnp.int32, (rows, rows), 1)
    channel = lax.broadcasted_iota(jnp.int32, (rows, rows), 0) + lax.axis_index("chan") * rows
    owner = jnp.zeros((rows, 1), jnp.int32)
    for peer in range(peers):
        found = (lists_ref[pl.ds(peer, 1), :] == channel).astype(jnp.int32)
        owner = owner + jnp.sum(found, axis=1, keepdims=True) * peer
    same = lane == owner
    before = counts_before(same.astype(jnp.float32))
    rank = jnp.sum(jnp.where(same, before, 0.0), axis=1, keepdims=True).astype(jnp.int32)
    pick_ref[...] = (lane == owner * share + rank).astype(jnp.bfloat16)


def place_kernel(pick_ref, panel_ref, arrived_ref, *out_refs):
    put(choice(pick_ref[...], arrived_ref[...]), panel_ref[...], out_refs)


def corr_kernel(refs, lag_width, *rest):
    *chunk_refs, out_ref, joined_ref, total_ref, done = rest
    kept = total_ref.shape[0]
    lags, segments = lax.axis_size("lag"), lax.axis_size("seg")
    width = chunk_refs[0].shape[1]
    for (lag_step, segment_step), chunk_ref in zip(steps(lags, segments), chunk_refs):
        lag = lax.bitwise_xor(lax.axis_index("lag"), lag_step)
        segment = lax.bitwise_xor(lax.axis_index("seg"), segment_step)
        start = pl.multiple_of((segment * lags + lag) * width, width)
        joined_ref[:, pl.ds(start, width)] = chunk_ref[...]
    series = joined_ref[:kept, :]
    panel = joined_ref[kept:, :]
    samples = panel.shape[1]
    terms = SAMPLES - LAGS
    times = lax.broadcasted_iota(jnp.int32, panel.shape, 1)
    panel = jnp.where(times < terms, panel, 0.0)
    series = pltpu.roll(series, samples - lax.axis_index("lag") * lag_width, 1)
    scale = 1.0 / math.sqrt(terms)
    columns = PHASES * refs
    each = lag_width // PHASES // GROUPS

    def shifted(value, shifts):
        parts = [pltpu.roll(value, shift % samples, 1) if shift else value for shift in shifts]
        return jnp.concatenate(parts, axis=0)

    panel_high, panel_low = (shifted(half, range(PHASES)) for half in halves(panel))
    series_high, series_low = halves(series)
    copies = []
    for group in range(GROUPS):
        shifts = [-PHASES * (group * each + i) for i in range(each)]
        high, low = shifted(series_high, shifts), shifted(series_low, shifts)
        lines = each * kept
        total = product_nt(jnp.concatenate([high, low], axis=0), panel_high)
        total = (total[:lines] + total[lines:] + product_nt(high, panel_low)) * scale
        for i in range(each):
            start = (group * each + i) * columns
            total_ref[:, start : start + columns] = total[i * kept : (i + 1) * kept]
        part = pl.ds(group * each * columns, each * columns)
        copies.append(pltpu.make_async_copy(total_ref.at[:, part], out_ref.at[:, part], done.at[group]))
        copies[-1].start()
    for copy in copies:
        copy.wait()


def shards(records_owned, section_list, ref_index):
    peers = lax.axis_size("chan")
    segments = lax.axis_size("seg")
    rows, _, samples = records_owned.shape
    refs = ref_index.shape[0]
    share = rows // peers
    kept = rows // segments
    lags = lax.axis_size("lag")
    lag_width = LAGS // lags
    lists = section_list.reshape(peers, rows)
    params = pltpu.CompilerParams(vmem_limit_bytes=48 * 1024 * 1024)
    wanted = ref_index.reshape(1, refs)

    def block(*shape, dtype=jnp.float32):
        return jax.ShapeDtypeStruct(shape, dtype)

    def call(kernel, name, shapes, *operands):
        return pl.pallas_call(kernel, out_shape=shapes, compiler_params=params, name=name)(*operands)

    shapes = [block(kept + refs, samples)] * segments
    if peers == 4:
        first = paired(records_owned, (1, 2))
        half = rows // 2
        whole = pl.BlockSpec(memory_space=pltpu.VMEM)
        parts, pick, take = pl.pallas_call(
            choose_four_kernel,
            out_shape=[
                block(2 * rows, samples, dtype=jnp.bfloat16),
                block(half + refs + rows, 4 * rows, dtype=jnp.bfloat16),
                block(rows, half, dtype=jnp.bfloat16),
            ],
            in_specs=[pl.BlockSpec(memory_space=pl.ANY), whole, whole],
            scratch_shapes=[pltpu.VMEM(records_owned.shape, jnp.float32), pltpu.SemaphoreType.DMA],
            compiler_params=params,
            name="choose",
        )(pltpu.with_memory_space_constraint(records_owned, pltpu.HBM), lists, wanted)
        results = [block(half + refs, samples), block(rows, samples)]
        sent, base = call(pick_kernel, "pick", results, first, pick, parts)
        placed = call(place_four_kernel, "place", shapes, base, take, sent, paired(sent, (2, 1)))
    else:
        packed, panel = call(
            pack_kernel,
            "pack",
            [block(rows, samples), block(refs, samples)],
            records_owned,
            lists,
            wanted,
        )
        blocks = packed.reshape(peers, share, samples)
        blocks = lax.all_to_all(blocks, "chan", split_axis=0, concat_axis=0, tiled=True)
        step = 1
        while step < peers:
            panel = panel + across(panel, step)
            step *= 2
        pick = call(
            functools.partial(choose_kernel, peers),
            "choose",
            block(rows, rows, dtype=jnp.bfloat16),
            lists,
        )
        placed = call(place_kernel, "place", shapes, pick, panel, blocks.reshape(rows, samples))
    held = {(0, 0): placed[0]}
    for lag_step in range(0, lags, 2):
        for segment_step in range(segments):
            if lag_step or segment_step:
                held[lag_step, segment_step] = swapped(placed[segment_step], lag_step, segment_step)
    for lag_step, segment_step in list(held):
        held[lag_step + 1, segment_step] = swapped(held[lag_step, segment_step], 1, 0)
    return pl.pallas_call(
        functools.partial(corr_kernel, refs, lag_width),
        out_shape=jax.ShapeDtypeStruct((kept, lag_width * refs), jnp.float32),
        out_specs=pl.BlockSpec(memory_space=pl.ANY),
        scratch_shapes=[
            pltpu.VMEM((kept + refs, lags * segments * samples), jnp.float32),
            pltpu.VMEM((kept, lag_width * refs), jnp.float32),
            pltpu.SemaphoreType.DMA((GROUPS,)),
        ],
        compiler_params=params,
        name="correlate",
    )(*[held[step] for step in steps(lags, segments)])


def solution(mesh):
    return jax.shard_map(
        shards,
        mesh=mesh,
        in_specs=(P("chan", "seg", "lag"), P(), P()),
        out_specs=P(("chan", "seg"), "lag"),
        check_vma=False,
    )
```

profile of v0, /device:TPU:0, one launch (start us, length us, event | category | flops | bytes accessed | tf_op | source)
XLA Modules:
  0.0 27.6 jit_solution(10870240072357120951)
XLA Ops:
  0.0 0.0 copy-start
  0.0 3.0 %collective-permute-start = (f32[128,1,256]{2,1,0:T(1,128)}, f32[128,1,256]{2,1,0:T(1,128)S(1)}, u32[]{:S(2)}, u32[]{:S(2)}) collective-permute-start(f32[128,1,256]{2,1,0:T(1,128)} %records_ref.1), channel_id=1, source_target_pairs={{0,8},{2,18},{4,12},{6,22},{8,0},{10,26},{12,4},{14,30},{16,24},{1... | collective-permute-start | bytes 393224 | tf_op jit(solution)/shard_map/ppermute | solution.py:57
  3.0 0.0 copy-start.1
  3.0 0.0 copy-done
  3.0 0.7 %copy-done.1 = s32[64]{0:T(128)S(1)} copy-done((s32[64]{0:T(128)S(1)}, s32[64]{0:T(128)}, u32[]{:S(2)}) %copy-start.1) | copy-done | bytes 280
  3.7 1.3 %choose.1 = (bf16[256,256]{1,0:T(8,128)(2,1)S(1)}, bf16[256,512]{1,0:T(8,128)(2,1)S(1)}, bf16[128,64]{1,0:T(8,128)(2,1)S(1)}) custom-call(f32[128,1,256]{2,1,0:T(1,128)} %records_ref.1, s32[4,128]{1,0:T(4,128)S(1)} %bitcast.2, s32[1,64]{1,0:T(1,128)S(1)} %bitcast.3), custom_call_target="tpu_custom_call" | custom-call | tf_op jit(solution)/shard_map/choose/pallas_call | solution.py:251
  5.0 2.3 %collective-permute-done.arrived_ref = f32[128,1,256]{2,1,0:T(1,128)S(1)} collective-permute-done((f32[128,1,256]{2,1,0:T(1,128)}, f32[128,1,256]{2,1,0:T(1,128)S(1)}, u32[]{:S(2)}, u32[]{:S(2)}) %collective-permute-start) | collective-permute-done | bytes 131104 | tf_op jit(solution)/shard_map/ppermute | solution.py:57
  7.3 0.6 %pick.1 = (f32[128,256]{1,0:T(8,128)S(1)}, f32[128,256]{1,0:T(8,128)S(1)}) custom-call(f32[128,1,256]{2,1,0:T(1,128)S(1)} %collective-permute-done.arrived_ref, bf16[256,512]{1,0:T(8,128)(2,1)S(1)} %get-tuple-element.12.pick_ref, bf16[256,256]{1,0:T(8,128)(2,1)S(1)} %get-tuple-element.13.parts_ref), custom_call_target="tpu_custom_call" | custom-call | tf_op jit(solution)/shard_map/pick/pallas_call | solution.py:244
  7.9 2.4 %collective-permute-start.1 = (f32[128,256]{1,0:T(8,128)S(1)}, f32[128,256]{1,0:T(8,128)S(1)}, u32[]{:S(2)}, u32[]{:S(2)}) collective-permute-start(f32[128,256]{1,0:T(8,128)S(1)} %get-tuple-element.16.sent_ref), channel_id=1, source_target_pairs={{0,16},{2,10},{4,20},{6,14},{8,24},{10,2},{12,28},{14,6},{16,0},{1... | collective-permute-start | bytes 393224 | tf_op jit(solution)/shard_map/ppermute | solution.py:57
  10.3 3.5 %collective-permute-done.1.arrived_ref = f32[128,256]{1,0:T(8,128)S(1)} collective-permute-done((f32[128,256]{1,0:T(8,128)S(1)}, f32[128,256]{1,0:T(8,128)S(1)}, u32[]{:S(2)}, u32[]{:S(2)}) %collective-permute-start.1) | collective-permute-done | bytes 131104 | tf_op jit(solution)/shard_map/ppermute | solution.py:57
  13.8 0.2 place.1
  14.0 2.9 %collective-permute-start.6 = (f32[128,256]{1,0:T(8,128)S(1)}, f32[128,256]{1,0:T(8,128)S(1)}, u32[]{:S(2)}, u32[]{:S(2)}) collective-permute-start(f32[128,256]{1,0:T(8,128)S(1)} %get-tuple-element.18), channel_id=1, source_target_pairs={{0,5},{1,4},{2,7},{3,6},{4,1},{5,0},{6,3},{7,2},{8,13},{9,12},{10,... | collective-permute-start | bytes 393224 | tf_op jit(solution)/shard_map/ppermute | solution.py:43
  16.9 0.5 %collective-permute-start.2 = (f32[128,256]{1,0:T(8,128)S(1)}, f32[128,256]{1,0:T(8,128)S(1)}, u32[]{:S(2)}, u32[]{:S(2)}) collective-permute-start(f32[128,256]{1,0:T(8,128)S(1)} %get-tuple-element.18), channel_id=1, source_target_pairs={{0,1},{1,0},{2,3},{3,2},{4,5},{5,4},{6,7},{7,6},{8,9},{9,8},{10,11... | collective-permute-start | bytes 393224 | tf_op jit(solution)/shard_map/ppermute | solution.py:43
  17.4 0.2 collective-permute-start.5
  17.6 0.0 collective-permute-start.3
  17.6 3.6 %collective-permute-done.6.rest_5_ = f32[128,256]{1,0:T(8,128)S(1)} collective-permute-done((f32[128,256]{1,0:T(8,128)S(1)}, f32[128,256]{1,0:T(8,128)S(1)}, u32[]{:S(2)}, u32[]{:S(2)}) %collective-permute-start.6) | collective-permute-done | bytes 131104 | tf_op jit(solution)/shard_map/ppermute | solution.py:43
  21.2 0.0 collective-permute-start.8
  21.2 1.1 %collective-permute-done.2.rest_1_ = f32[128,256]{1,0:T(8,128)S(1)} collective-permute-done((f32[128,256]{1,0:T(8,128)S(1)}, f32[128,256]{1,0:T(8,128)S(1)}, u32[]{:S(2)}, u32[]{:S(2)}) %collective-permute-start.2) | collective-permute-done | bytes 131104 | tf_op jit(solution)/shard_map/ppermute | solution.py:43
  22.3 0.0 collective-permute-start.4
  22.3 0.1 collective-permute-done.5.rest_4_
  22.4 0.5 %collective-permute-start.7 = (f32[128,256]{1,0:T(8,128)S(1)}, f32[128,256]{1,0:T(8,128)S(1)}, u32[]{:S(2)}, u32[]{:S(2)}) collective-permute-start(f32[128,256]{1,0:T(8,128)S(1)} %collective-permute-done.5.rest_4_), channel_id=1, source_target_pairs={{0,2},{1,3},{2,0},{3,1},{4,6},{5,7},{6,4},{7,5},{8,10},{9,11},{10,... | collective-permute-start | bytes 393224 | tf_op jit(solution)/shard_map/ppermute | solution.py:43
  22.8 0.0 collective-permute-done.3.rest_2_
  22.8 0.0 collective-permute-done.8.rest_7_
  22.8 0.8 %collective-permute-done.4.rest_3_ = f32[128,256]{1,0:T(8,128)S(1)} collective-permute-done((f32[128,256]{1,0:T(8,128)S(1)}, f32[128,256]{1,0:T(8,128)S(1)}, u32[]{:S(2)}, u32[]{:S(2)}) %collective-permute-start.4) | collective-permute-done | bytes 131104 | tf_op jit(solution)/shard_map/ppermute | solution.py:43
  23.6 0.2 collective-permute-done.7.rest_6_
  23.8 3.7 %correlate.1 = f32[64,2048]{1,0:T(8,128)} custom-call(f32[128,256]{1,0:T(8,128)S(1)} %get-tuple-element.17.rest_0_, f32[128,256]{1,0:T(8,128)S(1)} %collective-permute-done.2.rest_1_, f32[128,256]{1,0:T(8,128)S(1)} %collective-permute-done.3.rest_2_, f32[128,256]{1,0:T(8,128)S(1)} %collective-permute-done.4.rest_3_, ...), custom_call_target="tpu_custom_call" | custom-call | tf_op jit(solution)/shard_map/correlate/pallas_call | solution.py:295
Async XLA Ops:
  0.0 3.0 %copy-start = (s32[512]{0:T(512)S(1)}, s32[512]{0:T(512)}, u32[]{:S(2)}) copy-start(s32[512]{0:T(512)} %param.4) | copy-start | bytes 6148
  0.0 7.3 %collective-permute-start = (f32[128,1,256]{2,1,0:T(1,128)}, f32[128,1,256]{2,1,0:T(1,128)S(1)}, u32[]{:S(2)}, u32[]{:S(2)}) collective-permute-start(f32[128,1,256]{2,1,0:T(1,128)} %records_ref.1), channel_id=1, source_target_pairs={{0,8},{2,18},{4,12},{6,22},{8,0},{10,26},{12,4},{14,30},{16,24},{1... | collective-permute-start | bytes 393224 | tf_op jit(solution)/shard_map/ppermute | solution.py:57
  3.0 0.7 %copy-start.1 = (s32[64]{0:T(128)S(1)}, s32[64]{0:T(128)}, u32[]{:S(2)}) copy-start(s32[64]{0:T(128)} %param.5) | copy-start | bytes 772
  7.9 5.9 %collective-permute-start.1 = (f32[128,256]{1,0:T(8,128)S(1)}, f32[128,256]{1,0:T(8,128)S(1)}, u32[]{:S(2)}, u32[]{:S(2)}) collective-permute-start(f32[128,256]{1,0:T(8,128)S(1)} %get-tuple-element.16.sent_ref), channel_id=1, source_target_pairs={{0,16},{2,10},{4,20},{6,14},{8,24},{10,2},{12,28},{14,6},{16,0},{1... | collective-permute-start | bytes 393224 | tf_op jit(solution)/shard_map/ppermute | solution.py:57
  14.0 7.2 %collective-permute-start.6 = (f32[128,256]{1,0:T(8,128)S(1)}, f32[128,256]{1,0:T(8,128)S(1)}, u32[]{:S(2)}, u32[]{:S(2)}) collective-permute-start(f32[128,256]{1,0:T(8,128)S(1)} %get-tuple-element.18), channel_id=1, source_target_pairs={{0,5},{1,4},{2,7},{3,6},{4,1},{5,0},{6,3},{7,2},{8,13},{9,12},{10,... | collective-permute-start | bytes 393224 | tf_op jit(solution)/shard_map/ppermute | solution.py:43
  16.9 5.4 %collective-permute-start.2 = (f32[128,256]{1,0:T(8,128)S(1)}, f32[128,256]{1,0:T(8,128)S(1)}, u32[]{:S(2)}, u32[]{:S(2)}) collective-permute-start(f32[128,256]{1,0:T(8,128)S(1)} %get-tuple-element.18), channel_id=1, source_target_pairs={{0,1},{1,0},{2,3},{3,2},{4,5},{5,4},{6,7},{7,6},{8,9},{9,8},{10,11... | collective-permute-start | bytes 393224 | tf_op jit(solution)/shard_map/ppermute | solution.py:43
  17.4 5.0 %collective-permute-start.5 = (f32[128,256]{1,0:T(8,128)S(1)}, f32[128,256]{1,0:T(8,128)S(1)}, u32[]{:S(2)}, u32[]{:S(2)}) collective-permute-start(f32[128,256]{1,0:T(8,128)S(1)} %get-tuple-element.17.rest_0_), channel_id=1, source_target_pairs={{0,4},{1,5},{2,6},{3,7},{4,0},{5,1},{6,2},{7,3},{8,12},{9,13},{10,... | collective-permute-start | bytes 393224 | tf_op jit(solution)/shard_map/ppermute | solution.py:43
  17.6 5.3 %collective-permute-start.3 = (f32[128,256]{1,0:T(8,128)S(1)}, f32[128,256]{1,0:T(8,128)S(1)}, u32[]{:S(2)}, u32[]{:S(2)}) collective-permute-start(f32[128,256]{1,0:T(8,128)S(1)} %get-tuple-element.17.rest_0_), channel_id=1, source_target_pairs={{0,2},{1,3},{2,0},{3,1},{4,6},{5,7},{6,4},{7,5},{8,10},{9,11},{10,... | collective-permute-start | bytes 393224 | tf_op jit(solution)/shard_map/ppermute | solution.py:43
  21.2 1.6 %collective-permute-start.8 = (f32[128,256]{1,0:T(8,128)S(1)}, f32[128,256]{1,0:T(8,128)S(1)}, u32[]{:S(2)}, u32[]{:S(2)}) collective-permute-start(f32[128,256]{1,0:T(8,128)S(1)} %collective-permute-done.6.rest_5_), channel_id=1, source_target_pairs={{0,2},{1,3},{2,0},{3,1},{4,6},{5,7},{6,4},{7,5},{8,10},{9,11},{10,... | collective-permute-start | bytes 393224 | tf_op jit(solution)/shard_map/ppermute | solution.py:43
  22.3 1.3 %collective-permute-start.4 = (f32[128,256]{1,0:T(8,128)S(1)}, f32[128,256]{1,0:T(8,128)S(1)}, u32[]{:S(2)}, u32[]{:S(2)}) collective-permute-start(f32[128,256]{1,0:T(8,128)S(1)} %collective-permute-done.2.rest_1_), channel_id=1, source_target_pairs={{0,2},{1,3},{2,0},{3,1},{4,6},{5,7},{6,4},{7,5},{8,10},{9,11},{10,... | collective-permute-start | bytes 393224 | tf_op jit(solution)/shard_map/ppermute | solution.py:43
  22.4 1.5 %collective-permute-start.7 = (f32[128,256]{1,0:T(8,128)S(1)}, f32[128,256]{1,0:T(8,128)S(1)}, u32[]{:S(2)}, u32[]{:S(2)}) collective-permute-start(f32[128,256]{1,0:T(8,128)S(1)} %collective-permute-done.5.rest_4_), channel_id=1, source_target_pairs={{0,2},{1,3},{2,0},{3,1},{4,6},{5,7},{6,4},{7,5},{8,10},{9,11},{10,... | collective-permute-start | bytes 393224 | tf_op jit(solution)/shard_map/ppermute | solution.py:43
where the time goes:
time: 27.7 us; the launch traced here: 27.6 us
  waiting for transfers between devices  11.6 us (42%)
  starting transfers between devices  9.42 us (34%)
  Pallas kernels  5.79 us (21%)
  local copies, waits for them, and re-layouts  0.66 us (2%)
    ppermute x2, waiting for transfers between devices, paired(): return lax.ppermute(value, ('chan', 'lag'), pairs)  5.84 us
    ppermute x7, waiting for transfers between devices, swapped(): return lax.ppermute(value, ('lag', 'seg'), pairs)  5.8 us
    ppermute x2, starting transfers between devices, paired(): return lax.ppermute(value, ('chan', 'lag'), pairs)  5.41 us
    ppermute x7, starting transfers between devices, swapped(): return lax.ppermute(value, ('lag', 'seg'), pairs)  4.02 us
    pallas_call x1, Pallas kernels, shards(): pl.pallas_call(functools.partial(corr_kernel, refs, lag_width), out_shape...  3.73 us
    pallas_call x1, Pallas kernels, shards(): pl.pallas_call(choose_four_kernel, out_shape=[block(2 * rows, samples, dt...  1.32 us
    pallas_call x2, Pallas kernels, call(): pl.pallas_call(kernel, out_shape=shapes, compiler_params=params, name=name)  0.75 us
    unnamed x4, local copies, waits for them, and re-layouts  0.66 us
  transfers between devices with their start and end apart: 9, of which 7 were waited for; matrix products, arithmetic and copies ran while one was open for 0% of the time, Pallas kernels for 5%

commit v1 on v0

--- a/solution.py
+++ b/solution.py
@@ -11,7 +11,8 @@
 LAGS = 128
 SAMPLES = 2048
 PHASES = 4
-GROUPS = 4
+PARTS = 2
+MARGIN = 128
 
 
 def halves(value):
@@ -77,8 +78,9 @@
     records_ref,
     lists_ref,
     refs_ref,
-    parts_ref,
-    pick_ref,
+    own_ref,
+    send_ref,
+    keep_ref,
     take_ref,
     held_ref,
     done,
@@ -112,23 +114,21 @@
     send = jnp.concatenate([line[:kept] + 1 == slot, columns(refs_ref, 2 * rows) == pool(me)], axis=0)
     send = send.astype(jnp.bfloat16)
     keep = where(me, me).astype(jnp.bfloat16)
-    picks = jnp.concatenate([send, keep], axis=0)
-    own, arrived = picks[:, :rows], picks[:, rows:]
-    pick_ref[...] = jnp.concatenate([own, own, arrived, arrived], axis=1)
+    send_ref[...] = send
+    keep_ref[...] = keep
     present, rank = ranks(where(other, me))
     lane = lax.broadcasted_iota(jnp.int32, (rows, kept), 1)
     slot = jnp.where(present > 0.0, rank[:, :kept], -1.0).astype(jnp.int32)
     take_ref[...] = (lane == slot).astype(jnp.bfloat16)
     copy.wait()
-    parts_ref[...] = jnp.concatenate(halves(held_ref[:, 0, :]), axis=0)
-
-
-def pick_kernel(arrived_ref, pick_ref, parts_ref, sent_ref, base_ref):
-    parts = jnp.concatenate([parts_ref[...], *halves(arrived_ref[:, 0, :])], axis=0)
-    rows = product(pick_ref[...], parts)
-    lines = sent_ref.shape[0]
-    sent_ref[...] = rows[:lines]
-    base_ref[...] = rows[lines:]
+    own_ref[...] = held_ref[:, 0, :]
+
+
+def pick_kernel(own_ref, arrived_ref, send_ref, keep_ref, sent_ref, base_ref):
+    rows = jnp.concatenate([own_ref[...], arrived_ref[:, 0, :]], axis=0)
+    high, low = halves(rows)
+    sent_ref[...] = product(send_ref[...], high) + product(send_ref[...], low)
+    base_ref[...] = product(keep_ref[...], high) + product(keep_ref[...], low)
 
 
 def put(series, panel, out_refs):
@@ -181,8 +181,8 @@
 
 
 def corr_kernel(refs, lag_width, *rest):
-    *chunk_refs, out_ref, joined_ref, total_ref, done = rest
-    kept = total_ref.shape[0]
+    *chunk_refs, out_ref, joined_ref, total_ref = rest
+    kept = out_ref.shape[0]
     lags, segments = lax.axis_size("lag"), lax.axis_size("seg")
     width = chunk_refs[0].shape[1]
     for (lag_step, segment_step), chunk_ref in zip(steps(lags, segments), chunk_refs):
@@ -197,31 +197,37 @@
     times = lax.broadcasted_iota(jnp.int32, panel.shape, 1)
     panel = jnp.where(times < terms, panel, 0.0)
     series = pltpu.roll(series, samples - lax.axis_index("lag") * lag_width, 1)
+    groups = lag_width // PHASES
+    length = samples // PARTS
+
+    def shifted(value, shifts, first):
+        size = value.shape[1]
+        parts = [pltpu.roll(value, shift % size, 1) if shift else value for shift in shifts]
+        return jnp.concatenate([part[:, first : first + length] for part in parts], axis=0)
+
+    panel = jnp.concatenate([jnp.zeros((refs, MARGIN), jnp.float32), panel], axis=1)
+    series = jnp.concatenate([series, series[:, :MARGIN]], axis=1)
+    panel_parts, series_parts = halves(panel), halves(series)
+    lines = groups * kept
+    for part in range(PARTS):
+        window = slice(part * length, (part + 1) * length + MARGIN)
+        panel_high, panel_low = (
+            shifted(half[:, window], range(PHASES), MARGIN) for half in panel_parts
+        )
+        high, low = (
+            shifted(half[:, window], range(0, -lag_width, -PHASES), 0) for half in series_parts
+        )
+        total = product_nt(jnp.concatenate([high, low], axis=0), panel_high)
+        total = total[:lines] + total[lines:] + product_nt(high, panel_low)
+        total_ref[part] = total
     scale = 1.0 / math.sqrt(terms)
     columns = PHASES * refs
-    each = lag_width // PHASES // GROUPS
-
-    def shifted(value, shifts):
-        parts = [pltpu.roll(value, shift % samples, 1) if shift else value for shift in shifts]
-        return jnp.concatenate(parts, axis=0)
-
-    panel_high, panel_low = (shifted(half, range(PHASES)) for half in halves(panel))
-    series_high, series_low = halves(series)
-    copies = []
-    for group in range(GROUPS):
-        shifts = [-PHASES * (group * each + i) for i in range(each)]
-        high, low = shifted(series_high, shifts), shifted(series_low, shifts)
-        lines = each * kept
-        total = product_nt(jnp.concatenate([high, low], axis=0), panel_high)
-        total = (total[:lines] + total[lines:] + product_nt(high, panel_low)) * scale
-        for i in range(each):
-            start = (group * each + i) * columns
-            total_ref[:, start : start + columns] = total[i * kept : (i + 1) * kept]
-        part = pl.ds(group * each * columns, each * columns)
-        copies.append(pltpu.make_async_copy(total_ref.at[:, part], out_ref.at[:, part], done.at[group]))
-        copies[-1].start()
-    for copy in copies:
-        copy.wait()
+    for group in range(groups):
+        place = slice(group * kept, (group + 1) * kept)
+        total = total_ref[0, place, :]
+        for part in range(1, PARTS):
+            total = total + total_ref[part, place, :]
+        out_ref[:, group * columns : (group + 1) * columns] = total * scale
 
 
 def shards(records_owned, section_list, ref_index):
@@ -248,11 +254,12 @@
         first = paired(records_owned, (1, 2))
         half = rows // 2
         whole = pl.BlockSpec(memory_space=pltpu.VMEM)
-        parts, pick, take = pl.pallas_call(
+        own, send, keep, take = pl.pallas_call(
             choose_four_kernel,
             out_shape=[
-                block(2 * rows, samples, dtype=jnp.bfloat16),
-                block(half + refs + rows, 4 * rows, dtype=jnp.bfloat16),
+                block(rows, samples),
+                block(half + refs, 2 * rows, dtype=jnp.bfloat16),
+                block(rows, 2 * rows, dtype=jnp.bfloat16),
                 block(rows, half, dtype=jnp.bfloat16),
             ],
             in_specs=[pl.BlockSpec(memory_space=pl.ANY), whole, whole],
@@ -261,7 +268,7 @@
             name="choose",
         )(pltpu.with_memory_space_constraint(records_owned, pltpu.HBM), lists, wanted)
         results = [block(half + refs, samples), block(rows, samples)]
-        sent, base = call(pick_kernel, "pick", results, first, pick, parts)
+        sent, base = call(pick_kernel, "pick", results, own, first, send, keep)
         placed = call(place_four_kernel, "place", shapes, base, take, sent, paired(sent, (2, 1)))
     else:
         packed, panel = call(
@@ -295,11 +302,9 @@
     return pl.pallas_call(
         functools.partial(corr_kernel, refs, lag_width),
         out_shape=jax.ShapeDtypeStruct((kept, lag_width * refs), jnp.float32),
-        out_specs=pl.BlockSpec(memory_space=pl.ANY),
         scratch_shapes=[
             pltpu.VMEM((kept + refs, lags * segments * samples), jnp.float32),
-            pltpu.VMEM((kept, lag_width * refs), jnp.float32),
-            pltpu.SemaphoreType.DMA((GROUPS,)),
+            pltpu.VMEM((PARTS, lag_width // PHASES * kept, PHASES * refs), jnp.float32),
         ],
         compiler_params=params,
         name="correlate",

time: 27.7 us -> 26.7 us (0.964)
  Pallas kernels: 5.79 us -> 4.45 us
  waiting for transfers between devices: 11.6 us -> 12 us
    pallas_call x1, Pallas kernels: 3.73 us -> 3.06 us  [shards(): pl.pallas_call(functools.partial(corr_kernel, refs, lag_width), out_shape...]
    pallas_call x1, Pallas kernels: 1.32 us -> 0.96 us  [shards(): pl.pallas_call(choose_four_kernel, out_shape=[block(rows, samples), block...]
    ppermute x2, waiting for transfers between devices: 5.84 us -> 6.21 us  [paired(): return lax.ppermute(value, ('chan', 'lag'), pairs)]
    pallas_call x2, Pallas kernels: 0.75 us -> 0.43 us  [call(): pl.pallas_call(kernel, out_shape=shapes, compiler_params=params, name=name)]
  transfers between devices with their start and end apart: 9 -> 9, of which waited for: 7 -> 7; matrix products, arithmetic and copies ran while one was open for 0% -> 0% of each run, Pallas kernels for 5% -> 4%
where the time goes in v1:
time: 26.7 us; the launch traced here: 26.6 us
  waiting for transfers between devices  12 us (45%)
  starting transfers between devices  9.43 us (35%)
  Pallas kernels  4.45 us (17%)
  local copies, waits for them, and re-layouts  0.66 us (2%)
    ppermute x2, waiting for transfers between devices, paired(): return lax.ppermute(value, ('chan', 'lag'), pairs)  6.21 us
    ppermute x7, waiting for transfers between devices, swapped(): return lax.ppermute(value, ('lag', 'seg'), pairs)  5.81 us
    ppermute x2, starting transfers between devices, paired(): return lax.ppermute(value, ('chan', 'lag'), pairs)  5.41 us
    ppermute x7, starting transfers between devices, swapped(): return lax.ppermute(value, ('lag', 'seg'), pairs)  4.02 us
    pallas_call x1, Pallas kernels, shards(): pl.pallas_call(functools.partial(corr_kernel, refs, lag_width), out_shape...  3.06 us
    pallas_call x1, Pallas kernels, shards(): pl.pallas_call(choose_four_kernel, out_shape=[block(rows, samples), block...  0.96 us
    unnamed x4, local copies, waits for them, and re-layouts  0.66 us
  transfers between devices with their start and end apart: 9, of which 7 were waited for; matrix products, arithmetic and copies ran while one was open for 0% of the time, Pallas kernels for 4%

profile of v1, /device:TPU:0, one launch (start us, length us, event | category | flops | bytes accessed | tf_op | source)
XLA Modules:
  0.0 26.6 jit_solution(127747827349800340)
XLA Ops:
  0.0 0.0 copy-start
  0.0 3.0 %collective-permute-start = (f32[128,1,256]{2,1,0:T(1,128)}, f32[128,1,256]{2,1,0:T(1,128)S(1)}, u32[]{:S(2)}, u32[]{:S(2)}) collective-permute-start(f32[128,1,256]{2,1,0:T(1,128)} %records_ref.1), channel_id=1, source_target_pairs={{0,8},{2,18},{4,12},{6,22},{8,0},{10,26},{12,4},{14,30},{16,24},{1... | collective-permute-start | bytes 393224 | tf_op jit(solution)/shard_map/ppermute | solution.py:58
  3.0 0.0 copy-start.1
  3.0 0.0 copy-done
  3.0 0.7 %copy-done.1 = s32[64]{0:T(128)S(1)} copy-done((s32[64]{0:T(128)S(1)}, s32[64]{0:T(128)}, u32[]{:S(2)}) %copy-start.1) | copy-done | bytes 280
  3.7 1.0 %choose.1 = (f32[128,256]{1,0:T(8,128)S(1)}, bf16[128,256]{1,0:T(8,128)(2,1)S(1)}, bf16[128,256]{1,0:T(8,128)(2,1)S(1)}, bf16[128,64]{1,0:T(8,128)(2,1)S(1)}) custom-call(f32[128,1,256]{2,1,0:T(1,128)} %records_ref.1, s32[4,128]{1,0:T(4,128)S(1)} %bitcast.2, s32[1,64]{1,0:T(1,128)S(1)} %bitcast.3), custom_call_target="tpu_custom_call" | custom-call | tf_op jit(solution)/shard_map/choose/pallas_call | solution.py:257
  4.6 2.7 %collective-permute-done.arrived_ref = f32[128,1,256]{2,1,0:T(1,128)S(1)} collective-permute-done((f32[128,1,256]{2,1,0:T(1,128)}, f32[128,1,256]{2,1,0:T(1,128)S(1)}, u32[]{:S(2)}, u32[]{:S(2)}) %collective-permute-start) | collective-permute-done | bytes 131104 | tf_op jit(solution)/shard_map/ppermute | solution.py:58
  7.3 0.3 pick.1
  7.6 2.4 %collective-permute-start.1 = (f32[128,256]{1,0:T(8,128)S(1)}, f32[128,256]{1,0:T(8,128)S(1)}, u32[]{:S(2)}, u32[]{:S(2)}) collective-permute-start(f32[128,256]{1,0:T(8,128)S(1)} %get-tuple-element.18.sent_ref), channel_id=1, source_target_pairs={{0,16},{2,10},{4,20},{6,14},{8,24},{10,2},{12,28},{14,6},{16,0},{1... | collective-permute-start | bytes 393224 | tf_op jit(solution)/shard_map/ppermute | solution.py:58
  10.0 3.5 %collective-permute-done.1.arrived_ref = f32[128,256]{1,0:T(8,128)S(1)} collective-permute-done((f32[128,256]{1,0:T(8,128)S(1)}, f32[128,256]{1,0:T(8,128)S(1)}, u32[]{:S(2)}, u32[]{:S(2)}) %collective-permute-start.1) | collective-permute-done | bytes 131104 | tf_op jit(solution)/shard_map/ppermute | solution.py:58
  13.5 0.2 place.1
  13.7 2.9 %collective-permute-start.6 = (f32[128,256]{1,0:T(8,128)S(1)}, f32[128,256]{1,0:T(8,128)S(1)}, u32[]{:S(2)}, u32[]{:S(2)}) collective-permute-start(f32[128,256]{1,0:T(8,128)S(1)} %get-tuple-element.20), channel_id=1, source_target_pairs={{0,5},{1,4},{2,7},{3,6},{4,1},{5,0},{6,3},{7,2},{8,13},{9,12},{10,... | collective-permute-start | bytes 393224 | tf_op jit(solution)/shard_map/ppermute | solution.py:44
  16.6 0.5 %collective-permute-start.2 = (f32[128,256]{1,0:T(8,128)S(1)}, f32[128,256]{1,0:T(8,128)S(1)}, u32[]{:S(2)}, u32[]{:S(2)}) collective-permute-start(f32[128,256]{1,0:T(8,128)S(1)} %get-tuple-element.20), channel_id=1, source_target_pairs={{0,1},{1,0},{2,3},{3,2},{4,5},{5,4},{6,7},{7,6},{8,9},{9,8},{10,11... | collective-permute-start | bytes 393224 | tf_op jit(solution)/shard_map/ppermute | solution.py:44
  17.1 0.2 collective-permute-start.5
  17.2 0.0 collective-permute-start.3
  17.2 3.6 %collective-permute-done.6.rest_5_ = f32[128,256]{1,0:T(8,128)S(1)} collective-permute-done((f32[128,256]{1,0:T(8,128)S(1)}, f32[128,256]{1,0:T(8,128)S(1)}, u32[]{:S(2)}, u32[]{:S(2)}) %collective-permute-start.6) | collective-permute-done | bytes 131104 | tf_op jit(solution)/shard_map/ppermute | solution.py:44
  20.9 0.0 collective-permute-start.8
  20.9 1.1 %collective-permute-done.2.rest_1_ = f32[128,256]{1,0:T(8,128)S(1)} collective-permute-done((f32[128,256]{1,0:T(8,128)S(1)}, f32[128,256]{1,0:T(8,128)S(1)}, u32[]{:S(2)}, u32[]{:S(2)}) %collective-permute-start.2) | collective-permute-done | bytes 131104 | tf_op jit(solution)/shard_map/ppermute | solution.py:44
  22.0 0.0 collective-permute-start.4
  22.0 0.1 collective-permute-done.5.rest_4_
  22.0 0.5 %collective-permute-start.7 = (f32[128,256]{1,0:T(8,128)S(1)}, f32[128,256]{1,0:T(8,128)S(1)}, u32[]{:S(2)}, u32[]{:S(2)}) collective-permute-start(f32[128,256]{1,0:T(8,128)S(1)} %collective-permute-done.5.rest_4_), channel_id=1, source_target_pairs={{0,2},{1,3},{2,0},{3,1},{4,6},{5,7},{6,4},{7,5},{8,10},{9,11},{10,... | collective-permute-start | bytes 393224 | tf_op jit(solution)/shard_map/ppermute | solution.py:44
  22.5 0.0 collective-permute-done.3.rest_2_
  22.5 0.0 collective-permute-done.8.rest_7_
  22.5 0.8 %collective-permute-done.4.rest_3_ = f32[128,256]{1,0:T(8,128)S(1)} collective-permute-done((f32[128,256]{1,0:T(8,128)S(1)}, f32[128,256]{1,0:T(8,128)S(1)}, u32[]{:S(2)}, u32[]{:S(2)}) %collective-permute-start.4) | collective-permute-done | bytes 131104 | tf_op jit(solution)/shard_map/ppermute | solution.py:44
  23.3 0.2 collective-permute-done.7.rest_6_
  23.5 3.1 %correlate.1 = f32[64,2048]{1,0:T(8,128)} custom-call(f32[128,256]{1,0:T(8,128)S(1)} %get-tuple-element.19.rest_0_, f32[128,256]{1,0:T(8,128)S(1)} %collective-permute-done.2.rest_1_, f32[128,256]{1,0:T(8,128)S(1)} %collective-permute-done.3.rest_2_, f32[128,256]{1,0:T(8,128)S(1)} %collective-permute-done.4.rest_3_, ...), custom_call_target="tpu_custom_call" | custom-call | tf_op jit(solution)/shard_map/correlate/pallas_call | solution.py:302
Async XLA Ops:
  0.0 3.0 %copy-start = (s32[512]{0:T(512)S(1)}, s32[512]{0:T(512)}, u32[]{:S(2)}) copy-start(s32[512]{0:T(512)} %param.4) | copy-start | bytes 6148
  0.0 7.3 %collective-permute-start = (f32[128,1,256]{2,1,0:T(1,128)}, f32[128,1,256]{2,1,0:T(1,128)S(1)}, u32[]{:S(2)}, u32[]{:S(2)}) collective-permute-start(f32[128,1,256]{2,1,0:T(1,128)} %records_ref.1), channel_id=1, source_target_pairs={{0,8},{2,18},{4,12},{6,22},{8,0},{10,26},{12,4},{14,30},{16,24},{1... | collective-permute-start | bytes 393224 | tf_op jit(solution)/shard_map/ppermute | solution.py:58
  3.0 0.7 %copy-start.1 = (s32[64]{0:T(128)S(1)}, s32[64]{0:T(128)}, u32[]{:S(2)}) copy-start(s32[64]{0:T(128)} %param.5) | copy-start | bytes 772
  7.6 5.9 %collective-permute-start.1 = (f32[128,256]{1,0:T(8,128)S(1)}, f32[128,256]{1,0:T(8,128)S(1)}, u32[]{:S(2)}, u32[]{:S(2)}) collective-permute-start(f32[128,256]{1,0:T(8,128)S(1)} %get-tuple-element.18.sent_ref), channel_id=1, source_target_pairs={{0,16},{2,10},{4,20},{6,14},{8,24},{10,2},{12,28},{14,6},{16,0},{1... | collective-permute-start | bytes 393224 | tf_op jit(solution)/shard_map/ppermute | solution.py:58
  13.7 7.2 %collective-permute-start.6 = (f32[128,256]{1,0:T(8,128)S(1)}, f32[128,256]{1,0:T(8,128)S(1)}, u32[]{:S(2)}, u32[]{:S(2)}) collective-permute-start(f32[128,256]{1,0:T(8,128)S(1)} %get-tuple-element.20), channel_id=1, source_target_pairs={{0,5},{1,4},{2,7},{3,6},{4,1},{5,0},{6,3},{7,2},{8,13},{9,12},{10,... | collective-permute-start | bytes 393224 | tf_op jit(solution)/shard_map/ppermute | solution.py:44
  16.6 5.4 %collective-permute-start.2 = (f32[128,256]{1,0:T(8,128)S(1)}, f32[128,256]{1,0:T(8,128)S(1)}, u32[]{:S(2)}, u32[]{:S(2)}) collective-permute-start(f32[128,256]{1,0:T(8,128)S(1)} %get-tuple-element.20), channel_id=1, source_target_pairs={{0,1},{1,0},{2,3},{3,2},{4,5},{5,4},{6,7},{7,6},{8,9},{9,8},{10,11... | collective-permute-start | bytes 393224 | tf_op jit(solution)/shard_map/ppermute | solution.py:44
  17.1 5.0 %collective-permute-start.5 = (f32[128,256]{1,0:T(8,128)S(1)}, f32[128,256]{1,0:T(8,128)S(1)}, u32[]{:S(2)}, u32[]{:S(2)}) collective-permute-start(f32[128,256]{1,0:T(8,128)S(1)} %get-tuple-element.19.rest_0_), channel_id=1, source_target_pairs={{0,4},{1,5},{2,6},{3,7},{4,0},{5,1},{6,2},{7,3},{8,12},{9,13},{10,... | collective-permute-start | bytes 393224 | tf_op jit(solution)/shard_map/ppermute | solution.py:44
  17.2 5.3 %collective-permute-start.3 = (f32[128,256]{1,0:T(8,128)S(1)}, f32[128,256]{1,0:T(8,128)S(1)}, u32[]{:S(2)}, u32[]{:S(2)}) collective-permute-start(f32[128,256]{1,0:T(8,128)S(1)} %get-tuple-element.19.rest_0_), channel_id=1, source_target_pairs={{0,2},{1,3},{2,0},{3,1},{4,6},{5,7},{6,4},{7,5},{8,10},{9,11},{10,... | collective-permute-start | bytes 393224 | tf_op jit(solution)/shard_map/ppermute | solution.py:44
  20.9 1.6 %collective-permute-start.8 = (f32[128,256]{1,0:T(8,128)S(1)}, f32[128,256]{1,0:T(8,128)S(1)}, u32[]{:S(2)}, u32[]{:S(2)}) collective-permute-start(f32[128,256]{1,0:T(8,128)S(1)} %collective-permute-done.6.rest_5_), channel_id=1, source_target_pairs={{0,2},{1,3},{2,0},{3,1},{4,6},{5,7},{6,4},{7,5},{8,10},{9,11},{10,... | collective-permute-start | bytes 393224 | tf_op jit(solution)/shard_map/ppermute | solution.py:44
  22.0 1.3 %collective-permute-start.4 = (f32[128,256]{1,0:T(8,128)S(1)}, f32[128,256]{1,0:T(8,128)S(1)}, u32[]{:S(2)}, u32[]{:S(2)}) collective-permute-start(f32[128,256]{1,0:T(8,128)S(1)} %collective-permute-done.2.rest_1_), channel_id=1, source_target_pairs={{0,2},{1,3},{2,0},{3,1},{4,6},{5,7},{6,4},{7,5},{8,10},{9,11},{10,... | collective-permute-start | bytes 393224 | tf_op jit(solution)/shard_map/ppermute | solution.py:44
  22.0 1.5 %collective-permute-start.7 = (f32[128,256]{1,0:T(8,128)S(1)}, f32[128,256]{1,0:T(8,128)S(1)}, u32[]{:S(2)}, u32[]{:S(2)}) collective-permute-start(f32[128,256]{1,0:T(8,128)S(1)} %collective-permute-done.5.rest_4_), channel_id=1, source_target_pairs={{0,2},{1,3},{2,0},{3,1},{4,6},{5,7},{6,4},{7,5},{8,10},{9,11},{10,... | collective-permute-start | bytes 393224 | tf_op jit(solution)/shard_map/ppermute | solution.py:44

commit v2 on v1

--- a/solution.py
+++ b/solution.py
@@ -11,8 +11,6 @@
 LAGS = 128
 SAMPLES = 2048
 PHASES = 4
-PARTS = 2
-MARGIN = 128
 
 
 def halves(value):
@@ -181,7 +179,7 @@
 
 
 def corr_kernel(refs, lag_width, *rest):
-    *chunk_refs, out_ref, joined_ref, total_ref = rest
+    *chunk_refs, out_ref, joined_ref, series_ref, panel_ref = rest
     kept = out_ref.shape[0]
     lags, segments = lax.axis_size("lag"), lax.axis_size("seg")
     width = chunk_refs[0].shape[1]
@@ -198,36 +196,26 @@
     panel = jnp.where(times < terms, panel, 0.0)
     series = pltpu.roll(series, samples - lax.axis_index("lag") * lag_width, 1)
     groups = lag_width // PHASES
-    length = samples // PARTS
-
-    def shifted(value, shifts, first):
-        size = value.shape[1]
-        parts = [pltpu.roll(value, shift % size, 1) if shift else value for shift in shifts]
-        return jnp.concatenate([part[:, first : first + length] for part in parts], axis=0)
-
-    panel = jnp.concatenate([jnp.zeros((refs, MARGIN), jnp.float32), panel], axis=1)
-    series = jnp.concatenate([series, series[:, :MARGIN]], axis=1)
-    panel_parts, series_parts = halves(panel), halves(series)
-    lines = groups * kept
-    for part in range(PARTS):
-        window = slice(part * length, (part + 1) * length + MARGIN)
-        panel_high, panel_low = (
-            shifted(half[:, window], range(PHASES), MARGIN) for half in panel_parts
-        )
-        high, low = (
-            shifted(half[:, window], range(0, -lag_width, -PHASES), 0) for half in series_parts
-        )
-        total = product_nt(jnp.concatenate([high, low], axis=0), panel_high)
-        total = total[:lines] + total[lines:] + product_nt(high, panel_low)
-        total_ref[part] = total
-    scale = 1.0 / math.sqrt(terms)
-    columns = PHASES * refs
+
+    def spread(value, count, step, out_ref):
+        lines = value.shape[0]
+        for half, part in enumerate(halves(value)):
+            for i in range(count):
+                start = (half * count + i) * lines
+                out_ref[start : start + lines, :] = (
+                    pltpu.roll(part, (i * step) % samples, 1) if i else part
+                )
+
+    spread(panel, PHASES, 1, panel_ref)
+    spread(series, groups, -PHASES, series_ref)
+    lines, columns = groups * kept, PHASES * refs
+    upper = product_nt(series_ref[...], panel_ref[:columns, :])
+    lower = product_nt(series_ref[:lines, :], panel_ref[columns:, :])
+    total = (upper[:lines] + upper[lines:] + lower) * (1.0 / math.sqrt(terms))
     for group in range(groups):
-        place = slice(group * kept, (group + 1) * kept)
-        total = total_ref[0, place, :]
-        for part in range(1, PARTS):
-            total = total + total_ref[part, place, :]
-        out_ref[:, group * columns : (group + 1) * columns] = total * scale
+        out_ref[:, group * columns : (group + 1) * columns] = total[
+            group * kept : (group + 1) * kept
+        ]
 
 
 def shards(records_owned, section_list, ref_index):
@@ -304,7 +292,8 @@
         out_shape=jax.ShapeDtypeStruct((kept, lag_width * refs), jnp.float32),
         scratch_shapes=[
             pltpu.VMEM((kept + refs, lags * segments * samples), jnp.float32),
-            pltpu.VMEM((PARTS, lag_width // PHASES * kept, PHASES * refs), jnp.float32),
+            pltpu.VMEM((2 * lag_width // PHASES * kept, lags * segments * samples), jnp.bfloat16),
+            pltpu.VMEM((2 * PHASES * refs, lags * segments * samples), jnp.bfloat16),
         ],
         compiler_params=params,
         name="correlate",

time: 26.7 us -> 26.8 us (level)
  no operation moved by 1% of the time
where the time goes in v2:
time: 26.8 us; the launch traced here: 26.6 us
  waiting for transfers between devices  12 us (45%)
  starting transfers between devices  9.43 us (35%)
  Pallas kernels  4.5 us (17%)
  local copies, waits for them, and re-layouts  0.66 us (2%)
    ppermute x2, waiting for transfers between devices, paired(): return lax.ppermute(value, ('chan', 'lag'), pairs)  6.21 us
    ppermute x7, waiting for transfers between devices, swapped(): return lax.ppermute(value, ('lag', 'seg'), pairs)  5.81 us
    ppermute x2, starting transfers between devices, paired(): return lax.ppermute(value, ('chan', 'lag'), pairs)  5.41 us
    ppermute x7, starting transfers between devices, swapped(): return lax.ppermute(value, ('lag', 'seg'), pairs)  4.02 us
    pallas_call x1, Pallas kernels, shards(): pl.pallas_call(functools.partial(corr_kernel, refs, lag_width), out_shape...  3.11 us
    pallas_call x1, Pallas kernels, shards(): pl.pallas_call(choose_four_kernel, out_shape=[block(rows, samples), block...  0.96 us
    unnamed x4, local copies, waits for them, and re-layouts  0.66 us
  transfers between devices with their start and end apart: 9, of which 7 were waited for; matrix products, arithmetic and copies ran while one was open for 0% of the time, Pallas kernels for 4%

profile of v2, /device:TPU:0, one launch (start us, length us, event | category | flops | bytes accessed | tf_op | source)
XLA Modules:
  0.0 26.6 jit_solution(5657348904432657904)
XLA Ops:
  0.0 0.0 copy-start
  0.0 3.0 %collective-permute-start = (f32[128,1,256]{2,1,0:T(1,128)}, f32[128,1,256]{2,1,0:T(1,128)S(1)}, u32[]{:S(2)}, u32[]{:S(2)}) collective-permute-start(f32[128,1,256]{2,1,0:T(1,128)} %records_ref.1), channel_id=1, source_target_pairs={{0,8},{2,18},{4,12},{6,22},{8,0},{10,26},{12,4},{14,30},{16,24},{1... | collective-permute-start | bytes 393224 | tf_op jit(solution)/shard_map/ppermute | solution.py:56
  3.0 0.0 copy-start.1
  3.0 0.0 copy-done
  3.0 0.7 %copy-done.1 = s32[64]{0:T(128)S(1)} copy-done((s32[64]{0:T(128)S(1)}, s32[64]{0:T(128)}, u32[]{:S(2)}) %copy-start.1) | copy-done | bytes 280
  3.7 1.0 %choose.1 = (f32[128,256]{1,0:T(8,128)S(1)}, bf16[128,256]{1,0:T(8,128)(2,1)S(1)}, bf16[128,256]{1,0:T(8,128)(2,1)S(1)}, bf16[128,64]{1,0:T(8,128)(2,1)S(1)}) custom-call(f32[128,1,256]{2,1,0:T(1,128)} %records_ref.1, s32[4,128]{1,0:T(4,128)S(1)} %bitcast.2, s32[1,64]{1,0:T(1,128)S(1)} %bitcast.3), custom_call_target="tpu_custom_call" | custom-call | tf_op jit(solution)/shard_map/choose/pallas_call | solution.py:245
  4.6 2.7 %collective-permute-done.arrived_ref = f32[128,1,256]{2,1,0:T(1,128)S(1)} collective-permute-done((f32[128,1,256]{2,1,0:T(1,128)}, f32[128,1,256]{2,1,0:T(1,128)S(1)}, u32[]{:S(2)}, u32[]{:S(2)}) %collective-permute-start) | collective-permute-done | bytes 131104 | tf_op jit(solution)/shard_map/ppermute | solution.py:56
  7.3 0.3 pick.1
  7.6 2.4 %collective-permute-start.1 = (f32[128,256]{1,0:T(8,128)S(1)}, f32[128,256]{1,0:T(8,128)S(1)}, u32[]{:S(2)}, u32[]{:S(2)}) collective-permute-start(f32[128,256]{1,0:T(8,128)S(1)} %get-tuple-element.18.sent_ref), channel_id=1, source_target_pairs={{0,16},{2,10},{4,20},{6,14},{8,24},{10,2},{12,28},{14,6},{16,0},{1... | collective-permute-start | bytes 393224 | tf_op jit(solution)/shard_map/ppermute | solution.py:56
  10.0 3.5 %collective-permute-done.1.arrived_ref = f32[128,256]{1,0:T(8,128)S(1)} collective-permute-done((f32[128,256]{1,0:T(8,128)S(1)}, f32[128,256]{1,0:T(8,128)S(1)}, u32[]{:S(2)}, u32[]{:S(2)}) %collective-permute-start.1) | collective-permute-done | bytes 131104 | tf_op jit(solution)/shard_map/ppermute | solution.py:56
  13.5 0.2 place.1
  13.7 2.9 %collective-permute-start.6 = (f32[128,256]{1,0:T(8,128)S(1)}, f32[128,256]{1,0:T(8,128)S(1)}, u32[]{:S(2)}, u32[]{:S(2)}) collective-permute-start(f32[128,256]{1,0:T(8,128)S(1)} %get-tuple-element.20), channel_id=1, source_target_pairs={{0,5},{1,4},{2,7},{3,6},{4,1},{5,0},{6,3},{7,2},{8,13},{9,12},{10,... | collective-permute-start | bytes 393224 | tf_op jit(solution)/shard_map/ppermute | solution.py:42
  16.6 0.5 %collective-permute-start.2 = (f32[128,256]{1,0:T(8,128)S(1)}, f32[128,256]{1,0:T(8,128)S(1)}, u32[]{:S(2)}, u32[]{:S(2)}) collective-permute-start(f32[128,256]{1,0:T(8,128)S(1)} %get-tuple-element.20), channel_id=1, source_target_pairs={{0,1},{1,0},{2,3},{3,2},{4,5},{5,4},{6,7},{7,6},{8,9},{9,8},{10,11... | collective-permute-start | bytes 393224 | tf_op jit(solution)/shard_map/ppermute | solution.py:42
  17.1 0.2 collective-permute-start.5
  17.2 0.0 collective-permute-start.3
  17.2 3.6 %collective-permute-done.6.rest_5_ = f32[128,256]{1,0:T(8,128)S(1)} collective-permute-done((f32[128,256]{1,0:T(8,128)S(1)}, f32[128,256]{1,0:T(8,128)S(1)}, u32[]{:S(2)}, u32[]{:S(2)}) %collective-permute-start.6) | collective-permute-done | bytes 131104 | tf_op jit(solution)/shard_map/ppermute | solution.py:42
  20.9 0.0 collective-permute-start.8
  20.9 1.1 %collective-permute-done.2.rest_1_ = f32[128,256]{1,0:T(8,128)S(1)} collective-permute-done((f32[128,256]{1,0:T(8,128)S(1)}, f32[128,256]{1,0:T(8,128)S(1)}, u32[]{:S(2)}, u32[]{:S(2)}) %collective-permute-start.2) | collective-permute-done | bytes 131104 | tf_op jit(solution)/shard_map/ppermute | solution.py:42
  22.0 0.0 collective-permute-start.4
  22.0 0.1 collective-permute-done.5.rest_4_
  22.0 0.5 %collective-permute-start.7 = (f32[128,256]{1,0:T(8,128)S(1)}, f32[128,256]{1,0:T(8,128)S(1)}, u32[]{:S(2)}, u32[]{:S(2)}) collective-permute-start(f32[128,256]{1,0:T(8,128)S(1)} %collective-permute-done.5.rest_4_), channel_id=1, source_target_pairs={{0,2},{1,3},{2,0},{3,1},{4,6},{5,7},{6,4},{7,5},{8,10},{9,11},{10,... | collective-permute-start | bytes 393224 | tf_op jit(solution)/shard_map/ppermute | solution.py:42
  22.5 0.0 collective-permute-done.3.rest_2_
  22.5 0.0 collective-permute-done.8.rest_7_
  22.5 0.8 %collective-permute-done.4.rest_3_ = f32[128,256]{1,0:T(8,128)S(1)} collective-permute-done((f32[128,256]{1,0:T(8,128)S(1)}, f32[128,256]{1,0:T(8,128)S(1)}, u32[]{:S(2)}, u32[]{:S(2)}) %collective-permute-start.4) | collective-permute-done | bytes 131104 | tf_op jit(solution)/shard_map/ppermute | solution.py:42
  23.3 0.2 collective-permute-done.7.rest_6_
  23.5 3.1 %correlate.1 = f32[64,2048]{1,0:T(8,128)} custom-call(f32[128,256]{1,0:T(8,128)S(1)} %get-tuple-element.19.rest_0_, f32[128,256]{1,0:T(8,128)S(1)} %collective-permute-done.2.rest_1_, f32[128,256]{1,0:T(8,128)S(1)} %collective-permute-done.3.rest_2_, f32[128,256]{1,0:T(8,128)S(1)} %collective-permute-done.4.rest_3_, ...), custom_call_target="tpu_custom_call" | custom-call | tf_op jit(solution)/shard_map/correlate/pallas_call | solution.py:290
Async XLA Ops:
  0.0 3.0 %copy-start = (s32[512]{0:T(512)S(1)}, s32[512]{0:T(512)}, u32[]{:S(2)}) copy-start(s32[512]{0:T(512)} %param.4) | copy-start | bytes 6148
  0.0 7.3 %collective-permute-start = (f32[128,1,256]{2,1,0:T(1,128)}, f32[128,1,256]{2,1,0:T(1,128)S(1)}, u32[]{:S(2)}, u32[]{:S(2)}) collective-permute-start(f32[128,1,256]{2,1,0:T(1,128)} %records_ref.1), channel_id=1, source_target_pairs={{0,8},{2,18},{4,12},{6,22},{8,0},{10,26},{12,4},{14,30},{16,24},{1... | collective-permute-start | bytes 393224 | tf_op jit(solution)/shard_map/ppermute | solution.py:56
  3.0 0.7 %copy-start.1 = (s32[64]{0:T(128)S(1)}, s32[64]{0:T(128)}, u32[]{:S(2)}) copy-start(s32[64]{0:T(128)} %param.5) | copy-start | bytes 772
  7.6 5.9 %collective-permute-start.1 = (f32[128,256]{1,0:T(8,128)S(1)}, f32[128,256]{1,0:T(8,128)S(1)}, u32[]{:S(2)}, u32[]{:S(2)}) collective-permute-start(f32[128,256]{1,0:T(8,128)S(1)} %get-tuple-element.18.sent_ref), channel_id=1, source_target_pairs={{0,16},{2,10},{4,20},{6,14},{8,24},{10,2},{12,28},{14,6},{16,0},{1... | collective-permute-start | bytes 393224 | tf_op jit(solution)/shard_map/ppermute | solution.py:56
  13.7 7.2 %collective-permute-start.6 = (f32[128,256]{1,0:T(8,128)S(1)}, f32[128,256]{1,0:T(8,128)S(1)}, u32[]{:S(2)}, u32[]{:S(2)}) collective-permute-start(f32[128,256]{1,0:T(8,128)S(1)} %get-tuple-element.20), channel_id=1, source_target_pairs={{0,5},{1,4},{2,7},{3,6},{4,1},{5,0},{6,3},{7,2},{8,13},{9,12},{10,... | collective-permute-start | bytes 393224 | tf_op jit(solution)/shard_map/ppermute | solution.py:42
  16.6 5.4 %collective-permute-start.2 = (f32[128,256]{1,0:T(8,128)S(1)}, f32[128,256]{1,0:T(8,128)S(1)}, u32[]{:S(2)}, u32[]{:S(2)}) collective-permute-start(f32[128,256]{1,0:T(8,128)S(1)} %get-tuple-element.20), channel_id=1, source_target_pairs={{0,1},{1,0},{2,3},{3,2},{4,5},{5,4},{6,7},{7,6},{8,9},{9,8},{10,11... | collective-permute-start | bytes 393224 | tf_op jit(solution)/shard_map/ppermute | solution.py:42
  17.1 5.0 %collective-permute-start.5 = (f32[128,256]{1,0:T(8,128)S(1)}, f32[128,256]{1,0:T(8,128)S(1)}, u32[]{:S(2)}, u32[]{:S(2)}) collective-permute-start(f32[128,256]{1,0:T(8,128)S(1)} %get-tuple-element.19.rest_0_), channel_id=1, source_target_pairs={{0,4},{1,5},{2,6},{3,7},{4,0},{5,1},{6,2},{7,3},{8,12},{9,13},{10,... | collective-permute-start | bytes 393224 | tf_op jit(solution)/shard_map/ppermute | solution.py:42
  17.2 5.3 %collective-permute-start.3 = (f32[128,256]{1,0:T(8,128)S(1)}, f32[128,256]{1,0:T(8,128)S(1)}, u32[]{:S(2)}, u32[]{:S(2)}) collective-permute-start(f32[128,256]{1,0:T(8,128)S(1)} %get-tuple-element.19.rest_0_), channel_id=1, source_target_pairs={{0,2},{1,3},{2,0},{3,1},{4,6},{5,7},{6,4},{7,5},{8,10},{9,11},{10,... | collective-permute-start | bytes 393224 | tf_op jit(solution)/shard_map/ppermute | solution.py:42
  20.9 1.6 %collective-permute-start.8 = (f32[128,256]{1,0:T(8,128)S(1)}, f32[128,256]{1,0:T(8,128)S(1)}, u32[]{:S(2)}, u32[]{:S(2)}) collective-permute-start(f32[128,256]{1,0:T(8,128)S(1)} %collective-permute-done.6.rest_5_), channel_id=1, source_target_pairs={{0,2},{1,3},{2,0},{3,1},{4,6},{5,7},{6,4},{7,5},{8,10},{9,11},{10,... | collective-permute-start | bytes 393224 | tf_op jit(solution)/shard_map/ppermute | solution.py:42
  22.0 1.3 %collective-permute-start.4 = (f32[128,256]{1,0:T(8,128)S(1)}, f32[128,256]{1,0:T(8,128)S(1)}, u32[]{:S(2)}, u32[]{:S(2)}) collective-permute-start(f32[128,256]{1,0:T(8,128)S(1)} %collective-permute-done.2.rest_1_), channel_id=1, source_target_pairs={{0,2},{1,3},{2,0},{3,1},{4,6},{5,7},{6,4},{7,5},{8,10},{9,11},{10,... | collective-permute-start | bytes 393224 | tf_op jit(solution)/shard_map/ppermute | solution.py:42
  22.0 1.5 %collective-permute-start.7 = (f32[128,256]{1,0:T(8,128)S(1)}, f32[128,256]{1,0:T(8,128)S(1)}, u32[]{:S(2)}, u32[]{:S(2)}) collective-permute-start(f32[128,256]{1,0:T(8,128)S(1)} %collective-permute-done.5.rest_4_), channel_id=1, source_target_pairs={{0,2},{1,3},{2,0},{3,1},{4,6},{5,7},{6,4},{7,5},{8,10},{9,11},{10,... | collective-permute-start | bytes 393224 | tf_op jit(solution)/shard_map/ppermute | solution.py:42

commit v3 on v2

--- a/solution.py
+++ b/solution.py
@@ -11,6 +11,7 @@
 LAGS = 128
 SAMPLES = 2048
 PHASES = 4
+LAST = 2
 
 
 def halves(value):
@@ -179,8 +180,8 @@
 
 
 def corr_kernel(refs, lag_width, *rest):
-    *chunk_refs, out_ref, joined_ref, series_ref, panel_ref = rest
-    kept = out_ref.shape[0]
+    *chunk_refs, out_ref, joined_ref, series_ref, panel_ref, total_ref, done = rest
+    kept = total_ref.shape[0]
     lags, segments = lax.axis_size("lag"), lax.axis_size("seg")
     width = chunk_refs[0].shape[1]
     for (lag_step, segment_step), chunk_ref in zip(steps(lags, segments), chunk_refs):
@@ -197,25 +198,36 @@
     series = pltpu.roll(series, samples - lax.axis_index("lag") * lag_width, 1)
     groups = lag_width // PHASES
 
-    def spread(value, count, step, out_ref):
+    def spread(value, shifts, out_ref, base):
         lines = value.shape[0]
-        for half, part in enumerate(halves(value)):
-            for i in range(count):
-                start = (half * count + i) * lines
-                out_ref[start : start + lines, :] = (
-                    pltpu.roll(part, (i * step) % samples, 1) if i else part
+        for half in halves(value):
+            for shift in shifts:
+                out_ref[base : base + lines, :] = (
+                    pltpu.roll(half, shift % samples, 1) if shift else half
                 )
-
-    spread(panel, PHASES, 1, panel_ref)
-    spread(series, groups, -PHASES, series_ref)
-    lines, columns = groups * kept, PHASES * refs
-    upper = product_nt(series_ref[...], panel_ref[:columns, :])
-    lower = product_nt(series_ref[:lines, :], panel_ref[columns:, :])
-    total = (upper[:lines] + upper[lines:] + lower) * (1.0 / math.sqrt(terms))
-    for group in range(groups):
-        out_ref[:, group * columns : (group + 1) * columns] = total[
-            group * kept : (group + 1) * kept
-        ]
+                base += lines
+
+    spread(panel, range(PHASES), panel_ref, 0)
+    columns = PHASES * refs
+    copies = []
+    first = 0
+    for count in (groups - LAST, LAST):
+        base, lines = 2 * first * kept, count * kept
+        spread(series, range(-PHASES * first, -PHASES * (first + count), -PHASES), series_ref, base)
+        upper = product_nt(series_ref[base : base + 2 * lines, :], panel_ref[:columns, :])
+        lower = product_nt(series_ref[base : base + lines, :], panel_ref[columns:, :])
+        total = (upper[:lines] + upper[lines:] + lower) * (1.0 / math.sqrt(terms))
+        for i in range(count):
+            part = slice((first + i) * columns, (first + i + 1) * columns)
+            total_ref[:, part] = total[i * kept : (i + 1) * kept]
+            copy = pltpu.make_async_copy(
+                total_ref.at[:, part], out_ref.at[:, part], done.at[first + i]
+            )
+            copy.start()
+            copies.append(copy)
+        first += count
+    for copy in copies:
+        copy.wait()
 
 
 def shards(records_owned, section_list, ref_index):
@@ -290,10 +302,13 @@
     return pl.pallas_call(
         functools.partial(corr_kernel, refs, lag_width),
         out_shape=jax.ShapeDtypeStruct((kept, lag_width * refs), jnp.float32),
+        out_specs=pl.BlockSpec(memory_space=pl.ANY),
         scratch_shapes=[
             pltpu.VMEM((kept + refs, lags * segments * samples), jnp.float32),
             pltpu.VMEM((2 * lag_width // PHASES * kept, lags * segments * samples), jnp.bfloat16),
             pltpu.VMEM((2 * PHASES * refs, lags * segments * samples), jnp.bfloat16),
+            pltpu.VMEM((kept, lag_width * refs), jnp.float32),
+            pltpu.SemaphoreType.DMA((lag_width // PHASES,)),
         ],
         compiler_params=params,
         name="correlate",

time: 26.8 us -> 26.8 us (level)
  no operation moved by 1% of the time
where the time goes in v3:
time: 26.8 us; the launch traced here: 26.7 us
  waiting for transfers between devices  12 us (45%)
  starting transfers between devices  9.43 us (35%)
  Pallas kernels  4.56 us (17%)
  local copies, waits for them, and re-layouts  0.66 us (2%)
    ppermute x2, waiting for transfers between devices, paired(): return lax.ppermute(value, ('chan', 'lag'), pairs)  6.21 us
    ppermute x7, waiting for transfers between devices, swapped(): return lax.ppermute(value, ('lag', 'seg'), pairs)  5.81 us
    ppermute x2, starting transfers between devices, paired(): return lax.ppermute(value, ('chan', 'lag'), pairs)  5.41 us
    ppermute x7, starting transfers between devices, swapped(): return lax.ppermute(value, ('lag', 'seg'), pairs)  4.02 us
    pallas_call x1, Pallas kernels, shards(): pl.pallas_call(functools.partial(corr_kernel, refs, lag_width), out_shape...  3.17 us
    pallas_call x1, Pallas kernels, shards(): pl.pallas_call(choose_four_kernel, out_shape=[block(rows, samples), block...  0.96 us
    unnamed x4, local copies, waits for them, and re-layouts  0.66 us
  transfers between devices with their start and end apart: 9, of which 7 were waited for; matrix products, arithmetic and copies ran while one was open for 0% of the time, Pallas kernels for 4%

profile of v3, /device:TPU:0, one launch (start us, length us, event | category | flops | bytes accessed | tf_op | source)
XLA Modules:
  0.0 26.7 jit_solution(17189266777905650373)
XLA Ops:
  0.0 0.0 copy-start
  0.0 3.0 %collective-permute-start = (f32[128,1,256]{2,1,0:T(1,128)}, f32[128,1,256]{2,1,0:T(1,128)S(1)}, u32[]{:S(2)}, u32[]{:S(2)}) collective-permute-start(f32[128,1,256]{2,1,0:T(1,128)} %records_ref.1), channel_id=1, source_target_pairs={{0,8},{2,18},{4,12},{6,22},{8,0},{10,26},{12,4},{14,30},{16,24},{1... | collective-permute-start | bytes 393224 | tf_op jit(solution)/shard_map/ppermute | solution.py:57
  3.0 0.0 copy-start.1
  3.0 0.0 copy-done
  3.0 0.7 %copy-done.1 = s32[64]{0:T(128)S(1)} copy-done((s32[64]{0:T(128)S(1)}, s32[64]{0:T(128)}, u32[]{:S(2)}) %copy-start.1) | copy-done | bytes 280
  3.7 1.0 %choose.1 = (f32[128,256]{1,0:T(8,128)S(1)}, bf16[128,256]{1,0:T(8,128)(2,1)S(1)}, bf16[128,256]{1,0:T(8,128)(2,1)S(1)}, bf16[128,64]{1,0:T(8,128)(2,1)S(1)}) custom-call(f32[128,1,256]{2,1,0:T(1,128)} %records_ref.1, s32[4,128]{1,0:T(4,128)S(1)} %bitcast.2, s32[1,64]{1,0:T(1,128)S(1)} %bitcast.3), custom_call_target="tpu_custom_call" | custom-call | tf_op jit(solution)/shard_map/choose/pallas_call | solution.py:257
  4.6 2.7 %collective-permute-done.arrived_ref = f32[128,1,256]{2,1,0:T(1,128)S(1)} collective-permute-done((f32[128,1,256]{2,1,0:T(1,128)}, f32[128,1,256]{2,1,0:T(1,128)S(1)}, u32[]{:S(2)}, u32[]{:S(2)}) %collective-permute-start) | collective-permute-done | bytes 131104 | tf_op jit(solution)/shard_map/ppermute | solution.py:57
  7.3 0.3 pick.1
  7.6 2.4 %collective-permute-start.1 = (f32[128,256]{1,0:T(8,128)S(1)}, f32[128,256]{1,0:T(8,128)S(1)}, u32[]{:S(2)}, u32[]{:S(2)}) collective-permute-start(f32[128,256]{1,0:T(8,128)S(1)} %get-tuple-element.18.sent_ref), channel_id=1, source_target_pairs={{0,16},{2,10},{4,20},{6,14},{8,24},{10,2},{12,28},{14,6},{16,0},{1... | collective-permute-start | bytes 393224 | tf_op jit(solution)/shard_map/ppermute | solution.py:57
  10.0 3.5 %collective-permute-done.1.arrived_ref = f32[128,256]{1,0:T(8,128)S(1)} collective-permute-done((f32[128,256]{1,0:T(8,128)S(1)}, f32[128,256]{1,0:T(8,128)S(1)}, u32[]{:S(2)}, u32[]{:S(2)}) %collective-permute-start.1) | collective-permute-done | bytes 131104 | tf_op jit(solution)/shard_map/ppermute | solution.py:57
  13.5 0.2 place.1
  13.7 2.9 %collective-permute-start.6 = (f32[128,256]{1,0:T(8,128)S(1)}, f32[128,256]{1,0:T(8,128)S(1)}, u32[]{:S(2)}, u32[]{:S(2)}) collective-permute-start(f32[128,256]{1,0:T(8,128)S(1)} %get-tuple-element.20), channel_id=1, source_target_pairs={{0,5},{1,4},{2,7},{3,6},{4,1},{5,0},{6,3},{7,2},{8,13},{9,12},{10,... | collective-permute-start | bytes 393224 | tf_op jit(solution)/shard_map/ppermute | solution.py:43
  16.6 0.5 %collective-permute-start.2 = (f32[128,256]{1,0:T(8,128)S(1)}, f32[128,256]{1,0:T(8,128)S(1)}, u32[]{:S(2)}, u32[]{:S(2)}) collective-permute-start(f32[128,256]{1,0:T(8,128)S(1)} %get-tuple-element.20), channel_id=1, source_target_pairs={{0,1},{1,0},{2,3},{3,2},{4,5},{5,4},{6,7},{7,6},{8,9},{9,8},{10,11... | collective-permute-start | bytes 393224 | tf_op jit(solution)/shard_map/ppermute | solution.py:43
  17.1 0.2 collective-permute-start.5
  17.2 0.0 collective-permute-start.3
  17.2 3.6 %collective-permute-done.6.rest_5_ = f32[128,256]{1,0:T(8,128)S(1)} collective-permute-done((f32[128,256]{1,0:T(8,128)S(1)}, f32[128,256]{1,0:T(8,128)S(1)}, u32[]{:S(2)}, u32[]{:S(2)}) %collective-permute-start.6) | collective-permute-done | bytes 131104 | tf_op jit(solution)/shard_map/ppermute | solution.py:43
  20.9 0.0 collective-permute-start.8
  20.9 1.1 %collective-permute-done.2.rest_1_ = f32[128,256]{1,0:T(8,128)S(1)} collective-permute-done((f32[128,256]{1,0:T(8,128)S(1)}, f32[128,256]{1,0:T(8,128)S(1)}, u32[]{:S(2)}, u32[]{:S(2)}) %collective-permute-start.2) | collective-permute-done | bytes 131104 | tf_op jit(solution)/shard_map/ppermute | solution.py:43
  22.0 0.0 collective-permute-start.4
  22.0 0.1 collective-permute-done.5.rest_4_
  22.0 0.5 %collective-permute-start.7 = (f32[128,256]{1,0:T(8,128)S(1)}, f32[128,256]{1,0:T(8,128)S(1)}, u32[]{:S(2)}, u32[]{:S(2)}) collective-permute-start(f32[128,256]{1,0:T(8,128)S(1)} %collective-permute-done.5.rest_4_), channel_id=1, source_target_pairs={{0,2},{1,3},{2,0},{3,1},{4,6},{5,7},{6,4},{7,5},{8,10},{9,11},{10,... | collective-permute-start | bytes 393224 | tf_op jit(solution)/shard_map/ppermute | solution.py:43
  22.5 0.0 collective-permute-done.3.rest_2_
  22.5 0.0 collective-permute-done.8.rest_7_
  22.5 0.8 %collective-permute-done.4.rest_3_ = f32[128,256]{1,0:T(8,128)S(1)} collective-permute-done((f32[128,256]{1,0:T(8,128)S(1)}, f32[128,256]{1,0:T(8,128)S(1)}, u32[]{:S(2)}, u32[]{:S(2)}) %collective-permute-start.4) | collective-permute-done | bytes 131104 | tf_op jit(solution)/shard_map/ppermute | solution.py:43
  23.3 0.2 collective-permute-done.7.rest_6_
  23.5 3.2 %correlate.1 = f32[64,2048]{1,0:T(8,128)} custom-call(f32[128,256]{1,0:T(8,128)S(1)} %get-tuple-element.19.rest_0_, f32[128,256]{1,0:T(8,128)S(1)} %collective-permute-done.2.rest_1_, f32[128,256]{1,0:T(8,128)S(1)} %collective-permute-done.3.rest_2_, f32[128,256]{1,0:T(8,128)S(1)} %collective-permute-done.4.rest_3_, ...), custom_call_target="tpu_custom_call" | custom-call | tf_op jit(solution)/shard_map/correlate/pallas_call | solution.py:302
Async XLA Ops:
  0.0 3.0 %copy-start = (s32[512]{0:T(512)S(1)}, s32[512]{0:T(512)}, u32[]{:S(2)}) copy-start(s32[512]{0:T(512)} %param.4) | copy-start | bytes 6148
  0.0 7.3 %collective-permute-start = (f32[128,1,256]{2,1,0:T(1,128)}, f32[128,1,256]{2,1,0:T(1,128)S(1)}, u32[]{:S(2)}, u32[]{:S(2)}) collective-permute-start(f32[128,1,256]{2,1,0:T(1,128)} %records_ref.1), channel_id=1, source_target_pairs={{0,8},{2,18},{4,12},{6,22},{8,0},{10,26},{12,4},{14,30},{16,24},{1... | collective-permute-start | bytes 393224 | tf_op jit(solution)/shard_map/ppermute | solution.py:57
  3.0 0.7 %copy-start.1 = (s32[64]{0:T(128)S(1)}, s32[64]{0:T(128)}, u32[]{:S(2)}) copy-start(s32[64]{0:T(128)} %param.5) | copy-start | bytes 772
  7.6 5.9 %collective-permute-start.1 = (f32[128,256]{1,0:T(8,128)S(1)}, f32[128,256]{1,0:T(8,128)S(1)}, u32[]{:S(2)}, u32[]{:S(2)}) collective-permute-start(f32[128,256]{1,0:T(8,128)S(1)} %get-tuple-element.18.sent_ref), channel_id=1, source_target_pairs={{0,16},{2,10},{4,20},{6,14},{8,24},{10,2},{12,28},{14,6},{16,0},{1... | collective-permute-start | bytes 393224 | tf_op jit(solution)/shard_map/ppermute | solution.py:57
  13.7 7.2 %collective-permute-start.6 = (f32[128,256]{1,0:T(8,128)S(1)}, f32[128,256]{1,0:T(8,128)S(1)}, u32[]{:S(2)}, u32[]{:S(2)}) collective-permute-start(f32[128,256]{1,0:T(8,128)S(1)} %get-tuple-element.20), channel_id=1, source_target_pairs={{0,5},{1,4},{2,7},{3,6},{4,1},{5,0},{6,3},{7,2},{8,13},{9,12},{10,... | collective-permute-start | bytes 393224 | tf_op jit(solution)/shard_map/ppermute | solution.py:43
  16.6 5.4 %collective-permute-start.2 = (f32[128,256]{1,0:T(8,128)S(1)}, f32[128,256]{1,0:T(8,128)S(1)}, u32[]{:S(2)}, u32[]{:S(2)}) collective-permute-start(f32[128,256]{1,0:T(8,128)S(1)} %get-tuple-element.20), channel_id=1, source_target_pairs={{0,1},{1,0},{2,3},{3,2},{4,5},{5,4},{6,7},{7,6},{8,9},{9,8},{10,11... | collective-permute-start | bytes 393224 | tf_op jit(solution)/shard_map/ppermute | solution.py:43
  17.1 5.0 %collective-permute-start.5 = (f32[128,256]{1,0:T(8,128)S(1)}, f32[128,256]{1,0:T(8,128)S(1)}, u32[]{:S(2)}, u32[]{:S(2)}) collective-permute-start(f32[128,256]{1,0:T(8,128)S(1)} %get-tuple-element.19.rest_0_), channel_id=1, source_target_pairs={{0,4},{1,5},{2,6},{3,7},{4,0},{5,1},{6,2},{7,3},{8,12},{9,13},{10,... | collective-permute-start | bytes 393224 | tf_op jit(solution)/shard_map/ppermute | solution.py:43
  17.2 5.3 %collective-permute-start.3 = (f32[128,256]{1,0:T(8,128)S(1)}, f32[128,256]{1,0:T(8,128)S(1)}, u32[]{:S(2)}, u32[]{:S(2)}) collective-permute-start(f32[128,256]{1,0:T(8,128)S(1)} %get-tuple-element.19.rest_0_), channel_id=1, source_target_pairs={{0,2},{1,3},{2,0},{3,1},{4,6},{5,7},{6,4},{7,5},{8,10},{9,11},{10,... | collective-permute-start | bytes 393224 | tf_op jit(solution)/shard_map/ppermute | solution.py:43
  20.9 1.6 %collective-permute-start.8 = (f32[128,256]{1,0:T(8,128)S(1)}, f32[128,256]{1,0:T(8,128)S(1)}, u32[]{:S(2)}, u32[]{:S(2)}) collective-permute-start(f32[128,256]{1,0:T(8,128)S(1)} %collective-permute-done.6.rest_5_), channel_id=1, source_target_pairs={{0,2},{1,3},{2,0},{3,1},{4,6},{5,7},{6,4},{7,5},{8,10},{9,11},{10,... | collective-permute-start | bytes 393224 | tf_op jit(solution)/shard_map/ppermute | solution.py:43
  22.0 1.3 %collective-permute-start.4 = (f32[128,256]{1,0:T(8,128)S(1)}, f32[128,256]{1,0:T(8,128)S(1)}, u32[]{:S(2)}, u32[]{:S(2)}) collective-permute-start(f32[128,256]{1,0:T(8,128)S(1)} %collective-permute-done.2.rest_1_), channel_id=1, source_target_pairs={{0,2},{1,3},{2,0},{3,1},{4,6},{5,7},{6,4},{7,5},{8,10},{9,11},{10,... | collective-permute-start | bytes 393224 | tf_op jit(solution)/shard_map/ppermute | solution.py:43
  22.0 1.5 %collective-permute-start.7 = (f32[128,256]{1,0:T(8,128)S(1)}, f32[128,256]{1,0:T(8,128)S(1)}, u32[]{:S(2)}, u32[]{:S(2)}) collective-permute-start(f32[128,256]{1,0:T(8,128)S(1)} %collective-permute-done.5.rest_4_), channel_id=1, source_target_pairs={{0,2},{1,3},{2,0},{3,1},{4,6},{5,7},{6,4},{7,5},{8,10},{9,11},{10,... | collective-permute-start | bytes 393224 | tf_op jit(solution)/shard_map/ppermute | solution.py:43

commit v4 on v2

--- a/solution.py
+++ b/solution.py
@@ -183,7 +183,7 @@
     kept = out_ref.shape[0]
     lags, segments = lax.axis_size("lag"), lax.axis_size("seg")
     width = chunk_refs[0].shape[1]
-    for (lag_step, segment_step), chunk_ref in zip(steps(lags, segments), chunk_refs):
+    for (lag_step, segment_step), chunk_ref in zip(reversed(steps(lags, segments)), chunk_refs):
         lag = lax.bitwise_xor(lax.axis_index("lag"), lag_step)
         segment = lax.bitwise_xor(lax.axis_index("seg"), segment_step)
         start = pl.multiple_of((segment * lags + lag) * width, width)
@@ -297,7 +297,7 @@
         ],
         compiler_params=params,
         name="correlate",
-    )(*[held[step] for step in steps(lags, segments)])
+    )(*[held[step] for step in reversed(steps(lags, segments))])
 
 
 def solution(mesh):

time: 26.8 us -> 26.6 us (level)
  starting transfers between devices: 9.43 us -> 8.97 us
  waiting for transfers between devices: 12 us -> 12.3 us
    ppermute x7, starting transfers between devices: 4.02 us -> 3.56 us  [swapped(): return lax.ppermute(value, ('lag', 'seg'), pairs)]
    ppermute x7, waiting for transfers between devices: 5.81 us -> 6.13 us  [swapped(): return lax.ppermute(value, ('lag', 'seg'), pairs)]
where the time goes in v4:
time: 26.6 us; the launch traced here: 26.5 us
  waiting for transfers between devices  12.3 us (46%)
  starting transfers between devices  8.97 us (34%)
  Pallas kernels  4.5 us (17%)
  local copies, waits for them, and re-layouts  0.66 us (2%)
    ppermute x2, waiting for transfers between devices, paired(): return lax.ppermute(value, ('chan', 'lag'), pairs)  6.21 us
    ppermute x7, waiting for transfers between devices, swapped(): return lax.ppermute(value, ('lag', 'seg'), pairs)  6.13 us
    ppermute x2, starting transfers between devices, paired(): return lax.ppermute(value, ('chan', 'lag'), pairs)  5.41 us
    ppermute x7, starting transfers between devices, swapped(): return lax.ppermute(value, ('lag', 'seg'), pairs)  3.56 us
    pallas_call x1, Pallas kernels, shards(): pl.pallas_call(functools.partial(corr_kernel, refs, lag_width), out_shape...  3.11 us
    pallas_call x1, Pallas kernels, shards(): pl.pallas_call(choose_four_kernel, out_shape=[block(rows, samples), block...  0.96 us
    unnamed x4, local copies, waits for them, and re-layouts  0.66 us
  transfers between devices with their start and end apart: 9, of which 7 were waited for; matrix products, arithmetic and copies ran while one was open for 0% of the time, Pallas kernels for 4%

profile of v4, /device:TPU:0, one launch (start us, length us, event | category | flops | bytes accessed | tf_op | source)
XLA Modules:
  0.0 26.5 jit_solution(9149840007679977847)
XLA Ops:
  0.0 0.0 copy-start
  0.0 3.0 %collective-permute-start = (f32[128,1,256]{2,1,0:T(1,128)}, f32[128,1,256]{2,1,0:T(1,128)S(1)}, u32[]{:S(2)}, u32[]{:S(2)}) collective-permute-start(f32[128,1,256]{2,1,0:T(1,128)} %records_ref.1), channel_id=1, source_target_pairs={{0,8},{2,18},{4,12},{6,22},{8,0},{10,26},{12,4},{14,30},{16,24},{1... | collective-permute-start | bytes 393224 | tf_op jit(solution)/shard_map/ppermute | solution.py:56
  3.0 0.0 copy-start.1
  3.0 0.0 copy-done
  3.0 0.7 %copy-done.1 = s32[64]{0:T(128)S(1)} copy-done((s32[64]{0:T(128)S(1)}, s32[64]{0:T(128)}, u32[]{:S(2)}) %copy-start.1) | copy-done | bytes 280
  3.7 1.0 %choose.1 = (f32[128,256]{1,0:T(8,128)S(1)}, bf16[128,256]{1,0:T(8,128)(2,1)S(1)}, bf16[128,256]{1,0:T(8,128)(2,1)S(1)}, bf16[128,64]{1,0:T(8,128)(2,1)S(1)}) custom-call(f32[128,1,256]{2,1,0:T(1,128)} %records_ref.1, s32[4,128]{1,0:T(4,128)S(1)} %bitcast.2, s32[1,64]{1,0:T(1,128)S(1)} %bitcast.3), custom_call_target="tpu_custom_call" | custom-call | tf_op jit(solution)/shard_map/choose/pallas_call | solution.py:245
  4.6 2.7 %collective-permute-done.arrived_ref = f32[128,1,256]{2,1,0:T(1,128)S(1)} collective-permute-done((f32[128,1,256]{2,1,0:T(1,128)}, f32[128,1,256]{2,1,0:T(1,128)S(1)}, u32[]{:S(2)}, u32[]{:S(2)}) %collective-permute-start) | collective-permute-done | bytes 131104 | tf_op jit(solution)/shard_map/ppermute | solution.py:56
  7.3 0.3 pick.1
  7.6 2.4 %collective-permute-start.1 = (f32[128,256]{1,0:T(8,128)S(1)}, f32[128,256]{1,0:T(8,128)S(1)}, u32[]{:S(2)}, u32[]{:S(2)}) collective-permute-start(f32[128,256]{1,0:T(8,128)S(1)} %get-tuple-element.18.sent_ref), channel_id=1, source_target_pairs={{0,16},{2,10},{4,20},{6,14},{8,24},{10,2},{12,28},{14,6},{16,0},{1... | collective-permute-start | bytes 393224 | tf_op jit(solution)/shard_map/ppermute | solution.py:56
  10.0 3.5 %collective-permute-done.1.arrived_ref = f32[128,256]{1,0:T(8,128)S(1)} collective-permute-done((f32[128,256]{1,0:T(8,128)S(1)}, f32[128,256]{1,0:T(8,128)S(1)}, u32[]{:S(2)}, u32[]{:S(2)}) %collective-permute-start.1) | collective-permute-done | bytes 131104 | tf_op jit(solution)/shard_map/ppermute | solution.py:56
  13.5 0.2 place.1
  13.7 1.9 %collective-permute-start.6 = (f32[128,256]{1,0:T(8,128)S(1)}, f32[128,256]{1,0:T(8,128)S(1)}, u32[]{:S(2)}, u32[]{:S(2)}) collective-permute-start(f32[128,256]{1,0:T(8,128)S(1)} %get-tuple-element.19), channel_id=1, source_target_pairs={{0,1},{1,0},{2,3},{3,2},{4,5},{5,4},{6,7},{7,6},{8,9},{9,8},{10,11... | collective-permute-start | bytes 393224 | tf_op jit(solution)/shard_map/ppermute | solution.py:42
  15.6 1.4 %collective-permute-start.2 = (f32[128,256]{1,0:T(8,128)S(1)}, f32[128,256]{1,0:T(8,128)S(1)}, u32[]{:S(2)}, u32[]{:S(2)}) collective-permute-start(f32[128,256]{1,0:T(8,128)S(1)} %get-tuple-element.19), channel_id=1, source_target_pairs={{0,5},{1,4},{2,7},{3,6},{4,1},{5,0},{6,3},{7,2},{8,13},{9,12},{10,... | collective-permute-start | bytes 393224 | tf_op jit(solution)/shard_map/ppermute | solution.py:42
  17.1 0.2 collective-permute-start.4
  17.2 0.0 collective-permute-start.8
  17.2 2.3 %collective-permute-done.6.rest_6_ = f32[128,256]{1,0:T(8,128)S(1)} collective-permute-done((f32[128,256]{1,0:T(8,128)S(1)}, f32[128,256]{1,0:T(8,128)S(1)}, u32[]{:S(2)}, u32[]{:S(2)}) %collective-permute-start.6) | collective-permute-done | bytes 131104 | tf_op jit(solution)/shard_map/ppermute | solution.py:42
  19.6 0.0 collective-permute-start.7
  19.6 1.9 %collective-permute-done.2.rest_2_ = f32[128,256]{1,0:T(8,128)S(1)} collective-permute-done((f32[128,256]{1,0:T(8,128)S(1)}, f32[128,256]{1,0:T(8,128)S(1)}, u32[]{:S(2)}, u32[]{:S(2)}) %collective-permute-start.2) | collective-permute-done | bytes 131104 | tf_op jit(solution)/shard_map/ppermute | solution.py:42
  21.5 0.0 collective-permute-start.3
  21.5 0.5 %collective-permute-done.4.rest_3_ = f32[128,256]{1,0:T(8,128)S(1)} collective-permute-done((f32[128,256]{1,0:T(8,128)S(1)}, f32[128,256]{1,0:T(8,128)S(1)}, u32[]{:S(2)}, u32[]{:S(2)}) %collective-permute-start.4) | collective-permute-done | bytes 131104 | tf_op jit(solution)/shard_map/ppermute | solution.py:42
  22.0 0.0 collective-permute-start.5
  22.0 0.0 collective-permute-done.8.rest_5_
  22.0 0.0 collective-permute-done.7.rest_4_
  22.1 0.8 %collective-permute-done.3.rest_0_ = f32[128,256]{1,0:T(8,128)S(1)} collective-permute-done((f32[128,256]{1,0:T(8,128)S(1)}, f32[128,256]{1,0:T(8,128)S(1)}, u32[]{:S(2)}, u32[]{:S(2)}) %collective-permute-start.3) | collective-permute-done | bytes 131104 | tf_op jit(solution)/shard_map/ppermute | solution.py:42
  22.9 0.5 %collective-permute-done.5.rest_1_ = f32[128,256]{1,0:T(8,128)S(1)} collective-permute-done((f32[128,256]{1,0:T(8,128)S(1)}, f32[128,256]{1,0:T(8,128)S(1)}, u32[]{:S(2)}, u32[]{:S(2)}) %collective-permute-start.5) | collective-permute-done | bytes 131104 | tf_op jit(solution)/shard_map/ppermute | solution.py:42
  23.4 3.1 %correlate.1 = f32[64,2048]{1,0:T(8,128)} custom-call(f32[128,256]{1,0:T(8,128)S(1)} %collective-permute-done.3.rest_0_, f32[128,256]{1,0:T(8,128)S(1)} %collective-permute-done.5.rest_1_, f32[128,256]{1,0:T(8,128)S(1)} %collective-permute-done.2.rest_2_, f32[128,256]{1,0:T(8,128)S(1)} %collective-permute-done.4.rest_3_, ...), custom_call_target="tpu_custom_call" | custom-call | tf_op jit(solution)/shard_map/correlate/pallas_call | solution.py:290
Async XLA Ops:
  0.0 3.0 %copy-start = (s32[512]{0:T(512)S(1)}, s32[512]{0:T(512)}, u32[]{:S(2)}) copy-start(s32[512]{0:T(512)} %param.4) | copy-start | bytes 6148
  0.0 7.3 %collective-permute-start = (f32[128,1,256]{2,1,0:T(1,128)}, f32[128,1,256]{2,1,0:T(1,128)S(1)}, u32[]{:S(2)}, u32[]{:S(2)}) collective-permute-start(f32[128,1,256]{2,1,0:T(1,128)} %records_ref.1), channel_id=1, source_target_pairs={{0,8},{2,18},{4,12},{6,22},{8,0},{10,26},{12,4},{14,30},{16,24},{1... | collective-permute-start | bytes 393224 | tf_op jit(solution)/shard_map/ppermute | solution.py:56
  3.0 0.7 %copy-start.1 = (s32[64]{0:T(128)S(1)}, s32[64]{0:T(128)}, u32[]{:S(2)}) copy-start(s32[64]{0:T(128)} %param.5) | copy-start | bytes 772
  7.6 5.9 %collective-permute-start.1 = (f32[128,256]{1,0:T(8,128)S(1)}, f32[128,256]{1,0:T(8,128)S(1)}, u32[]{:S(2)}, u32[]{:S(2)}) collective-permute-start(f32[128,256]{1,0:T(8,128)S(1)} %get-tuple-element.18.sent_ref), channel_id=1, source_target_pairs={{0,16},{2,10},{4,20},{6,14},{8,24},{10,2},{12,28},{14,6},{16,0},{1... | collective-permute-start | bytes 393224 | tf_op jit(solution)/shard_map/ppermute | solution.py:56
  13.7 5.9 %collective-permute-start.6 = (f32[128,256]{1,0:T(8,128)S(1)}, f32[128,256]{1,0:T(8,128)S(1)}, u32[]{:S(2)}, u32[]{:S(2)}) collective-permute-start(f32[128,256]{1,0:T(8,128)S(1)} %get-tuple-element.19), channel_id=1, source_target_pairs={{0,1},{1,0},{2,3},{3,2},{4,5},{5,4},{6,7},{7,6},{8,9},{9,8},{10,11... | collective-permute-start | bytes 393224 | tf_op jit(solution)/shard_map/ppermute | solution.py:42
  15.6 5.9 %collective-permute-start.2 = (f32[128,256]{1,0:T(8,128)S(1)}, f32[128,256]{1,0:T(8,128)S(1)}, u32[]{:S(2)}, u32[]{:S(2)}) collective-permute-start(f32[128,256]{1,0:T(8,128)S(1)} %get-tuple-element.19), channel_id=1, source_target_pairs={{0,5},{1,4},{2,7},{3,6},{4,1},{5,0},{6,3},{7,2},{8,13},{9,12},{10,... | collective-permute-start | bytes 393224 | tf_op jit(solution)/shard_map/ppermute | solution.py:42
  17.1 5.0 %collective-permute-start.4 = (f32[128,256]{1,0:T(8,128)S(1)}, f32[128,256]{1,0:T(8,128)S(1)}, u32[]{:S(2)}, u32[]{:S(2)}) collective-permute-start(f32[128,256]{1,0:T(8,128)S(1)} %get-tuple-element.20.rest_7_), channel_id=1, source_target_pairs={{0,4},{1,5},{2,6},{3,7},{4,0},{5,1},{6,2},{7,3},{8,12},{9,13},{10,... | collective-permute-start | bytes 393224 | tf_op jit(solution)/shard_map/ppermute | solution.py:42
  17.2 4.8 %collective-permute-start.8 = (f32[128,256]{1,0:T(8,128)S(1)}, f32[128,256]{1,0:T(8,128)S(1)}, u32[]{:S(2)}, u32[]{:S(2)}) collective-permute-start(f32[128,256]{1,0:T(8,128)S(1)} %get-tuple-element.20.rest_7_), channel_id=1, source_target_pairs={{0,2},{1,3},{2,0},{3,1},{4,6},{5,7},{6,4},{7,5},{8,10},{9,11},{10,... | collective-permute-start | bytes 393224 | tf_op jit(solution)/shard_map/ppermute | solution.py:42
  19.6 2.5 %collective-permute-start.7 = (f32[128,256]{1,0:T(8,128)S(1)}, f32[128,256]{1,0:T(8,128)S(1)}, u32[]{:S(2)}, u32[]{:S(2)}) collective-permute-start(f32[128,256]{1,0:T(8,128)S(1)} %collective-permute-done.6.rest_6_), channel_id=1, source_target_pairs={{0,2},{1,3},{2,0},{3,1},{4,6},{5,7},{6,4},{7,5},{8,10},{9,11},{10,... | collective-permute-start | bytes 393224 | tf_op jit(solution)/shard_map/ppermute | solution.py:42
  21.5 1.3 %collective-permute-start.3 = (f32[128,256]{1,0:T(8,128)S(1)}, f32[128,256]{1,0:T(8,128)S(1)}, u32[]{:S(2)}, u32[]{:S(2)}) collective-permute-start(f32[128,256]{1,0:T(8,128)S(1)} %collective-permute-done.2.rest_2_), channel_id=1, source_target_pairs={{0,2},{1,3},{2,0},{3,1},{4,6},{5,7},{6,4},{7,5},{8,10},{9,11},{10,... | collective-permute-start | bytes 393224 | tf_op jit(solution)/shard_map/ppermute | solution.py:42
  22.0 1.3 %collective-permute-start.5 = (f32[128,256]{1,0:T(8,128)S(1)}, f32[128,256]{1,0:T(8,128)S(1)}, u32[]{:S(2)}, u32[]{:S(2)}) collective-permute-start(f32[128,256]{1,0:T(8,128)S(1)} %collective-permute-done.4.rest_3_), channel_id=1, source_target_pairs={{0,2},{1,3},{2,0},{3,1},{4,6},{5,7},{6,4},{7,5},{8,10},{9,11},{10,... | collective-permute-start | bytes 393224 | tf_op jit(solution)/shard_map/ppermute | solution.py:42

commit v5 on v4

--- a/solution.py
+++ b/solution.py
@@ -11,6 +11,7 @@
 LAGS = 128
 SAMPLES = 2048
 PHASES = 4
+MARGIN = 128
 
 
 def halves(value):
@@ -178,41 +179,91 @@
     put(choice(pick_ref[...], arrived_ref[...]), panel_ref[...], out_refs)
 
 
-def corr_kernel(refs, lag_width, *rest):
-    *chunk_refs, out_ref, joined_ref, series_ref, panel_ref = rest
-    kept = out_ref.shape[0]
-    lags, segments = lax.axis_size("lag"), lax.axis_size("seg")
+def join(chunk_refs, joined_ref):
     width = chunk_refs[0].shape[1]
-    for (lag_step, segment_step), chunk_ref in zip(reversed(steps(lags, segments)), chunk_refs):
+    for lag_step, chunk_ref in enumerate(chunk_refs):
         lag = lax.bitwise_xor(lax.axis_index("lag"), lag_step)
-        segment = lax.bitwise_xor(lax.axis_index("seg"), segment_step)
-        start = pl.multiple_of((segment * lags + lag) * width, width)
-        joined_ref[:, pl.ds(start, width)] = chunk_ref[...]
-    series = joined_ref[:kept, :]
-    panel = joined_ref[kept:, :]
+        joined_ref[:, pl.ds(pl.multiple_of(lag * width, width), width)] = chunk_ref[...]
+
+
+def within(panel, segment):
     samples = panel.shape[1]
-    terms = SAMPLES - LAGS
-    times = lax.broadcasted_iota(jnp.int32, panel.shape, 1)
-    panel = jnp.where(times < terms, panel, 0.0)
-    series = pltpu.roll(series, samples - lax.axis_index("lag") * lag_width, 1)
-    groups = lag_width // PHASES
-
-    def spread(value, count, step, out_ref):
-        lines = value.shape[0]
-        for half, part in enumerate(halves(value)):
-            for i in range(count):
-                start = (half * count + i) * lines
-                out_ref[start : start + lines, :] = (
-                    pltpu.roll(part, (i * step) % samples, 1) if i else part
-                )
-
-    spread(panel, PHASES, 1, panel_ref)
-    spread(series, groups, -PHASES, series_ref)
-    lines, columns = groups * kept, PHASES * refs
+    times = lax.broadcasted_iota(jnp.int32, panel.shape, 1) + segment * samples
+    return jnp.where(times < SAMPLES - LAGS, panel, 0.0)
+
+
+def spread(series, panel, lag_width, series_ref, panel_ref, start):
+    span = series.shape[1]
+    length = span - MARGIN
+    series = pltpu.roll(series, span - lax.axis_index("lag") * lag_width, 1)
+    for value, shifts, first, out_ref in (
+        (panel, range(PHASES), MARGIN, panel_ref),
+        (series, range(0, -lag_width, -PHASES), 0, series_ref),
+    ):
+        lines, base = value.shape[0], 0
+        for half in halves(value):
+            for shift in shifts:
+                moved = pltpu.roll(half, shift % span, 1) if shift else half
+                out_ref[base : base + lines, start : start + length] = moved[:, first : first + length]
+                base += lines
+
+
+def products(series_ref, panel_ref):
+    lines, columns = series_ref.shape[0] // 2, panel_ref.shape[0] // 2
     upper = product_nt(series_ref[...], panel_ref[:columns, :])
     lower = product_nt(series_ref[:lines, :], panel_ref[columns:, :])
-    total = (upper[:lines] + upper[lines:] + lower) * (1.0 / math.sqrt(terms))
-    for group in range(groups):
+    return upper[:lines] + upper[lines:] + lower
+
+
+def other_kernel(kept, lag_width, *rest):
+    *chunk_refs, partial_ref, head_ref, tail_ref, joined_ref, series_ref, panel_ref = rest
+    join(chunk_refs, joined_ref)
+    series = joined_ref[:kept, :]
+    panel = within(joined_ref[kept:, :], 1 - lax.axis_index("seg"))
+    head_ref[...] = series[:, : 2 * MARGIN]
+    tail_ref[...] = panel[:, -MARGIN:]
+    nothing = jnp.zeros((kept, MARGIN), jnp.float32)
+    spread(
+        jnp.concatenate([series, nothing], axis=1),
+        jnp.concatenate([nothing, panel], axis=1),
+        lag_width,
+        series_ref,
+        panel_ref,
+        0,
+    )
+    partial_ref[...] = products(series_ref, panel_ref)
+
+
+def own_kernel(kept, lag_width, partial_ref, head_ref, tail_ref, *rest):
+    *chunk_refs, out_ref, joined_ref, series_ref, panel_ref = rest
+    join(chunk_refs, joined_ref)
+    segment = lax.axis_index("seg")
+    series = joined_ref[:kept, :]
+    panel = within(joined_ref[kept:, :], segment)
+    length = series.shape[1]
+    nothing = jnp.zeros((kept, MARGIN), jnp.float32)
+    head = jnp.where(segment == 0, head_ref[...], series[:, : 2 * MARGIN])
+    tail = jnp.where(segment == 0, panel[:, -MARGIN:], tail_ref[...])
+    spread(
+        jnp.concatenate([series, nothing], axis=1),
+        jnp.concatenate([nothing, panel], axis=1),
+        lag_width,
+        series_ref,
+        panel_ref,
+        0,
+    )
+    spread(
+        jnp.concatenate([nothing, head], axis=1),
+        jnp.concatenate([nothing, tail, nothing], axis=1),
+        lag_width,
+        series_ref,
+        panel_ref,
+        length,
+    )
+    total = products(series_ref, panel_ref) + partial_ref[...]
+    total = total * (1.0 / math.sqrt(SAMPLES - LAGS))
+    columns = total.shape[1]
+    for group in range(total.shape[0] // kept):
         out_ref[:, group * columns : (group + 1) * columns] = total[
             group * kept : (group + 1) * kept
         ]
@@ -287,17 +338,30 @@
                 held[lag_step, segment_step] = swapped(placed[segment_step], lag_step, segment_step)
     for lag_step, segment_step in list(held):
         held[lag_step + 1, segment_step] = swapped(held[lag_step, segment_step], 1, 0)
+    length = lags * samples
+    lines, columns = lag_width // PHASES * kept, PHASES * refs
+
+    def scratch(width):
+        return [
+            pltpu.VMEM((kept + refs, length), jnp.float32),
+            pltpu.VMEM((2 * lines, width), jnp.bfloat16),
+            pltpu.VMEM((2 * columns, width), jnp.bfloat16),
+        ]
+
+    other = pl.pallas_call(
+        functools.partial(other_kernel, kept, lag_width),
+        out_shape=[block(lines, columns), block(kept, 2 * MARGIN), block(refs, MARGIN)],
+        scratch_shapes=scratch(length),
+        compiler_params=params,
+        name="other",
+    )(*[held[lag_step, 1] for lag_step in range(lags)])
     return pl.pallas_call(
-        functools.partial(corr_kernel, refs, lag_width),
-        out_shape=jax.ShapeDtypeStruct((kept, lag_width * refs), jnp.float32),
-        scratch_shapes=[
-            pltpu.VMEM((kept + refs, lags * segments * samples), jnp.float32),
-            pltpu.VMEM((2 * lag_width // PHASES * kept, lags * segments * samples), jnp.bfloat16),
-            pltpu.VMEM((2 * PHASES * refs, lags * segments * samples), jnp.bfloat16),
-        ],
+        functools.partial(own_kernel, kept, lag_width),
+        out_shape=block(kept, lag_width * refs),
+        scratch_shapes=scratch(length + 2 * MARGIN),
         compiler_params=params,
-        name="correlate",
-    )(*[held[step] for step in reversed(steps(lags, segments))])
+        name="own",
+    )(*other, *[held[lag_step, 0] for lag_step in range(lags)])
 
 
 def solution(mesh):

time: 26.6 us -> 27.4 us (1.030)
  Pallas kernels: 4.5 us -> 5.25 us
  starting transfers between devices: 8.97 us -> 9.48 us
  waiting for transfers between devices: 12.3 us -> 11.8 us
    pallas_call x1 -> x2, Pallas kernels: 3.11 us -> 3.86 us  [the longest x1 2.47 us: shards(): pl.pallas_call(functools.partial(own_kernel, kept, lag_width), out_shape=...]
    ppermute x7, waiting for transfers between devices: 6.13 us -> 5.57 us  [swapped(): return lax.ppermute(value, ('lag', 'seg'), pairs)]
    ppermute x7, starting transfers between devices: 3.56 us -> 4.07 us  [swapped(): return lax.ppermute(value, ('lag', 'seg'), pairs)]
  transfers between devices with their start and end apart: 9 -> 9, of which waited for: 7 -> 5; matrix products, arithmetic and copies ran while one was open for 0% -> 0% of each run, Pallas kernels for 4% -> 9%
where the time goes in v5:
time: 27.4 us; the launch traced here: 27.2 us
  waiting for transfers between devices  11.8 us (43%)
  starting transfers between devices  9.48 us (35%)
  Pallas kernels  5.25 us (19%)
  local copies, waits for them, and re-layouts  0.66 us (2%)
    ppermute x2, waiting for transfers between devices, paired(): return lax.ppermute(value, ('chan', 'lag'), pairs)  6.21 us
    ppermute x7, waiting for transfers between devices, swapped(): return lax.ppermute(value, ('lag', 'seg'), pairs)  5.57 us
    ppermute x2, starting transfers between devices, paired(): return lax.ppermute(value, ('chan', 'lag'), pairs)  5.41 us
    ppermute x7, starting transfers between devices, swapped(): return lax.ppermute(value, ('lag', 'seg'), pairs)  4.07 us
    pallas_call x1, Pallas kernels, shards(): pl.pallas_call(functools.partial(own_kernel, kept, lag_width), out_shape=...  2.47 us
    pallas_call x1, Pallas kernels, shards(): pl.pallas_call(functools.partial(other_kernel, kept, lag_width), out_shap...  1.39 us
    pallas_call x1, Pallas kernels, shards(): pl.pallas_call(choose_four_kernel, out_shape=[block(rows, samples), block...  0.96 us
    unnamed x4, local copies, waits for them, and re-layouts  0.66 us
  transfers between devices with their start and end apart: 9, of which 5 were waited for; matrix products, arithmetic and copies ran while one was open for 0% of the time, Pallas kernels for 9%

profile of v5, /device:TPU:0, one launch (start us, length us, event | category | flops | bytes accessed | tf_op | source)
XLA Modules:
  0.0 27.2 jit_solution(6979471235494326365)
XLA Ops:
  0.0 0.0 copy-start
  0.0 3.0 %collective-permute-start = (f32[128,1,256]{2,1,0:T(1,128)}, f32[128,1,256]{2,1,0:T(1,128)S(1)}, u32[]{:S(2)}, u32[]{:S(2)}) collective-permute-start(f32[128,1,256]{2,1,0:T(1,128)} %records_ref.1), channel_id=1, source_target_pairs={{0,8},{2,18},{4,12},{6,22},{8,0},{10,26},{12,4},{14,30},{16,24},{1... | collective-permute-start | bytes 393224 | tf_op jit(solution)/shard_map/ppermute | solution.py:57
  3.0 0.0 copy-start.1
  3.0 0.0 copy-done
  3.0 0.7 %copy-done.1 = s32[64]{0:T(128)S(1)} copy-done((s32[64]{0:T(128)S(1)}, s32[64]{0:T(128)}, u32[]{:S(2)}) %copy-start.1) | copy-done | bytes 280
  3.7 1.0 %choose.1 = (f32[128,256]{1,0:T(8,128)S(1)}, bf16[128,256]{1,0:T(8,128)(2,1)S(1)}, bf16[128,256]{1,0:T(8,128)(2,1)S(1)}, bf16[128,64]{1,0:T(8,128)(2,1)S(1)}) custom-call(f32[128,1,256]{2,1,0:T(1,128)} %records_ref.1, s32[4,128]{1,0:T(4,128)S(1)} %bitcast.2, s32[1,64]{1,0:T(1,128)S(1)} %bitcast.3), custom_call_target="tpu_custom_call" | custom-call | tf_op jit(solution)/shard_map/choose/pallas_call | solution.py:296
  4.6 2.7 %collective-permute-done.arrived_ref = f32[128,1,256]{2,1,0:T(1,128)S(1)} collective-permute-done((f32[128,1,256]{2,1,0:T(1,128)}, f32[128,1,256]{2,1,0:T(1,128)S(1)}, u32[]{:S(2)}, u32[]{:S(2)}) %collective-permute-start) | collective-permute-done | bytes 131104 | tf_op jit(solution)/shard_map/ppermute | solution.py:57
  7.3 0.3 pick.1
  7.6 2.4 %collective-permute-start.1 = (f32[128,256]{1,0:T(8,128)S(1)}, f32[128,256]{1,0:T(8,128)S(1)}, u32[]{:S(2)}, u32[]{:S(2)}) collective-permute-start(f32[128,256]{1,0:T(8,128)S(1)} %get-tuple-element.21.sent_ref), channel_id=1, source_target_pairs={{0,16},{2,10},{4,20},{6,14},{8,24},{10,2},{12,28},{14,6},{16,0},{1... | collective-permute-start | bytes 393224 | tf_op jit(solution)/shard_map/ppermute | solution.py:57
  10.0 3.5 %collective-permute-done.1.arrived_ref = f32[128,256]{1,0:T(8,128)S(1)} collective-permute-done((f32[128,256]{1,0:T(8,128)S(1)}, f32[128,256]{1,0:T(8,128)S(1)}, u32[]{:S(2)}, u32[]{:S(2)}) %collective-permute-start.1) | collective-permute-done | bytes 131104 | tf_op jit(solution)/shard_map/ppermute | solution.py:57
  13.5 0.2 place.1
  13.7 2.9 %collective-permute-start.4 = (f32[128,256]{1,0:T(8,128)S(1)}, f32[128,256]{1,0:T(8,128)S(1)}, u32[]{:S(2)}, u32[]{:S(2)}) collective-permute-start(f32[128,256]{1,0:T(8,128)S(1)} %get-tuple-element.22), channel_id=1, source_target_pairs={{0,5},{1,4},{2,7},{3,6},{4,1},{5,0},{6,3},{7,2},{8,13},{9,12},{10,... | collective-permute-start | bytes 393224 | tf_op jit(solution)/shard_map/ppermute | solution.py:43
  16.6 0.5 %collective-permute-start.2 = (f32[128,256]{1,0:T(8,128)S(1)}, f32[128,256]{1,0:T(8,128)S(1)}, u32[]{:S(2)}, u32[]{:S(2)}) collective-permute-start(f32[128,256]{1,0:T(8,128)S(1)} %get-tuple-element.22), channel_id=1, source_target_pairs={{0,1},{1,0},{2,3},{3,2},{4,5},{5,4},{6,7},{7,6},{8,9},{9,8},{10,11... | collective-permute-start | bytes 393224 | tf_op jit(solution)/shard_map/ppermute | solution.py:43
  17.1 0.2 collective-permute-start.7
  17.2 3.6 %collective-permute-done.4.rest_2_ = f32[128,256]{1,0:T(8,128)S(1)} collective-permute-done((f32[128,256]{1,0:T(8,128)S(1)}, f32[128,256]{1,0:T(8,128)S(1)}, u32[]{:S(2)}, u32[]{:S(2)}) %collective-permute-start.4) | collective-permute-done | bytes 131104 | tf_op jit(solution)/shard_map/ppermute | solution.py:43
  20.9 0.0 collective-permute-start.5
  20.9 1.1 %collective-permute-done.2.rest_0_ = f32[128,256]{1,0:T(8,128)S(1)} collective-permute-done((f32[128,256]{1,0:T(8,128)S(1)}, f32[128,256]{1,0:T(8,128)S(1)}, u32[]{:S(2)}, u32[]{:S(2)}) %collective-permute-start.2) | collective-permute-done | bytes 131104 | tf_op jit(solution)/shard_map/ppermute | solution.py:43
  22.0 0.0 collective-permute-start.3
  22.0 0.5 %collective-permute-start.6 = (f32[128,256]{1,0:T(8,128)S(1)}, f32[128,256]{1,0:T(8,128)S(1)}, u32[]{:S(2)}, u32[]{:S(2)}) collective-permute-start(f32[128,256]{1,0:T(8,128)S(1)} %get-tuple-element.26.rest_0_), channel_id=1, source_target_pairs={{0,2},{1,3},{2,0},{3,1},{4,6},{5,7},{6,4},{7,5},{8,10},{9,11},{10,... | collective-permute-start | bytes 393224 | tf_op jit(solution)/shard_map/ppermute | solution.py:43
  22.5 0.0 collective-permute-done.7.rest_2_
  22.5 0.0 collective-permute-start.8
  22.5 0.0 collective-permute-done.5.rest_3_
  22.5 0.8 %collective-permute-done.3.rest_1_ = f32[128,256]{1,0:T(8,128)S(1)} collective-permute-done((f32[128,256]{1,0:T(8,128)S(1)}, f32[128,256]{1,0:T(8,128)S(1)}, u32[]{:S(2)}, u32[]{:S(2)}) %collective-permute-start.3) | collective-permute-done | bytes 131104 | tf_op jit(solution)/shard_map/ppermute | solution.py:43
  23.3 1.4 %other.1 = (f32[512,256]{1,0:T(8,128)S(1)}, f32[64,256]{1,0:T(8,128)S(1)}, f32[64,128]{1,0:T(8,128)S(1)}) custom-call(f32[128,256]{1,0:T(8,128)S(1)} %collective-permute-done.2.rest_0_, f32[128,256]{1,0:T(8,128)S(1)} %collective-permute-done.3.rest_1_, f32[128,256]{1,0:T(8,128)S(1)} %collective-permute-done.4.rest_2_, ...), custom_call_target="tpu_custom_call" | custom-call | tf_op jit(solution)/shard_map/other/pallas_call | solution.py:351
  24.7 0.0 collective-permute-done.6.rest_1_
  24.7 0.0 collective-permute-done.8.rest_3_
  24.8 2.5 %own.1 = f32[64,2048]{1,0:T(8,128)} custom-call(f32[512,256]{1,0:T(8,128)S(1)} %get-tuple-element.23.partial_ref, f32[64,256]{1,0:T(8,128)S(1)} %get-tuple-element.24.head_ref, f32[64,128]{1,0:T(8,128)S(1)} %get-tuple-element.25.tail_ref, f32[128,256]{1,0:T(8,128)S(1)} %get-tuple-element.26.rest_0_, f32[128,256]{1,0:T(8,128)S(1)} %collective-permute-done.6.rest_1_, ...), custom_call_target="tpu_custom_call" | custom-call | tf_op jit(solution)/shard_map/own/pallas_call | solution.py:358
Async XLA Ops:
  0.0 3.0 %copy-start = (s32[512]{0:T(512)S(1)}, s32[512]{0:T(512)}, u32[]{:S(2)}) copy-start(s32[512]{0:T(512)} %param.4) | copy-start | bytes 6148
  0.0 7.3 %collective-permute-start = (f32[128,1,256]{2,1,0:T(1,128)}, f32[128,1,256]{2,1,0:T(1,128)S(1)}, u32[]{:S(2)}, u32[]{:S(2)}) collective-permute-start(f32[128,1,256]{2,1,0:T(1,128)} %records_ref.1), channel_id=1, source_target_pairs={{0,8},{2,18},{4,12},{6,22},{8,0},{10,26},{12,4},{14,30},{16,24},{1... | collective-permute-start | bytes 393224 | tf_op jit(solution)/shard_map/ppermute | solution.py:57
  3.0 0.7 %copy-start.1 = (s32[64]{0:T(128)S(1)}, s32[64]{0:T(128)}, u32[]{:S(2)}) copy-start(s32[64]{0:T(128)} %param.5) | copy-start | bytes 772
  7.6 5.9 %collective-permute-start.1 = (f32[128,256]{1,0:T(8,128)S(1)}, f32[128,256]{1,0:T(8,128)S(1)}, u32[]{:S(2)}, u32[]{:S(2)}) collective-permute-start(f32[128,256]{1,0:T(8,128)S(1)} %get-tuple-element.21.sent_ref), channel_id=1, source_target_pairs={{0,16},{2,10},{4,20},{6,14},{8,24},{10,2},{12,28},{14,6},{16,0},{1... | collective-permute-start | bytes 393224 | tf_op jit(solution)/shard_map/ppermute | solution.py:57
  13.7 7.2 %collective-permute-start.4 = (f32[128,256]{1,0:T(8,128)S(1)}, f32[128,256]{1,0:T(8,128)S(1)}, u32[]{:S(2)}, u32[]{:S(2)}) collective-permute-start(f32[128,256]{1,0:T(8,128)S(1)} %get-tuple-element.22), channel_id=1, source_target_pairs={{0,5},{1,4},{2,7},{3,6},{4,1},{5,0},{6,3},{7,2},{8,13},{9,12},{10,... | collective-permute-start | bytes 393224 | tf_op jit(solution)/shard_map/ppermute | solution.py:43
  16.6 5.4 %collective-permute-start.2 = (f32[128,256]{1,0:T(8,128)S(1)}, f32[128,256]{1,0:T(8,128)S(1)}, u32[]{:S(2)}, u32[]{:S(2)}) collective-permute-start(f32[128,256]{1,0:T(8,128)S(1)} %get-tuple-element.22), channel_id=1, source_target_pairs={{0,1},{1,0},{2,3},{3,2},{4,5},{5,4},{6,7},{7,6},{8,9},{9,8},{10,11... | collective-permute-start | bytes 393224 | tf_op jit(solution)/shard_map/ppermute | solution.py:43
  17.1 5.4 %collective-permute-start.7 = (f32[128,256]{1,0:T(8,128)S(1)}, f32[128,256]{1,0:T(8,128)S(1)}, u32[]{:S(2)}, u32[]{:S(2)}) collective-permute-start(f32[128,256]{1,0:T(8,128)S(1)} %get-tuple-element.26.rest_0_), channel_id=1, source_target_pairs={{0,4},{1,5},{2,6},{3,7},{4,0},{5,1},{6,2},{7,3},{8,12},{9,13},{10,... | collective-permute-start | bytes 393224 | tf_op jit(solution)/shard_map/ppermute | solution.py:43
  20.9 1.6 %collective-permute-start.5 = (f32[128,256]{1,0:T(8,128)S(1)}, f32[128,256]{1,0:T(8,128)S(1)}, u32[]{:S(2)}, u32[]{:S(2)}) collective-permute-start(f32[128,256]{1,0:T(8,128)S(1)} %collective-permute-done.4.rest_2_), channel_id=1, source_target_pairs={{0,2},{1,3},{2,0},{3,1},{4,6},{5,7},{6,4},{7,5},{8,10},{9,11},{10,... | collective-permute-start | bytes 393224 | tf_op jit(solution)/shard_map/ppermute | solution.py:43
  22.0 1.3 %collective-permute-start.3 = (f32[128,256]{1,0:T(8,128)S(1)}, f32[128,256]{1,0:T(8,128)S(1)}, u32[]{:S(2)}, u32[]{:S(2)}) collective-permute-start(f32[128,256]{1,0:T(8,128)S(1)} %collective-permute-done.2.rest_0_), channel_id=1, source_target_pairs={{0,2},{1,3},{2,0},{3,1},{4,6},{5,7},{6,4},{7,5},{8,10},{9,11},{10,... | collective-permute-start | bytes 393224 | tf_op jit(solution)/shard_map/ppermute | solution.py:43
  22.0 2.8 %collective-permute-start.6 = (f32[128,256]{1,0:T(8,128)S(1)}, f32[128,256]{1,0:T(8,128)S(1)}, u32[]{:S(2)}, u32[]{:S(2)}) collective-permute-start(f32[128,256]{1,0:T(8,128)S(1)} %get-tuple-element.26.rest_0_), channel_id=1, source_target_pairs={{0,2},{1,3},{2,0},{3,1},{4,6},{5,7},{6,4},{7,5},{8,10},{9,11},{10,... | collective-permute-start | bytes 393224 | tf_op jit(solution)/shard_map/ppermute | solution.py:43
  22.5 2.2 %collective-permute-start.8 = (f32[128,256]{1,0:T(8,128)S(1)}, f32[128,256]{1,0:T(8,128)S(1)}, u32[]{:S(2)}, u32[]{:S(2)}) collective-permute-start(f32[128,256]{1,0:T(8,128)S(1)} %collective-permute-done.7.rest_2_), channel_id=1, source_target_pairs={{0,2},{1,3},{2,0},{3,1},{4,6},{5,7},{6,4},{7,5},{8,10},{9,11},{10,... | collective-permute-start | bytes 393224 | tf_op jit(solution)/shard_map/ppermute | solution.py:43

commit v6 on v2

--- a/solution.py
+++ b/solution.py
@@ -10,7 +10,7 @@
 
 LAGS = 128
 SAMPLES = 2048
-PHASES = 4
+PHASES = 8
 
 
 def halves(value):

time: 26.8 us -> 26.7 us (level)
  no operation moved by 1% of the time
where the time goes in v6:
time: 26.7 us; the launch traced here: 26.5 us
  waiting for transfers between devices  12 us (45%)
  starting transfers between devices  9.43 us (35%)
  Pallas kernels  4.4 us (16%)
  local copies, waits for them, and re-layouts  0.66 us (2%)
    ppermute x2, waiting for transfers between devices, paired(): return lax.ppermute(value, ('chan', 'lag'), pairs)  6.21 us
    ppermute x7, waiting for transfers between devices, swapped(): return lax.ppermute(value, ('lag', 'seg'), pairs)  5.81 us
    ppermute x2, starting transfers between devices, paired(): return lax.ppermute(value, ('chan', 'lag'), pairs)  5.41 us
    ppermute x7, starting transfers between devices, swapped(): return lax.ppermute(value, ('lag', 'seg'), pairs)  4.02 us
    pallas_call x1, Pallas kernels, shards(): pl.pallas_call(functools.partial(corr_kernel, refs, lag_width), out_shape...  3.01 us
    pallas_call x1, Pallas kernels, shards(): pl.pallas_call(choose_four_kernel, out_shape=[block(rows, samples), block...  0.96 us
    unnamed x4, local copies, waits for them, and re-layouts  0.66 us
  transfers between devices with their start and end apart: 9, of which 7 were waited for; matrix products, arithmetic and copies ran while one was open for 0% of the time, Pallas kernels for 4%

profile of v6, /device:TPU:0, one launch (start us, length us, event | category | flops | bytes accessed | tf_op | source)
XLA Modules:
  0.0 26.5 jit_solution(7346164029432480748)
XLA Ops:
  0.0 0.0 copy-start
  0.0 3.0 %collective-permute-start = (f32[128,1,256]{2,1,0:T(1,128)}, f32[128,1,256]{2,1,0:T(1,128)S(1)}, u32[]{:S(2)}, u32[]{:S(2)}) collective-permute-start(f32[128,1,256]{2,1,0:T(1,128)} %records_ref.1), channel_id=1, source_target_pairs={{0,8},{2,18},{4,12},{6,22},{8,0},{10,26},{12,4},{14,30},{16,24},{1... | collective-permute-start | bytes 393224 | tf_op jit(solution)/shard_map/ppermute | solution.py:56
  3.0 0.0 copy-start.1
  3.0 0.0 copy-done
  3.0 0.7 %copy-done.1 = s32[64]{0:T(128)S(1)} copy-done((s32[64]{0:T(128)S(1)}, s32[64]{0:T(128)}, u32[]{:S(2)}) %copy-start.1) | copy-done | bytes 280
  3.7 1.0 %choose.1 = (f32[128,256]{1,0:T(8,128)S(1)}, bf16[128,256]{1,0:T(8,128)(2,1)S(1)}, bf16[128,256]{1,0:T(8,128)(2,1)S(1)}, bf16[128,64]{1,0:T(8,128)(2,1)S(1)}) custom-call(f32[128,1,256]{2,1,0:T(1,128)} %records_ref.1, s32[4,128]{1,0:T(4,128)S(1)} %bitcast.2, s32[1,64]{1,0:T(1,128)S(1)} %bitcast.3), custom_call_target="tpu_custom_call" | custom-call | tf_op jit(solution)/shard_map/choose/pallas_call | solution.py:245
  4.6 2.7 %collective-permute-done.arrived_ref = f32[128,1,256]{2,1,0:T(1,128)S(1)} collective-permute-done((f32[128,1,256]{2,1,0:T(1,128)}, f32[128,1,256]{2,1,0:T(1,128)S(1)}, u32[]{:S(2)}, u32[]{:S(2)}) %collective-permute-start) | collective-permute-done | bytes 131104 | tf_op jit(solution)/shard_map/ppermute | solution.py:56
  7.3 0.3 pick.1
  7.6 2.4 %collective-permute-start.1 = (f32[128,256]{1,0:T(8,128)S(1)}, f32[128,256]{1,0:T(8,128)S(1)}, u32[]{:S(2)}, u32[]{:S(2)}) collective-permute-start(f32[128,256]{1,0:T(8,128)S(1)} %get-tuple-element.18.sent_ref), channel_id=1, source_target_pairs={{0,16},{2,10},{4,20},{6,14},{8,24},{10,2},{12,28},{14,6},{16,0},{1... | collective-permute-start | bytes 393224 | tf_op jit(solution)/shard_map/ppermute | solution.py:56
  10.0 3.5 %collective-permute-done.1.arrived_ref = f32[128,256]{1,0:T(8,128)S(1)} collective-permute-done((f32[128,256]{1,0:T(8,128)S(1)}, f32[128,256]{1,0:T(8,128)S(1)}, u32[]{:S(2)}, u32[]{:S(2)}) %collective-permute-start.1) | collective-permute-done | bytes 131104 | tf_op jit(solution)/shard_map/ppermute | solution.py:56
  13.5 0.2 place.1
  13.7 2.9 %collective-permute-start.6 = (f32[128,256]{1,0:T(8,128)S(1)}, f32[128,256]{1,0:T(8,128)S(1)}, u32[]{:S(2)}, u32[]{:S(2)}) collective-permute-start(f32[128,256]{1,0:T(8,128)S(1)} %get-tuple-element.20), channel_id=1, source_target_pairs={{0,5},{1,4},{2,7},{3,6},{4,1},{5,0},{6,3},{7,2},{8,13},{9,12},{10,... | collective-permute-start | bytes 393224 | tf_op jit(solution)/shard_map/ppermute | solution.py:42
  16.6 0.5 %collective-permute-start.2 = (f32[128,256]{1,0:T(8,128)S(1)}, f32[128,256]{1,0:T(8,128)S(1)}, u32[]{:S(2)}, u32[]{:S(2)}) collective-permute-start(f32[128,256]{1,0:T(8,128)S(1)} %get-tuple-element.20), channel_id=1, source_target_pairs={{0,1},{1,0},{2,3},{3,2},{4,5},{5,4},{6,7},{7,6},{8,9},{9,8},{10,11... | collective-permute-start | bytes 393224 | tf_op jit(solution)/shard_map/ppermute | solution.py:42
  17.1 0.2 collective-permute-start.5
  17.2 0.0 collective-permute-start.3
  17.2 3.6 %collective-permute-done.6.rest_5_ = f32[128,256]{1,0:T(8,128)S(1)} collective-permute-done((f32[128,256]{1,0:T(8,128)S(1)}, f32[128,256]{1,0:T(8,128)S(1)}, u32[]{:S(2)}, u32[]{:S(2)}) %collective-permute-start.6) | collective-permute-done | bytes 131104 | tf_op jit(solution)/shard_map/ppermute | solution.py:42
  20.9 0.0 collective-permute-start.8
  20.9 1.1 %collective-permute-done.2.rest_1_ = f32[128,256]{1,0:T(8,128)S(1)} collective-permute-done((f32[128,256]{1,0:T(8,128)S(1)}, f32[128,256]{1,0:T(8,128)S(1)}, u32[]{:S(2)}, u32[]{:S(2)}) %collective-permute-start.2) | collective-permute-done | bytes 131104 | tf_op jit(solution)/shard_map/ppermute | solution.py:42
  22.0 0.0 collective-permute-start.4
  22.0 0.1 collective-permute-done.5.rest_4_
  22.0 0.5 %collective-permute-start.7 = (f32[128,256]{1,0:T(8,128)S(1)}, f32[128,256]{1,0:T(8,128)S(1)}, u32[]{:S(2)}, u32[]{:S(2)}) collective-permute-start(f32[128,256]{1,0:T(8,128)S(1)} %collective-permute-done.5.rest_4_), channel_id=1, source_target_pairs={{0,2},{1,3},{2,0},{3,1},{4,6},{5,7},{6,4},{7,5},{8,10},{9,11},{10,... | collective-permute-start | bytes 393224 | tf_op jit(solution)/shard_map/ppermute | solution.py:42
  22.5 0.0 collective-permute-done.3.rest_2_
  22.5 0.0 collective-permute-done.8.rest_7_
  22.5 0.8 %collective-permute-done.4.rest_3_ = f32[128,256]{1,0:T(8,128)S(1)} collective-permute-done((f32[128,256]{1,0:T(8,128)S(1)}, f32[128,256]{1,0:T(8,128)S(1)}, u32[]{:S(2)}, u32[]{:S(2)}) %collective-permute-start.4) | collective-permute-done | bytes 131104 | tf_op jit(solution)/shard_map/ppermute | solution.py:42
  23.3 0.2 collective-permute-done.7.rest_6_
  23.5 3.0 %correlate.1 = f32[64,2048]{1,0:T(8,128)} custom-call(f32[128,256]{1,0:T(8,128)S(1)} %get-tuple-element.19.rest_0_, f32[128,256]{1,0:T(8,128)S(1)} %collective-permute-done.2.rest_1_, f32[128,256]{1,0:T(8,128)S(1)} %collective-permute-done.3.rest_2_, f32[128,256]{1,0:T(8,128)S(1)} %collective-permute-done.4.rest_3_, ...), custom_call_target="tpu_custom_call" | custom-call | tf_op jit(solution)/shard_map/correlate/pallas_call | solution.py:290
Async XLA Ops:
  0.0 3.0 %copy-start = (s32[512]{0:T(512)S(1)}, s32[512]{0:T(512)}, u32[]{:S(2)}) copy-start(s32[512]{0:T(512)} %param.4) | copy-start | bytes 6148
  0.0 7.3 %collective-permute-start = (f32[128,1,256]{2,1,0:T(1,128)}, f32[128,1,256]{2,1,0:T(1,128)S(1)}, u32[]{:S(2)}, u32[]{:S(2)}) collective-permute-start(f32[128,1,256]{2,1,0:T(1,128)} %records_ref.1), channel_id=1, source_target_pairs={{0,8},{2,18},{4,12},{6,22},{8,0},{10,26},{12,4},{14,30},{16,24},{1... | collective-permute-start | bytes 393224 | tf_op jit(solution)/shard_map/ppermute | solution.py:56
  3.0 0.7 %copy-start.1 = (s32[64]{0:T(128)S(1)}, s32[64]{0:T(128)}, u32[]{:S(2)}) copy-start(s32[64]{0:T(128)} %param.5) | copy-start | bytes 772
  7.6 5.9 %collective-permute-start.1 = (f32[128,256]{1,0:T(8,128)S(1)}, f32[128,256]{1,0:T(8,128)S(1)}, u32[]{:S(2)}, u32[]{:S(2)}) collective-permute-start(f32[128,256]{1,0:T(8,128)S(1)} %get-tuple-element.18.sent_ref), channel_id=1, source_target_pairs={{0,16},{2,10},{4,20},{6,14},{8,24},{10,2},{12,28},{14,6},{16,0},{1... | collective-permute-start | bytes 393224 | tf_op jit(solution)/shard_map/ppermute | solution.py:56
  13.7 7.2 %collective-permute-start.6 = (f32[128,256]{1,0:T(8,128)S(1)}, f32[128,256]{1,0:T(8,128)S(1)}, u32[]{:S(2)}, u32[]{:S(2)}) collective-permute-start(f32[128,256]{1,0:T(8,128)S(1)} %get-tuple-element.20), channel_id=1, source_target_pairs={{0,5},{1,4},{2,7},{3,6},{4,1},{5,0},{6,3},{7,2},{8,13},{9,12},{10,... | collective-permute-start | bytes 393224 | tf_op jit(solution)/shard_map/ppermute | solution.py:42
  16.6 5.4 %collective-permute-start.2 = (f32[128,256]{1,0:T(8,128)S(1)}, f32[128,256]{1,0:T(8,128)S(1)}, u32[]{:S(2)}, u32[]{:S(2)}) collective-permute-start(f32[128,256]{1,0:T(8,128)S(1)} %get-tuple-element.20), channel_id=1, source_target_pairs={{0,1},{1,0},{2,3},{3,2},{4,5},{5,4},{6,7},{7,6},{8,9},{9,8},{10,11... | collective-permute-start | bytes 393224 | tf_op jit(solution)/shard_map/ppermute | solution.py:42
  17.1 5.0 %collective-permute-start.5 = (f32[128,256]{1,0:T(8,128)S(1)}, f32[128,256]{1,0:T(8,128)S(1)}, u32[]{:S(2)}, u32[]{:S(2)}) collective-permute-start(f32[128,256]{1,0:T(8,128)S(1)} %get-tuple-element.19.rest_0_), channel_id=1, source_target_pairs={{0,4},{1,5},{2,6},{3,7},{4,0},{5,1},{6,2},{7,3},{8,12},{9,13},{10,... | collective-permute-start | bytes 393224 | tf_op jit(solution)/shard_map/ppermute | solution.py:42
  17.2 5.3 %collective-permute-start.3 = (f32[128,256]{1,0:T(8,128)S(1)}, f32[128,256]{1,0:T(8,128)S(1)}, u32[]{:S(2)}, u32[]{:S(2)}) collective-permute-start(f32[128,256]{1,0:T(8,128)S(1)} %get-tuple-element.19.rest_0_), channel_id=1, source_target_pairs={{0,2},{1,3},{2,0},{3,1},{4,6},{5,7},{6,4},{7,5},{8,10},{9,11},{10,... | collective-permute-start | bytes 393224 | tf_op jit(solution)/shard_map/ppermute | solution.py:42
  20.9 1.6 %collective-permute-start.8 = (f32[128,256]{1,0:T(8,128)S(1)}, f32[128,256]{1,0:T(8,128)S(1)}, u32[]{:S(2)}, u32[]{:S(2)}) collective-permute-start(f32[128,256]{1,0:T(8,128)S(1)} %collective-permute-done.6.rest_5_), channel_id=1, source_target_pairs={{0,2},{1,3},{2,0},{3,1},{4,6},{5,7},{6,4},{7,5},{8,10},{9,11},{10,... | collective-permute-start | bytes 393224 | tf_op jit(solution)/shard_map/ppermute | solution.py:42
  22.0 1.3 %collective-permute-start.4 = (f32[128,256]{1,0:T(8,128)S(1)}, f32[128,256]{1,0:T(8,128)S(1)}, u32[]{:S(2)}, u32[]{:S(2)}) collective-permute-start(f32[128,256]{1,0:T(8,128)S(1)} %collective-permute-done.2.rest_1_), channel_id=1, source_target_pairs={{0,2},{1,3},{2,0},{3,1},{4,6},{5,7},{6,4},{7,5},{8,10},{9,11},{10,... | collective-permute-start | bytes 393224 | tf_op jit(solution)/shard_map/ppermute | solution.py:42
  22.0 1.5 %collective-permute-start.7 = (f32[128,256]{1,0:T(8,128)S(1)}, f32[128,256]{1,0:T(8,128)S(1)}, u32[]{:S(2)}, u32[]{:S(2)}) collective-permute-start(f32[128,256]{1,0:T(8,128)S(1)} %collective-permute-done.5.rest_4_), channel_id=1, source_target_pairs={{0,2},{1,3},{2,0},{3,1},{4,6},{5,7},{6,4},{7,5},{8,10},{9,11},{10,... | collective-permute-start | bytes 393224 | tf_op jit(solution)/shard_map/ppermute | solution.py:42

commit v7 on v3

--- a/solution.py
+++ b/solution.py
@@ -10,8 +10,8 @@
 
 LAGS = 128
 SAMPLES = 2048
-PHASES = 4
-LAST = 2
+PHASES = 8
+PARTS = 2
 
 
 def halves(value):
@@ -207,25 +207,25 @@
                 )
                 base += lines
 
-    spread(panel, range(PHASES), panel_ref, 0)
-    columns = PHASES * refs
+    spread(series, range(0, -lag_width, -PHASES), series_ref, 0)
+    lines, each = groups * kept, PHASES // PARTS
+    columns = each * refs
     copies = []
-    first = 0
-    for count in (groups - LAST, LAST):
-        base, lines = 2 * first * kept, count * kept
-        spread(series, range(-PHASES * first, -PHASES * (first + count), -PHASES), series_ref, base)
-        upper = product_nt(series_ref[base : base + 2 * lines, :], panel_ref[:columns, :])
-        lower = product_nt(series_ref[base : base + lines, :], panel_ref[columns:, :])
+    for part in range(PARTS):
+        base = part * 2 * columns
+        spread(panel, range(part * each, (part + 1) * each), panel_ref, base)
+        upper = product_nt(series_ref[...], panel_ref[base : base + columns, :])
+        lower = product_nt(series_ref[:lines, :], panel_ref[base + columns : base + 2 * columns, :])
         total = (upper[:lines] + upper[lines:] + lower) * (1.0 / math.sqrt(terms))
-        for i in range(count):
-            part = slice((first + i) * columns, (first + i + 1) * columns)
-            total_ref[:, part] = total[i * kept : (i + 1) * kept]
+        for group in range(groups):
+            start = (group * PARTS + part) * columns
+            place = slice(start, start + columns)
+            total_ref[:, place] = total[group * kept : (group + 1) * kept]
             copy = pltpu.make_async_copy(
-                total_ref.at[:, part], out_ref.at[:, part], done.at[first + i]
+                total_ref.at[:, place], out_ref.at[:, place], done.at[part * groups + group]
             )
             copy.start()
             copies.append(copy)
-        first += count
     for copy in copies:
         copy.wait()
 
@@ -308,7 +308,7 @@
             pltpu.VMEM((2 * lag_width // PHASES * kept, lags * segments * samples), jnp.bfloat16),
             pltpu.VMEM((2 * PHASES * refs, lags * segments * samples), jnp.bfloat16),
             pltpu.VMEM((kept, lag_width * refs), jnp.float32),
-            pltpu.SemaphoreType.DMA((lag_width // PHASES,)),
+            pltpu.SemaphoreType.DMA((lag_width // PHASES * PARTS,)),
         ],
         compiler_params=params,
         name="correlate",

time: 26.8 us -> 26.7 us (level)
  no operation moved by 1% of the time
where the time goes in v7:
time: 26.7 us; the launch traced here: 26.5 us
  waiting for transfers between devices  12 us (45%)
  starting transfers between devices  9.43 us (35%)
  Pallas kernels  4.39 us (16%)
  local copies, waits for them, and re-layouts  0.66 us (2%)
    ppermute x2, waiting for transfers between devices, paired(): return lax.ppermute(value, ('chan', 'lag'), pairs)  6.21 us
    ppermute x7, waiting for transfers between devices, swapped(): return lax.ppermute(value, ('lag', 'seg'), pairs)  5.81 us
    ppermute x2, starting transfers between devices, paired(): return lax.ppermute(value, ('chan', 'lag'), pairs)  5.41 us
    ppermute x7, starting transfers between devices, swapped(): return lax.ppermute(value, ('lag', 'seg'), pairs)  4.02 us
    pallas_call x1, Pallas kernels, shards(): pl.pallas_call(functools.partial(corr_kernel, refs, lag_width), out_shape...  3 us
    pallas_call x1, Pallas kernels, shards(): pl.pallas_call(choose_four_kernel, out_shape=[block(rows, samples), block...  0.96 us
    unnamed x4, local copies, waits for them, and re-layouts  0.66 us
  transfers between devices with their start and end apart: 9, of which 7 were waited for; matrix products, arithmetic and copies ran while one was open for 0% of the time, Pallas kernels for 4%

profile of v7, /device:TPU:0, one launch (start us, length us, event | category | flops | bytes accessed | tf_op | source)
XLA Modules:
  0.0 26.5 jit_solution(1961221638955445864)
XLA Ops:
  0.0 0.0 copy-start
  0.0 3.0 %collective-permute-start = (f32[128,1,256]{2,1,0:T(1,128)}, f32[128,1,256]{2,1,0:T(1,128)S(1)}, u32[]{:S(2)}, u32[]{:S(2)}) collective-permute-start(f32[128,1,256]{2,1,0:T(1,128)} %records_ref.1), channel_id=1, source_target_pairs={{0,8},{2,18},{4,12},{6,22},{8,0},{10,26},{12,4},{14,30},{16,24},{1... | collective-permute-start | bytes 393224 | tf_op jit(solution)/shard_map/ppermute | solution.py:57
  3.0 0.0 copy-start.1
  3.0 0.0 copy-done
  3.0 0.7 %copy-done.1 = s32[64]{0:T(128)S(1)} copy-done((s32[64]{0:T(128)S(1)}, s32[64]{0:T(128)}, u32[]{:S(2)}) %copy-start.1) | copy-done | bytes 280
  3.7 1.0 %choose.1 = (f32[128,256]{1,0:T(8,128)S(1)}, bf16[128,256]{1,0:T(8,128)(2,1)S(1)}, bf16[128,256]{1,0:T(8,128)(2,1)S(1)}, bf16[128,64]{1,0:T(8,128)(2,1)S(1)}) custom-call(f32[128,1,256]{2,1,0:T(1,128)} %records_ref.1, s32[4,128]{1,0:T(4,128)S(1)} %bitcast.2, s32[1,64]{1,0:T(1,128)S(1)} %bitcast.3), custom_call_target="tpu_custom_call" | custom-call | tf_op jit(solution)/shard_map/choose/pallas_call | solution.py:257
  4.6 2.7 %collective-permute-done.arrived_ref = f32[128,1,256]{2,1,0:T(1,128)S(1)} collective-permute-done((f32[128,1,256]{2,1,0:T(1,128)}, f32[128,1,256]{2,1,0:T(1,128)S(1)}, u32[]{:S(2)}, u32[]{:S(2)}) %collective-permute-start) | collective-permute-done | bytes 131104 | tf_op jit(solution)/shard_map/ppermute | solution.py:57
  7.3 0.3 pick.1
  7.6 2.4 %collective-permute-start.1 = (f32[128,256]{1,0:T(8,128)S(1)}, f32[128,256]{1,0:T(8,128)S(1)}, u32[]{:S(2)}, u32[]{:S(2)}) collective-permute-start(f32[128,256]{1,0:T(8,128)S(1)} %get-tuple-element.18.sent_ref), channel_id=1, source_target_pairs={{0,16},{2,10},{4,20},{6,14},{8,24},{10,2},{12,28},{14,6},{16,0},{1... | collective-permute-start | bytes 393224 | tf_op jit(solution)/shard_map/ppermute | solution.py:57
  10.0 3.5 %collective-permute-done.1.arrived_ref = f32[128,256]{1,0:T(8,128)S(1)} collective-permute-done((f32[128,256]{1,0:T(8,128)S(1)}, f32[128,256]{1,0:T(8,128)S(1)}, u32[]{:S(2)}, u32[]{:S(2)}) %collective-permute-start.1) | collective-permute-done | bytes 131104 | tf_op jit(solution)/shard_map/ppermute | solution.py:57
  13.5 0.2 place.1
  13.7 2.9 %collective-permute-start.6 = (f32[128,256]{1,0:T(8,128)S(1)}, f32[128,256]{1,0:T(8,128)S(1)}, u32[]{:S(2)}, u32[]{:S(2)}) collective-permute-start(f32[128,256]{1,0:T(8,128)S(1)} %get-tuple-element.20), channel_id=1, source_target_pairs={{0,5},{1,4},{2,7},{3,6},{4,1},{5,0},{6,3},{7,2},{8,13},{9,12},{10,... | collective-permute-start | bytes 393224 | tf_op jit(solution)/shard_map/ppermute | solution.py:43
  16.6 0.5 %collective-permute-start.2 = (f32[128,256]{1,0:T(8,128)S(1)}, f32[128,256]{1,0:T(8,128)S(1)}, u32[]{:S(2)}, u32[]{:S(2)}) collective-permute-start(f32[128,256]{1,0:T(8,128)S(1)} %get-tuple-element.20), channel_id=1, source_target_pairs={{0,1},{1,0},{2,3},{3,2},{4,5},{5,4},{6,7},{7,6},{8,9},{9,8},{10,11... | collective-permute-start | bytes 393224 | tf_op jit(solution)/shard_map/ppermute | solution.py:43
  17.1 0.2 collective-permute-start.5
  17.2 0.0 collective-permute-start.3
  17.2 3.6 %collective-permute-done.6.rest_5_ = f32[128,256]{1,0:T(8,128)S(1)} collective-permute-done((f32[128,256]{1,0:T(8,128)S(1)}, f32[128,256]{1,0:T(8,128)S(1)}, u32[]{:S(2)}, u32[]{:S(2)}) %collective-permute-start.6) | collective-permute-done | bytes 131104 | tf_op jit(solution)/shard_map/ppermute | solution.py:43
  20.9 0.0 collective-permute-start.8
  20.9 1.1 %collective-permute-done.2.rest_1_ = f32[128,256]{1,0:T(8,128)S(1)} collective-permute-done((f32[128,256]{1,0:T(8,128)S(1)}, f32[128,256]{1,0:T(8,128)S(1)}, u32[]{:S(2)}, u32[]{:S(2)}) %collective-permute-start.2) | collective-permute-done | bytes 131104 | tf_op jit(solution)/shard_map/ppermute | solution.py:43
  22.0 0.0 collective-permute-start.4
  22.0 0.1 collective-permute-done.5.rest_4_
  22.0 0.5 %collective-permute-start.7 = (f32[128,256]{1,0:T(8,128)S(1)}, f32[128,256]{1,0:T(8,128)S(1)}, u32[]{:S(2)}, u32[]{:S(2)}) collective-permute-start(f32[128,256]{1,0:T(8,128)S(1)} %collective-permute-done.5.rest_4_), channel_id=1, source_target_pairs={{0,2},{1,3},{2,0},{3,1},{4,6},{5,7},{6,4},{7,5},{8,10},{9,11},{10,... | collective-permute-start | bytes 393224 | tf_op jit(solution)/shard_map/ppermute | solution.py:43
  22.5 0.0 collective-permute-done.3.rest_2_
  22.5 0.0 collective-permute-done.8.rest_7_
  22.5 0.8 %collective-permute-done.4.rest_3_ = f32[128,256]{1,0:T(8,128)S(1)} collective-permute-done((f32[128,256]{1,0:T(8,128)S(1)}, f32[128,256]{1,0:T(8,128)S(1)}, u32[]{:S(2)}, u32[]{:S(2)}) %collective-permute-start.4) | collective-permute-done | bytes 131104 | tf_op jit(solution)/shard_map/ppermute | solution.py:43
  23.3 0.2 collective-permute-done.7.rest_6_
  23.5 3.0 %correlate.1 = f32[64,2048]{1,0:T(8,128)} custom-call(f32[128,256]{1,0:T(8,128)S(1)} %get-tuple-element.19.rest_0_, f32[128,256]{1,0:T(8,128)S(1)} %collective-permute-done.2.rest_1_, f32[128,256]{1,0:T(8,128)S(1)} %collective-permute-done.3.rest_2_, f32[128,256]{1,0:T(8,128)S(1)} %collective-permute-done.4.rest_3_, ...), custom_call_target="tpu_custom_call" | custom-call | tf_op jit(solution)/shard_map/correlate/pallas_call | solution.py:302
Async XLA Ops:
  0.0 3.0 %copy-start = (s32[512]{0:T(512)S(1)}, s32[512]{0:T(512)}, u32[]{:S(2)}) copy-start(s32[512]{0:T(512)} %param.4) | copy-start | bytes 6148
  0.0 7.3 %collective-permute-start = (f32[128,1,256]{2,1,0:T(1,128)}, f32[128,1,256]{2,1,0:T(1,128)S(1)}, u32[]{:S(2)}, u32[]{:S(2)}) collective-permute-start(f32[128,1,256]{2,1,0:T(1,128)} %records_ref.1), channel_id=1, source_target_pairs={{0,8},{2,18},{4,12},{6,22},{8,0},{10,26},{12,4},{14,30},{16,24},{1... | collective-permute-start | bytes 393224 | tf_op jit(solution)/shard_map/ppermute | solution.py:57
  3.0 0.7 %copy-start.1 = (s32[64]{0:T(128)S(1)}, s32[64]{0:T(128)}, u32[]{:S(2)}) copy-start(s32[64]{0:T(128)} %param.5) | copy-start | bytes 772
  7.6 5.9 %collective-permute-start.1 = (f32[128,256]{1,0:T(8,128)S(1)}, f32[128,256]{1,0:T(8,128)S(1)}, u32[]{:S(2)}, u32[]{:S(2)}) collective-permute-start(f32[128,256]{1,0:T(8,128)S(1)} %get-tuple-element.18.sent_ref), channel_id=1, source_target_pairs={{0,16},{2,10},{4,20},{6,14},{8,24},{10,2},{12,28},{14,6},{16,0},{1... | collective-permute-start | bytes 393224 | tf_op jit(solution)/shard_map/ppermute | solution.py:57
  13.7 7.2 %collective-permute-start.6 = (f32[128,256]{1,0:T(8,128)S(1)}, f32[128,256]{1,0:T(8,128)S(1)}, u32[]{:S(2)}, u32[]{:S(2)}) collective-permute-start(f32[128,256]{1,0:T(8,128)S(1)} %get-tuple-element.20), channel_id=1, source_target_pairs={{0,5},{1,4},{2,7},{3,6},{4,1},{5,0},{6,3},{7,2},{8,13},{9,12},{10,... | collective-permute-start | bytes 393224 | tf_op jit(solution)/shard_map/ppermute | solution.py:43
  16.6 5.4 %collective-permute-start.2 = (f32[128,256]{1,0:T(8,128)S(1)}, f32[128,256]{1,0:T(8,128)S(1)}, u32[]{:S(2)}, u32[]{:S(2)}) collective-permute-start(f32[128,256]{1,0:T(8,128)S(1)} %get-tuple-element.20), channel_id=1, source_target_pairs={{0,1},{1,0},{2,3},{3,2},{4,5},{5,4},{6,7},{7,6},{8,9},{9,8},{10,11... | collective-permute-start | bytes 393224 | tf_op jit(solution)/shard_map/ppermute | solution.py:43
  17.1 5.0 %collective-permute-start.5 = (f32[128,256]{1,0:T(8,128)S(1)}, f32[128,256]{1,0:T(8,128)S(1)}, u32[]{:S(2)}, u32[]{:S(2)}) collective-permute-start(f32[128,256]{1,0:T(8,128)S(1)} %get-tuple-element.19.rest_0_), channel_id=1, source_target_pairs={{0,4},{1,5},{2,6},{3,7},{4,0},{5,1},{6,2},{7,3},{8,12},{9,13},{10,... | collective-permute-start | bytes 393224 | tf_op jit(solution)/shard_map/ppermute | solution.py:43
  17.2 5.3 %collective-permute-start.3 = (f32[128,256]{1,0:T(8,128)S(1)}, f32[128,256]{1,0:T(8,128)S(1)}, u32[]{:S(2)}, u32[]{:S(2)}) collective-permute-start(f32[128,256]{1,0:T(8,128)S(1)} %get-tuple-element.19.rest_0_), channel_id=1, source_target_pairs={{0,2},{1,3},{2,0},{3,1},{4,6},{5,7},{6,4},{7,5},{8,10},{9,11},{10,... | collective-permute-start | bytes 393224 | tf_op jit(solution)/shard_map/ppermute | solution.py:43
  20.9 1.6 %collective-permute-start.8 = (f32[128,256]{1,0:T(8,128)S(1)}, f32[128,256]{1,0:T(8,128)S(1)}, u32[]{:S(2)}, u32[]{:S(2)}) collective-permute-start(f32[128,256]{1,0:T(8,128)S(1)} %collective-permute-done.6.rest_5_), channel_id=1, source_target_pairs={{0,2},{1,3},{2,0},{3,1},{4,6},{5,7},{6,4},{7,5},{8,10},{9,11},{10,... | collective-permute-start | bytes 393224 | tf_op jit(solution)/shard_map/ppermute | solution.py:43
  22.0 1.3 %collective-permute-start.4 = (f32[128,256]{1,0:T(8,128)S(1)}, f32[128,256]{1,0:T(8,128)S(1)}, u32[]{:S(2)}, u32[]{:S(2)}) collective-permute-start(f32[128,256]{1,0:T(8,128)S(1)} %collective-permute-done.2.rest_1_), channel_id=1, source_target_pairs={{0,2},{1,3},{2,0},{3,1},{4,6},{5,7},{6,4},{7,5},{8,10},{9,11},{10,... | collective-permute-start | bytes 393224 | tf_op jit(solution)/shard_map/ppermute | solution.py:43
  22.0 1.5 %collective-permute-start.7 = (f32[128,256]{1,0:T(8,128)S(1)}, f32[128,256]{1,0:T(8,128)S(1)}, u32[]{:S(2)}, u32[]{:S(2)}) collective-permute-start(f32[128,256]{1,0:T(8,128)S(1)} %collective-permute-done.5.rest_4_), channel_id=1, source_target_pairs={{0,2},{1,3},{2,0},{3,1},{4,6},{5,7},{6,4},{7,5},{8,10},{9,11},{10,... | collective-permute-start | bytes 393224 | tf_op jit(solution)/shard_map/ppermute | solution.py:43

commit v8 on v6

--- a/solution.py
+++ b/solution.py
@@ -90,7 +90,7 @@
     refs = refs_ref.shape[1]
     me = lax.axis_index("chan")
     odd = lax.rem(lax.axis_index("lag"), 2)
-    near, far = 1 + odd, 2 - odd
+    near, far = 2 - odd, 1 + odd
     line = lax.broadcasted_iota(jnp.int32, (rows, 2 * rows), 0)
 
     def pool(owner):
@@ -239,7 +239,7 @@
 
     shapes = [block(kept + refs, samples)] * segments
     if peers == 4:
-        first = paired(records_owned, (1, 2))
+        first = paired(records_owned, (2, 1))
         half = rows // 2
         whole = pl.BlockSpec(memory_space=pltpu.VMEM)
         own, send, keep, take = pl.pallas_call(
@@ -257,7 +257,7 @@
         )(pltpu.with_memory_space_constraint(records_owned, pltpu.HBM), lists, wanted)
         results = [block(half + refs, samples), block(rows, samples)]
         sent, base = call(pick_kernel, "pick", results, own, first, send, keep)
-        placed = call(place_four_kernel, "place", shapes, base, take, sent, paired(sent, (2, 1)))
+        placed = call(place_four_kernel, "place", shapes, base, take, sent, paired(sent, (1, 2)))
     else:
         packed, panel = call(
             pack_kernel,

time: 26.7 us -> 26.6 us (level)
  waiting for transfers between devices: 12 us -> 10.7 us
  starting transfers between devices: 9.43 us -> 10.6 us
    ppermute x2, starting transfers between devices: 5.41 us -> 6.56 us  [paired(): return lax.ppermute(value, ('chan', 'lag'), pairs)]
    ppermute x2, waiting for transfers between devices: 6.21 us -> 5.15 us  [paired(): return lax.ppermute(value, ('chan', 'lag'), pairs)]
  transfers between devices with their start and end apart: 9 -> 9, of which waited for: 7 -> 6; matrix products, arithmetic and copies ran while one was open for 0% -> 0% of each run, Pallas kernels for 4% -> 4%
where the time goes in v8:
time: 26.6 us; the launch traced here: 26.5 us
  waiting for transfers between devices  10.7 us (40%)
  starting transfers between devices  10.6 us (40%)
  Pallas kernels  4.41 us (17%)
  local copies, waits for them, and re-layouts  0.66 us (2%)
    ppermute x2, starting transfers between devices, paired(): return lax.ppermute(value, ('chan', 'lag'), pairs)  6.56 us
    ppermute x7, waiting for transfers between devices, swapped(): return lax.ppermute(value, ('lag', 'seg'), pairs)  5.6 us
    ppermute x2, waiting for transfers between devices, paired(): return lax.ppermute(value, ('chan', 'lag'), pairs)  5.15 us
    ppermute x7, starting transfers between devices, swapped(): return lax.ppermute(value, ('lag', 'seg'), pairs)  4.07 us
    pallas_call x1, Pallas kernels, shards(): pl.pallas_call(functools.partial(corr_kernel, refs, lag_width), out_shape...  3.01 us
    pallas_call x1, Pallas kernels, shards(): pl.pallas_call(choose_four_kernel, out_shape=[block(rows, samples), block...  0.96 us
    unnamed x4, local copies, waits for them, and re-layouts  0.66 us
  transfers between devices with their start and end apart: 9, of which 6 were waited for; matrix products, arithmetic and copies ran while one was open for 0% of the time, Pallas kernels for 4%

profile of v8, /device:TPU:0, one launch (start us, length us, event | category | flops | bytes accessed | tf_op | source)
XLA Modules:
  0.0 26.5 jit_solution(17337838739090030840)
XLA Ops:
  0.0 0.0 copy-start
  0.0 4.0 %collective-permute-start = (f32[128,1,256]{2,1,0:T(1,128)}, f32[128,1,256]{2,1,0:T(1,128)S(1)}, u32[]{:S(2)}, u32[]{:S(2)}) collective-permute-start(f32[128,1,256]{2,1,0:T(1,128)} %records_ref.1), channel_id=1, source_target_pairs={{0,16},{2,10},{4,20},{6,14},{8,24},{10,2},{12,28},{14,6},{16,0},{1... | collective-permute-start | bytes 393224 | tf_op jit(solution)/shard_map/ppermute | solution.py:56
  4.0 0.0 copy-start.1
  4.0 0.0 copy-done
  4.0 0.7 %copy-done.1 = s32[64]{0:T(128)S(1)} copy-done((s32[64]{0:T(128)S(1)}, s32[64]{0:T(128)}, u32[]{:S(2)}) %copy-start.1) | copy-done | bytes 280
  4.7 1.0 %choose.1 = (f32[128,256]{1,0:T(8,128)S(1)}, bf16[128,256]{1,0:T(8,128)(2,1)S(1)}, bf16[128,256]{1,0:T(8,128)(2,1)S(1)}, bf16[128,64]{1,0:T(8,128)(2,1)S(1)}) custom-call(f32[128,1,256]{2,1,0:T(1,128)} %records_ref.1, s32[4,128]{1,0:T(4,128)S(1)} %bitcast.2, s32[1,64]{1,0:T(1,128)S(1)} %bitcast.3), custom_call_target="tpu_custom_call" | custom-call | tf_op jit(solution)/shard_map/choose/pallas_call | solution.py:245
  5.7 1.6 %collective-permute-done.arrived_ref = f32[128,1,256]{2,1,0:T(1,128)S(1)} collective-permute-done((f32[128,1,256]{2,1,0:T(1,128)}, f32[128,1,256]{2,1,0:T(1,128)S(1)}, u32[]{:S(2)}, u32[]{:S(2)}) %collective-permute-start) | collective-permute-done | bytes 131104 | tf_op jit(solution)/shard_map/ppermute | solution.py:56
  7.2 0.3 %pick.1 = (f32[128,256]{1,0:T(8,128)S(1)}, f32[128,256]{1,0:T(8,128)S(1)}) custom-call(f32[128,256]{1,0:T(8,128)S(1)} %get-tuple-element.13.own_ref, f32[128,1,256]{2,1,0:T(1,128)S(1)} %collective-permute-done.arrived_ref, bf16[128,256]{1,0:T(8,128)(2,1)S(1)} %get-tuple-element.14.send_ref, bf16[128,256]{1,0:T(8,128)(2,1)S(1)} %get-tuple-element.15.keep_ref), custom_call_target="tpu_custom_call" | custom-call | tf_op jit(solution)/shard_map/pick/pallas_call | solution.py:238
  7.5 2.5 %collective-permute-start.1 = (f32[128,256]{1,0:T(8,128)S(1)}, f32[128,256]{1,0:T(8,128)S(1)}, u32[]{:S(2)}, u32[]{:S(2)}) collective-permute-start(f32[128,256]{1,0:T(8,128)S(1)} %get-tuple-element.18.sent_ref), channel_id=1, source_target_pairs={{0,8},{2,18},{4,12},{6,22},{8,0},{10,26},{12,4},{14,30},{16,24},{1... | collective-permute-start | bytes 393224 | tf_op jit(solution)/shard_map/ppermute | solution.py:56
  10.0 3.6 %collective-permute-done.1.arrived_ref = f32[128,256]{1,0:T(8,128)S(1)} collective-permute-done((f32[128,256]{1,0:T(8,128)S(1)}, f32[128,256]{1,0:T(8,128)S(1)}, u32[]{:S(2)}, u32[]{:S(2)}) %collective-permute-start.1) | collective-permute-done | bytes 131104 | tf_op jit(solution)/shard_map/ppermute | solution.py:56
  13.6 0.2 place.1
  13.8 2.6 %collective-permute-start.6 = (f32[128,256]{1,0:T(8,128)S(1)}, f32[128,256]{1,0:T(8,128)S(1)}, u32[]{:S(2)}, u32[]{:S(2)}) collective-permute-start(f32[128,256]{1,0:T(8,128)S(1)} %get-tuple-element.20), channel_id=1, source_target_pairs={{0,5},{1,4},{2,7},{3,6},{4,1},{5,0},{6,3},{7,2},{8,13},{9,12},{10,... | collective-permute-start | bytes 393224 | tf_op jit(solution)/shard_map/ppermute | solution.py:42
  16.4 0.5 %collective-permute-start.2 = (f32[128,256]{1,0:T(8,128)S(1)}, f32[128,256]{1,0:T(8,128)S(1)}, u32[]{:S(2)}, u32[]{:S(2)}) collective-permute-start(f32[128,256]{1,0:T(8,128)S(1)} %get-tuple-element.20), channel_id=1, source_target_pairs={{0,1},{1,0},{2,3},{3,2},{4,5},{5,4},{6,7},{7,6},{8,9},{9,8},{10,11... | collective-permute-start | bytes 393224 | tf_op jit(solution)/shard_map/ppermute | solution.py:42
  16.9 0.5 %collective-permute-start.5 = (f32[128,256]{1,0:T(8,128)S(1)}, f32[128,256]{1,0:T(8,128)S(1)}, u32[]{:S(2)}, u32[]{:S(2)}) collective-permute-start(f32[128,256]{1,0:T(8,128)S(1)} %get-tuple-element.19.rest_0_), channel_id=1, source_target_pairs={{0,4},{1,5},{2,6},{3,7},{4,0},{5,1},{6,2},{7,3},{8,12},{9,13},{10,... | collective-permute-start | bytes 393224 | tf_op jit(solution)/shard_map/ppermute | solution.py:42
  17.3 0.0 collective-permute-start.3
  17.3 3.8 %collective-permute-done.6.rest_5_ = f32[128,256]{1,0:T(8,128)S(1)} collective-permute-done((f32[128,256]{1,0:T(8,128)S(1)}, f32[128,256]{1,0:T(8,128)S(1)}, u32[]{:S(2)}, u32[]{:S(2)}) %collective-permute-start.6) | collective-permute-done | bytes 131104 | tf_op jit(solution)/shard_map/ppermute | solution.py:42
  21.1 0.0 collective-permute-start.8
  21.1 0.8 %collective-permute-done.2.rest_1_ = f32[128,256]{1,0:T(8,128)S(1)} collective-permute-done((f32[128,256]{1,0:T(8,128)S(1)}, f32[128,256]{1,0:T(8,128)S(1)}, u32[]{:S(2)}, u32[]{:S(2)}) %collective-permute-start.2) | collective-permute-done | bytes 131104 | tf_op jit(solution)/shard_map/ppermute | solution.py:42
  21.9 0.0 collective-permute-start.4
  21.9 0.0 collective-permute-done.5.rest_4_
  21.9 0.5 %collective-permute-start.7 = (f32[128,256]{1,0:T(8,128)S(1)}, f32[128,256]{1,0:T(8,128)S(1)}, u32[]{:S(2)}, u32[]{:S(2)}) collective-permute-start(f32[128,256]{1,0:T(8,128)S(1)} %collective-permute-done.5.rest_4_), channel_id=1, source_target_pairs={{0,2},{1,3},{2,0},{3,1},{4,6},{5,7},{6,4},{7,5},{8,10},{9,11},{10,... | collective-permute-start | bytes 393224 | tf_op jit(solution)/shard_map/ppermute | solution.py:42
  22.4 0.0 collective-permute-done.3.rest_2_
  22.4 0.0 collective-permute-done.8.rest_7_
  22.5 0.8 %collective-permute-done.4.rest_3_ = f32[128,256]{1,0:T(8,128)S(1)} collective-permute-done((f32[128,256]{1,0:T(8,128)S(1)}, f32[128,256]{1,0:T(8,128)S(1)}, u32[]{:S(2)}, u32[]{:S(2)}) %collective-permute-start.4) | collective-permute-done | bytes 131104 | tf_op jit(solution)/shard_map/ppermute | solution.py:42
  23.3 0.2 collective-permute-done.7.rest_6_
  23.5 3.0 %correlate.1 = f32[64,2048]{1,0:T(8,128)} custom-call(f32[128,256]{1,0:T(8,128)S(1)} %get-tuple-element.19.rest_0_, f32[128,256]{1,0:T(8,128)S(1)} %collective-permute-done.2.rest_1_, f32[128,256]{1,0:T(8,128)S(1)} %collective-permute-done.3.rest_2_, f32[128,256]{1,0:T(8,128)S(1)} %collective-permute-done.4.rest_3_, ...), custom_call_target="tpu_custom_call" | custom-call | tf_op jit(solution)/shard_map/correlate/pallas_call | solution.py:290
Async XLA Ops:
  0.0 4.0 %copy-start = (s32[512]{0:T(512)S(1)}, s32[512]{0:T(512)}, u32[]{:S(2)}) copy-start(s32[512]{0:T(512)} %param.4) | copy-start | bytes 6148
  0.0 7.2 %collective-permute-start = (f32[128,1,256]{2,1,0:T(1,128)}, f32[128,1,256]{2,1,0:T(1,128)S(1)}, u32[]{:S(2)}, u32[]{:S(2)}) collective-permute-start(f32[128,1,256]{2,1,0:T(1,128)} %records_ref.1), channel_id=1, source_target_pairs={{0,16},{2,10},{4,20},{6,14},{8,24},{10,2},{12,28},{14,6},{16,0},{1... | collective-permute-start | bytes 393224 | tf_op jit(solution)/shard_map/ppermute | solution.py:56
  4.0 0.7 %copy-start.1 = (s32[64]{0:T(128)S(1)}, s32[64]{0:T(128)}, u32[]{:S(2)}) copy-start(s32[64]{0:T(128)} %param.5) | copy-start | bytes 772
  7.5 6.1 %collective-permute-start.1 = (f32[128,256]{1,0:T(8,128)S(1)}, f32[128,256]{1,0:T(8,128)S(1)}, u32[]{:S(2)}, u32[]{:S(2)}) collective-permute-start(f32[128,256]{1,0:T(8,128)S(1)} %get-tuple-element.18.sent_ref), channel_id=1, source_target_pairs={{0,8},{2,18},{4,12},{6,22},{8,0},{10,26},{12,4},{14,30},{16,24},{1... | collective-permute-start | bytes 393224 | tf_op jit(solution)/shard_map/ppermute | solution.py:56
  13.8 7.3 %collective-permute-start.6 = (f32[128,256]{1,0:T(8,128)S(1)}, f32[128,256]{1,0:T(8,128)S(1)}, u32[]{:S(2)}, u32[]{:S(2)}) collective-permute-start(f32[128,256]{1,0:T(8,128)S(1)} %get-tuple-element.20), channel_id=1, source_target_pairs={{0,5},{1,4},{2,7},{3,6},{4,1},{5,0},{6,3},{7,2},{8,13},{9,12},{10,... | collective-permute-start | bytes 393224 | tf_op jit(solution)/shard_map/ppermute | solution.py:42
  16.4 5.6 %collective-permute-start.2 = (f32[128,256]{1,0:T(8,128)S(1)}, f32[128,256]{1,0:T(8,128)S(1)}, u32[]{:S(2)}, u32[]{:S(2)}) collective-permute-start(f32[128,256]{1,0:T(8,128)S(1)} %get-tuple-element.20), channel_id=1, source_target_pairs={{0,1},{1,0},{2,3},{3,2},{4,5},{5,4},{6,7},{7,6},{8,9},{9,8},{10,11... | collective-permute-start | bytes 393224 | tf_op jit(solution)/shard_map/ppermute | solution.py:42
  16.9 5.1 %collective-permute-start.5 = (f32[128,256]{1,0:T(8,128)S(1)}, f32[128,256]{1,0:T(8,128)S(1)}, u32[]{:S(2)}, u32[]{:S(2)}) collective-permute-start(f32[128,256]{1,0:T(8,128)S(1)} %get-tuple-element.19.rest_0_), channel_id=1, source_target_pairs={{0,4},{1,5},{2,6},{3,7},{4,0},{5,1},{6,2},{7,3},{8,12},{9,13},{10,... | collective-permute-start | bytes 393224 | tf_op jit(solution)/shard_map/ppermute | solution.py:42
  17.3 5.1 %collective-permute-start.3 = (f32[128,256]{1,0:T(8,128)S(1)}, f32[128,256]{1,0:T(8,128)S(1)}, u32[]{:S(2)}, u32[]{:S(2)}) collective-permute-start(f32[128,256]{1,0:T(8,128)S(1)} %get-tuple-element.19.rest_0_), channel_id=1, source_target_pairs={{0,2},{1,3},{2,0},{3,1},{4,6},{5,7},{6,4},{7,5},{8,10},{9,11},{10,... | collective-permute-start | bytes 393224 | tf_op jit(solution)/shard_map/ppermute | solution.py:42
  21.1 1.3 %collective-permute-start.8 = (f32[128,256]{1,0:T(8,128)S(1)}, f32[128,256]{1,0:T(8,128)S(1)}, u32[]{:S(2)}, u32[]{:S(2)}) collective-permute-start(f32[128,256]{1,0:T(8,128)S(1)} %collective-permute-done.6.rest_5_), channel_id=1, source_target_pairs={{0,2},{1,3},{2,0},{3,1},{4,6},{5,7},{6,4},{7,5},{8,10},{9,11},{10,... | collective-permute-start | bytes 393224 | tf_op jit(solution)/shard_map/ppermute | solution.py:42
  21.9 1.3 %collective-permute-start.4 = (f32[128,256]{1,0:T(8,128)S(1)}, f32[128,256]{1,0:T(8,128)S(1)}, u32[]{:S(2)}, u32[]{:S(2)}) collective-permute-start(f32[128,256]{1,0:T(8,128)S(1)} %collective-permute-done.2.rest_1_), channel_id=1, source_target_pairs={{0,2},{1,3},{2,0},{3,1},{4,6},{5,7},{6,4},{7,5},{8,10},{9,11},{10,... | collective-permute-start | bytes 393224 | tf_op jit(solution)/shard_map/ppermute | solution.py:42
  21.9 1.5 %collective-permute-start.7 = (f32[128,256]{1,0:T(8,128)S(1)}, f32[128,256]{1,0:T(8,128)S(1)}, u32[]{:S(2)}, u32[]{:S(2)}) collective-permute-start(f32[128,256]{1,0:T(8,128)S(1)} %collective-permute-done.5.rest_4_), channel_id=1, source_target_pairs={{0,2},{1,3},{2,0},{3,1},{4,6},{5,7},{6,4},{7,5},{8,10},{9,11},{10,... | collective-permute-start | bytes 393224 | tf_op jit(solution)/shard_map/ppermute | solution.py:42

commit v9 on v7

--- a/solution.py
+++ b/solution.py
@@ -91,7 +91,7 @@
     refs = refs_ref.shape[1]
     me = lax.axis_index("chan")
     odd = lax.rem(lax.axis_index("lag"), 2)
-    near, far = 1 + odd, 2 - odd
+    near, far = 2 - odd, 1 + odd
     line = lax.broadcasted_iota(jnp.int32, (rows, 2 * rows), 0)
 
     def pool(owner):
@@ -251,7 +251,7 @@
 
     shapes = [block(kept + refs, samples)] * segments
     if peers == 4:
-        first = paired(records_owned, (1, 2))
+        first = paired(records_owned, (2, 1))
         half = rows // 2
         whole = pl.BlockSpec(memory_space=pltpu.VMEM)
         own, send, keep, take = pl.pallas_call(
@@ -269,7 +269,7 @@
         )(pltpu.with_memory_space_constraint(records_owned, pltpu.HBM), lists, wanted)
         results = [block(half + refs, samples), block(rows, samples)]
         sent, base = call(pick_kernel, "pick", results, own, first, send, keep)
-        placed = call(place_four_kernel, "place", shapes, base, take, sent, paired(sent, (2, 1)))
+        placed = call(place_four_kernel, "place", shapes, base, take, sent, paired(sent, (1, 2)))
     else:
         packed, panel = call(
             pack_kernel,

time: 26.7 us -> 26.6 us (level)
  waiting for transfers between devices: 12 us -> 10.7 us
  starting transfers between devices: 9.43 us -> 10.6 us
    ppermute x2, starting transfers between devices: 5.41 us -> 6.56 us  [paired(): return lax.ppermute(value, ('chan', 'lag'), pairs)]
    ppermute x2, waiting for transfers between devices: 6.21 us -> 5.15 us  [paired(): return lax.ppermute(value, ('chan', 'lag'), pairs)]
  transfers between devices with their start and end apart: 9 -> 9, of which waited for: 7 -> 6; matrix products, arithmetic and copies ran while one was open for 0% -> 0% of each run, Pallas kernels for 4% -> 4%
where the time goes in v9:
time: 26.6 us; the launch traced here: 26.5 us
  waiting for transfers between devices  10.7 us (40%)
  starting transfers between devices  10.6 us (40%)
  Pallas kernels  4.39 us (17%)
  local copies, waits for them, and re-layouts  0.66 us (2%)
    ppermute x2, starting transfers between devices, paired(): return lax.ppermute(value, ('chan', 'lag'), pairs)  6.56 us
    ppermute x7, waiting for transfers between devices, swapped(): return lax.ppermute(value, ('lag', 'seg'), pairs)  5.6 us
    ppermute x2, waiting for transfers between devices, paired(): return lax.ppermute(value, ('chan', 'lag'), pairs)  5.15 us
    ppermute x7, starting transfers between devices, swapped(): return lax.ppermute(value, ('lag', 'seg'), pairs)  4.07 us
    pallas_call x1, Pallas kernels, shards(): pl.pallas_call(functools.partial(corr_kernel, refs, lag_width), out_shape...  3 us
    pallas_call x1, Pallas kernels, shards(): pl.pallas_call(choose_four_kernel, out_shape=[block(rows, samples), block...  0.96 us
    unnamed x4, local copies, waits for them, and re-layouts  0.66 us
  transfers between devices with their start and end apart: 9, of which 6 were waited for; matrix products, arithmetic and copies ran while one was open for 0% of the time, Pallas kernels for 4%

profile of v9, /device:TPU:0, one launch (start us, length us, event | category | flops | bytes accessed | tf_op | source)
XLA Modules:
  0.0 26.5 jit_solution(16943311175427951700)
XLA Ops:
  0.0 0.0 copy-start
  0.0 4.0 %collective-permute-start = (f32[128,1,256]{2,1,0:T(1,128)}, f32[128,1,256]{2,1,0:T(1,128)S(1)}, u32[]{:S(2)}, u32[]{:S(2)}) collective-permute-start(f32[128,1,256]{2,1,0:T(1,128)} %records_ref.1), channel_id=1, source_target_pairs={{0,16},{2,10},{4,20},{6,14},{8,24},{10,2},{12,28},{14,6},{16,0},{1... | collective-permute-start | bytes 393224 | tf_op jit(solution)/shard_map/ppermute | solution.py:57
  4.0 0.0 copy-start.1
  4.0 0.0 copy-done
  4.0 0.7 %copy-done.1 = s32[64]{0:T(128)S(1)} copy-done((s32[64]{0:T(128)S(1)}, s32[64]{0:T(128)}, u32[]{:S(2)}) %copy-start.1) | copy-done | bytes 280
  4.7 1.0 %choose.1 = (f32[128,256]{1,0:T(8,128)S(1)}, bf16[128,256]{1,0:T(8,128)(2,1)S(1)}, bf16[128,256]{1,0:T(8,128)(2,1)S(1)}, bf16[128,64]{1,0:T(8,128)(2,1)S(1)}) custom-call(f32[128,1,256]{2,1,0:T(1,128)} %records_ref.1, s32[4,128]{1,0:T(4,128)S(1)} %bitcast.2, s32[1,64]{1,0:T(1,128)S(1)} %bitcast.3), custom_call_target="tpu_custom_call" | custom-call | tf_op jit(solution)/shard_map/choose/pallas_call | solution.py:257
  5.7 1.6 %collective-permute-done.arrived_ref = f32[128,1,256]{2,1,0:T(1,128)S(1)} collective-permute-done((f32[128,1,256]{2,1,0:T(1,128)}, f32[128,1,256]{2,1,0:T(1,128)S(1)}, u32[]{:S(2)}, u32[]{:S(2)}) %collective-permute-start) | collective-permute-done | bytes 131104 | tf_op jit(solution)/shard_map/ppermute | solution.py:57
  7.2 0.3 %pick.1 = (f32[128,256]{1,0:T(8,128)S(1)}, f32[128,256]{1,0:T(8,128)S(1)}) custom-call(f32[128,256]{1,0:T(8,128)S(1)} %get-tuple-element.13.own_ref, f32[128,1,256]{2,1,0:T(1,128)S(1)} %collective-permute-done.arrived_ref, bf16[128,256]{1,0:T(8,128)(2,1)S(1)} %get-tuple-element.14.send_ref, bf16[128,256]{1,0:T(8,128)(2,1)S(1)} %get-tuple-element.15.keep_ref), custom_call_target="tpu_custom_call" | custom-call | tf_op jit(solution)/shard_map/pick/pallas_call | solution.py:250
  7.5 2.5 %collective-permute-start.1 = (f32[128,256]{1,0:T(8,128)S(1)}, f32[128,256]{1,0:T(8,128)S(1)}, u32[]{:S(2)}, u32[]{:S(2)}) collective-permute-start(f32[128,256]{1,0:T(8,128)S(1)} %get-tuple-element.18.sent_ref), channel_id=1, source_target_pairs={{0,8},{2,18},{4,12},{6,22},{8,0},{10,26},{12,4},{14,30},{16,24},{1... | collective-permute-start | bytes 393224 | tf_op jit(solution)/shard_map/ppermute | solution.py:57
  10.0 3.6 %collective-permute-done.1.arrived_ref = f32[128,256]{1,0:T(8,128)S(1)} collective-permute-done((f32[128,256]{1,0:T(8,128)S(1)}, f32[128,256]{1,0:T(8,128)S(1)}, u32[]{:S(2)}, u32[]{:S(2)}) %collective-permute-start.1) | collective-permute-done | bytes 131104 | tf_op jit(solution)/shard_map/ppermute | solution.py:57
  13.6 0.2 place.1
  13.8 2.6 %collective-permute-start.6 = (f32[128,256]{1,0:T(8,128)S(1)}, f32[128,256]{1,0:T(8,128)S(1)}, u32[]{:S(2)}, u32[]{:S(2)}) collective-permute-start(f32[128,256]{1,0:T(8,128)S(1)} %get-tuple-element.20), channel_id=1, source_target_pairs={{0,5},{1,4},{2,7},{3,6},{4,1},{5,0},{6,3},{7,2},{8,13},{9,12},{10,... | collective-permute-start | bytes 393224 | tf_op jit(solution)/shard_map/ppermute | solution.py:43
  16.4 0.5 %collective-permute-start.2 = (f32[128,256]{1,0:T(8,128)S(1)}, f32[128,256]{1,0:T(8,128)S(1)}, u32[]{:S(2)}, u32[]{:S(2)}) collective-permute-start(f32[128,256]{1,0:T(8,128)S(1)} %get-tuple-element.20), channel_id=1, source_target_pairs={{0,1},{1,0},{2,3},{3,2},{4,5},{5,4},{6,7},{7,6},{8,9},{9,8},{10,11... | collective-permute-start | bytes 393224 | tf_op jit(solution)/shard_map/ppermute | solution.py:43
  16.9 0.5 %collective-permute-start.5 = (f32[128,256]{1,0:T(8,128)S(1)}, f32[128,256]{1,0:T(8,128)S(1)}, u32[]{:S(2)}, u32[]{:S(2)}) collective-permute-start(f32[128,256]{1,0:T(8,128)S(1)} %get-tuple-element.19.rest_0_), channel_id=1, source_target_pairs={{0,4},{1,5},{2,6},{3,7},{4,0},{5,1},{6,2},{7,3},{8,12},{9,13},{10,... | collective-permute-start | bytes 393224 | tf_op jit(solution)/shard_map/ppermute | solution.py:43
  17.3 0.0 collective-permute-start.3
  17.3 3.8 %collective-permute-done.6.rest_5_ = f32[128,256]{1,0:T(8,128)S(1)} collective-permute-done((f32[128,256]{1,0:T(8,128)S(1)}, f32[128,256]{1,0:T(8,128)S(1)}, u32[]{:S(2)}, u32[]{:S(2)}) %collective-permute-start.6) | collective-permute-done | bytes 131104 | tf_op jit(solution)/shard_map/ppermute | solution.py:43
  21.1 0.0 collective-permute-start.8
  21.1 0.8 %collective-permute-done.2.rest_1_ = f32[128,256]{1,0:T(8,128)S(1)} collective-permute-done((f32[128,256]{1,0:T(8,128)S(1)}, f32[128,256]{1,0:T(8,128)S(1)}, u32[]{:S(2)}, u32[]{:S(2)}) %collective-permute-start.2) | collective-permute-done | bytes 131104 | tf_op jit(solution)/shard_map/ppermute | solution.py:43
  21.9 0.0 collective-permute-start.4
  21.9 0.0 collective-permute-done.5.rest_4_
  21.9 0.5 %collective-permute-start.7 = (f32[128,256]{1,0:T(8,128)S(1)}, f32[128,256]{1,0:T(8,128)S(1)}, u32[]{:S(2)}, u32[]{:S(2)}) collective-permute-start(f32[128,256]{1,0:T(8,128)S(1)} %collective-permute-done.5.rest_4_), channel_id=1, source_target_pairs={{0,2},{1,3},{2,0},{3,1},{4,6},{5,7},{6,4},{7,5},{8,10},{9,11},{10,... | collective-permute-start | bytes 393224 | tf_op jit(solution)/shard_map/ppermute | solution.py:43
  22.4 0.0 collective-permute-done.3.rest_2_
  22.4 0.0 collective-permute-done.8.rest_7_
  22.5 0.8 %collective-permute-done.4.rest_3_ = f32[128,256]{1,0:T(8,128)S(1)} collective-permute-done((f32[128,256]{1,0:T(8,128)S(1)}, f32[128,256]{1,0:T(8,128)S(1)}, u32[]{:S(2)}, u32[]{:S(2)}) %collective-permute-start.4) | collective-permute-done | bytes 131104 | tf_op jit(solution)/shard_map/ppermute | solution.py:43
  23.3 0.2 collective-permute-done.7.rest_6_
  23.5 3.0 %correlate.1 = f32[64,2048]{1,0:T(8,128)} custom-call(f32[128,256]{1,0:T(8,128)S(1)} %get-tuple-element.19.rest_0_, f32[128,256]{1,0:T(8,128)S(1)} %collective-permute-done.2.rest_1_, f32[128,256]{1,0:T(8,128)S(1)} %collective-permute-done.3.rest_2_, f32[128,256]{1,0:T(8,128)S(1)} %collective-permute-done.4.rest_3_, ...), custom_call_target="tpu_custom_call" | custom-call | tf_op jit(solution)/shard_map/correlate/pallas_call | solution.py:302
Async XLA Ops:
  0.0 4.0 %copy-start = (s32[512]{0:T(512)S(1)}, s32[512]{0:T(512)}, u32[]{:S(2)}) copy-start(s32[512]{0:T(512)} %param.4) | copy-start | bytes 6148
  0.0 7.2 %collective-permute-start = (f32[128,1,256]{2,1,0:T(1,128)}, f32[128,1,256]{2,1,0:T(1,128)S(1)}, u32[]{:S(2)}, u32[]{:S(2)}) collective-permute-start(f32[128,1,256]{2,1,0:T(1,128)} %records_ref.1), channel_id=1, source_target_pairs={{0,16},{2,10},{4,20},{6,14},{8,24},{10,2},{12,28},{14,6},{16,0},{1... | collective-permute-start | bytes 393224 | tf_op jit(solution)/shard_map/ppermute | solution.py:57
  4.0 0.7 %copy-start.1 = (s32[64]{0:T(128)S(1)}, s32[64]{0:T(128)}, u32[]{:S(2)}) copy-start(s32[64]{0:T(128)} %param.5) | copy-start | bytes 772
  7.5 6.1 %collective-permute-start.1 = (f32[128,256]{1,0:T(8,128)S(1)}, f32[128,256]{1,0:T(8,128)S(1)}, u32[]{:S(2)}, u32[]{:S(2)}) collective-permute-start(f32[128,256]{1,0:T(8,128)S(1)} %get-tuple-element.18.sent_ref), channel_id=1, source_target_pairs={{0,8},{2,18},{4,12},{6,22},{8,0},{10,26},{12,4},{14,30},{16,24},{1... | collective-permute-start | bytes 393224 | tf_op jit(solution)/shard_map/ppermute | solution.py:57
  13.8 7.3 %collective-permute-start.6 = (f32[128,256]{1,0:T(8,128)S(1)}, f32[128,256]{1,0:T(8,128)S(1)}, u32[]{:S(2)}, u32[]{:S(2)}) collective-permute-start(f32[128,256]{1,0:T(8,128)S(1)} %get-tuple-element.20), channel_id=1, source_target_pairs={{0,5},{1,4},{2,7},{3,6},{4,1},{5,0},{6,3},{7,2},{8,13},{9,12},{10,... | collective-permute-start | bytes 393224 | tf_op jit(solution)/shard_map/ppermute | solution.py:43
  16.4 5.6 %collective-permute-start.2 = (f32[128,256]{1,0:T(8,128)S(1)}, f32[128,256]{1,0:T(8,128)S(1)}, u32[]{:S(2)}, u32[]{:S(2)}) collective-permute-start(f32[128,256]{1,0:T(8,128)S(1)} %get-tuple-element.20), channel_id=1, source_target_pairs={{0,1},{1,0},{2,3},{3,2},{4,5},{5,4},{6,7},{7,6},{8,9},{9,8},{10,11... | collective-permute-start | bytes 393224 | tf_op jit(solution)/shard_map/ppermute | solution.py:43
  16.9 5.1 %collective-permute-start.5 = (f32[128,256]{1,0:T(8,128)S(1)}, f32[128,256]{1,0:T(8,128)S(1)}, u32[]{:S(2)}, u32[]{:S(2)}) collective-permute-start(f32[128,256]{1,0:T(8,128)S(1)} %get-tuple-element.19.rest_0_), channel_id=1, source_target_pairs={{0,4},{1,5},{2,6},{3,7},{4,0},{5,1},{6,2},{7,3},{8,12},{9,13},{10,... | collective-permute-start | bytes 393224 | tf_op jit(solution)/shard_map/ppermute | solution.py:43
  17.3 5.1 %collective-permute-start.3 = (f32[128,256]{1,0:T(8,128)S(1)}, f32[128,256]{1,0:T(8,128)S(1)}, u32[]{:S(2)}, u32[]{:S(2)}) collective-permute-start(f32[128,256]{1,0:T(8,128)S(1)} %get-tuple-element.19.rest_0_), channel_id=1, source_target_pairs={{0,2},{1,3},{2,0},{3,1},{4,6},{5,7},{6,4},{7,5},{8,10},{9,11},{10,... | collective-permute-start | bytes 393224 | tf_op jit(solution)/shard_map/ppermute | solution.py:43
  21.1 1.3 %collective-permute-start.8 = (f32[128,256]{1,0:T(8,128)S(1)}, f32[128,256]{1,0:T(8,128)S(1)}, u32[]{:S(2)}, u32[]{:S(2)}) collective-permute-start(f32[128,256]{1,0:T(8,128)S(1)} %collective-permute-done.6.rest_5_), channel_id=1, source_target_pairs={{0,2},{1,3},{2,0},{3,1},{4,6},{5,7},{6,4},{7,5},{8,10},{9,11},{10,... | collective-permute-start | bytes 393224 | tf_op jit(solution)/shard_map/ppermute | solution.py:43
  21.9 1.3 %collective-permute-start.4 = (f32[128,256]{1,0:T(8,128)S(1)}, f32[128,256]{1,0:T(8,128)S(1)}, u32[]{:S(2)}, u32[]{:S(2)}) collective-permute-start(f32[128,256]{1,0:T(8,128)S(1)} %collective-permute-done.2.rest_1_), channel_id=1, source_target_pairs={{0,2},{1,3},{2,0},{3,1},{4,6},{5,7},{6,4},{7,5},{8,10},{9,11},{10,... | collective-permute-start | bytes 393224 | tf_op jit(solution)/shard_map/ppermute | solution.py:43
  21.9 1.5 %collective-permute-start.7 = (f32[128,256]{1,0:T(8,128)S(1)}, f32[128,256]{1,0:T(8,128)S(1)}, u32[]{:S(2)}, u32[]{:S(2)}) collective-permute-start(f32[128,256]{1,0:T(8,128)S(1)} %collective-permute-done.5.rest_4_), channel_id=1, source_target_pairs={{0,2},{1,3},{2,0},{3,1},{4,6},{5,7},{6,4},{7,5},{8,10},{9,11},{10,... | collective-permute-start | bytes 393224 | tf_op jit(solution)/shard_map/ppermute | solution.py:43

commit v10 on v8

--- a/solution.py
+++ b/solution.py
@@ -194,20 +194,22 @@
     terms = SAMPLES - LAGS
     times = lax.broadcasted_iota(jnp.int32, panel.shape, 1)
     panel = jnp.where(times < terms, panel, 0.0)
-    series = pltpu.roll(series, samples - lax.axis_index("lag") * lag_width, 1)
     groups = lag_width // PHASES
 
-    def spread(value, count, step, out_ref):
+    def spread(value, count, step, out_ref, begin=0):
         lines = value.shape[0]
         for half, part in enumerate(halves(value)):
             for i in range(count):
                 start = (half * count + i) * lines
                 out_ref[start : start + lines, :] = (
-                    pltpu.roll(part, (i * step) % samples, 1) if i else part
+                    part
+                    if not i and step > 0
+                    else pltpu.roll(part, begin + i * step, 1)
                 )
 
     spread(panel, PHASES, 1, panel_ref)
-    spread(series, groups, -PHASES, series_ref)
+    begin = -lax.axis_index("lag") * lag_width
+    spread(series, groups, -PHASES, series_ref, begin + samples)
     lines, columns = groups * kept, PHASES * refs
     upper = product_nt(series_ref[...], panel_ref[:columns, :])
     lower = product_nt(series_ref[:lines, :], panel_ref[columns:, :])

time: 26.6 us -> 26.9 us (1.011)
  no operation moved by 1% of the time
where the time goes in v10:
time: 26.9 us; the launch traced here: 26.7 us
  waiting for transfers between devices  10.7 us (40%)
  starting transfers between devices  10.6 us (39%)
  Pallas kernels  4.67 us (17%)
  local copies, waits for them, and re-layouts  0.66 us (2%)
    ppermute x2, starting transfers between devices, paired(): return lax.ppermute(value, ('chan', 'lag'), pairs)  6.56 us
    ppermute x7, waiting for transfers between devices, swapped(): return lax.ppermute(value, ('lag', 'seg'), pairs)  5.6 us
    ppermute x2, waiting for transfers between devices, paired(): return lax.ppermute(value, ('chan', 'lag'), pairs)  5.15 us
    ppermute x7, starting transfers between devices, swapped(): return lax.ppermute(value, ('lag', 'seg'), pairs)  4.07 us
    pallas_call x1, Pallas kernels, shards(): pl.pallas_call(functools.partial(corr_kernel, refs, lag_width), out_shape...  3.27 us
    pallas_call x1, Pallas kernels, shards(): pl.pallas_call(choose_four_kernel, out_shape=[block(rows, samples), block...  0.96 us
    unnamed x4, local copies, waits for them, and re-layouts  0.66 us
  transfers between devices with their start and end apart: 9, of which 6 were waited for; matrix products, arithmetic and copies ran while one was open for 0% of the time, Pallas kernels for 4%

profile of v10, /device:TPU:0, one launch (start us, length us, event | category | flops | bytes accessed | tf_op | source)
XLA Modules:
  0.0 26.7 jit_solution(9525302266743843490)
XLA Ops:
  0.0 0.0 copy-start
  0.0 4.0 %collective-permute-start = (f32[128,1,256]{2,1,0:T(1,128)}, f32[128,1,256]{2,1,0:T(1,128)S(1)}, u32[]{:S(2)}, u32[]{:S(2)}) collective-permute-start(f32[128,1,256]{2,1,0:T(1,128)} %records_ref.1), channel_id=1, source_target_pairs={{0,16},{2,10},{4,20},{6,14},{8,24},{10,2},{12,28},{14,6},{16,0},{1... | collective-permute-start | bytes 393224 | tf_op jit(solution)/shard_map/ppermute | solution.py:56
  4.0 0.0 copy-start.1
  4.0 0.0 copy-done
  4.0 0.7 %copy-done.1 = s32[64]{0:T(128)S(1)} copy-done((s32[64]{0:T(128)S(1)}, s32[64]{0:T(128)}, u32[]{:S(2)}) %copy-start.1) | copy-done | bytes 280
  4.7 1.0 %choose.1 = (f32[128,256]{1,0:T(8,128)S(1)}, bf16[128,256]{1,0:T(8,128)(2,1)S(1)}, bf16[128,256]{1,0:T(8,128)(2,1)S(1)}, bf16[128,64]{1,0:T(8,128)(2,1)S(1)}) custom-call(f32[128,1,256]{2,1,0:T(1,128)} %records_ref.1, s32[4,128]{1,0:T(4,128)S(1)} %bitcast.2, s32[1,64]{1,0:T(1,128)S(1)} %bitcast.3), custom_call_target="tpu_custom_call" | custom-call | tf_op jit(solution)/shard_map/choose/pallas_call | solution.py:247
  5.7 1.6 %collective-permute-done.arrived_ref = f32[128,1,256]{2,1,0:T(1,128)S(1)} collective-permute-done((f32[128,1,256]{2,1,0:T(1,128)}, f32[128,1,256]{2,1,0:T(1,128)S(1)}, u32[]{:S(2)}, u32[]{:S(2)}) %collective-permute-start) | collective-permute-done | bytes 131104 | tf_op jit(solution)/shard_map/ppermute | solution.py:56
  7.2 0.3 pick.1
  7.5 2.5 %collective-permute-start.1 = (f32[128,256]{1,0:T(8,128)S(1)}, f32[128,256]{1,0:T(8,128)S(1)}, u32[]{:S(2)}, u32[]{:S(2)}) collective-permute-start(f32[128,256]{1,0:T(8,128)S(1)} %get-tuple-element.18.sent_ref), channel_id=1, source_target_pairs={{0,8},{2,18},{4,12},{6,22},{8,0},{10,26},{12,4},{14,30},{16,24},{1... | collective-permute-start | bytes 393224 | tf_op jit(solution)/shard_map/ppermute | solution.py:56
  10.0 3.6 %collective-permute-done.1.arrived_ref = f32[128,256]{1,0:T(8,128)S(1)} collective-permute-done((f32[128,256]{1,0:T(8,128)S(1)}, f32[128,256]{1,0:T(8,128)S(1)}, u32[]{:S(2)}, u32[]{:S(2)}) %collective-permute-start.1) | collective-permute-done | bytes 131104 | tf_op jit(solution)/shard_map/ppermute | solution.py:56
  13.6 0.2 place.1
  13.8 2.6 %collective-permute-start.6 = (f32[128,256]{1,0:T(8,128)S(1)}, f32[128,256]{1,0:T(8,128)S(1)}, u32[]{:S(2)}, u32[]{:S(2)}) collective-permute-start(f32[128,256]{1,0:T(8,128)S(1)} %get-tuple-element.20), channel_id=1, source_target_pairs={{0,5},{1,4},{2,7},{3,6},{4,1},{5,0},{6,3},{7,2},{8,13},{9,12},{10,... | collective-permute-start | bytes 393224 | tf_op jit(solution)/shard_map/ppermute | solution.py:42
  16.4 0.5 %collective-permute-start.2 = (f32[128,256]{1,0:T(8,128)S(1)}, f32[128,256]{1,0:T(8,128)S(1)}, u32[]{:S(2)}, u32[]{:S(2)}) collective-permute-start(f32[128,256]{1,0:T(8,128)S(1)} %get-tuple-element.20), channel_id=1, source_target_pairs={{0,1},{1,0},{2,3},{3,2},{4,5},{5,4},{6,7},{7,6},{8,9},{9,8},{10,11... | collective-permute-start | bytes 393224 | tf_op jit(solution)/shard_map/ppermute | solution.py:42
  16.9 0.5 %collective-permute-start.5 = (f32[128,256]{1,0:T(8,128)S(1)}, f32[128,256]{1,0:T(8,128)S(1)}, u32[]{:S(2)}, u32[]{:S(2)}) collective-permute-start(f32[128,256]{1,0:T(8,128)S(1)} %get-tuple-element.19.rest_0_), channel_id=1, source_target_pairs={{0,4},{1,5},{2,6},{3,7},{4,0},{5,1},{6,2},{7,3},{8,12},{9,13},{10,... | collective-permute-start | bytes 393224 | tf_op jit(solution)/shard_map/ppermute | solution.py:42
  17.3 0.0 collective-permute-start.3
  17.3 3.8 %collective-permute-done.6.rest_5_ = f32[128,256]{1,0:T(8,128)S(1)} collective-permute-done((f32[128,256]{1,0:T(8,128)S(1)}, f32[128,256]{1,0:T(8,128)S(1)}, u32[]{:S(2)}, u32[]{:S(2)}) %collective-permute-start.6) | collective-permute-done | bytes 131104 | tf_op jit(solution)/shard_map/ppermute | solution.py:42
  21.1 0.0 collective-permute-start.8
  21.1 0.8 %collective-permute-done.2.rest_1_ = f32[128,256]{1,0:T(8,128)S(1)} collective-permute-done((f32[128,256]{1,0:T(8,128)S(1)}, f32[128,256]{1,0:T(8,128)S(1)}, u32[]{:S(2)}, u32[]{:S(2)}) %collective-permute-start.2) | collective-permute-done | bytes 131104 | tf_op jit(solution)/shard_map/ppermute | solution.py:42
  21.9 0.0 collective-permute-start.4
  21.9 0.0 collective-permute-done.5.rest_4_
  21.9 0.5 %collective-permute-start.7 = (f32[128,256]{1,0:T(8,128)S(1)}, f32[128,256]{1,0:T(8,128)S(1)}, u32[]{:S(2)}, u32[]{:S(2)}) collective-permute-start(f32[128,256]{1,0:T(8,128)S(1)} %collective-permute-done.5.rest_4_), channel_id=1, source_target_pairs={{0,2},{1,3},{2,0},{3,1},{4,6},{5,7},{6,4},{7,5},{8,10},{9,11},{10,... | collective-permute-start | bytes 393224 | tf_op jit(solution)/shard_map/ppermute | solution.py:42
  22.4 0.0 collective-permute-done.3.rest_2_
  22.4 0.0 collective-permute-done.8.rest_7_
  22.5 0.8 %collective-permute-done.4.rest_3_ = f32[128,256]{1,0:T(8,128)S(1)} collective-permute-done((f32[128,256]{1,0:T(8,128)S(1)}, f32[128,256]{1,0:T(8,128)S(1)}, u32[]{:S(2)}, u32[]{:S(2)}) %collective-permute-start.4) | collective-permute-done | bytes 131104 | tf_op jit(solution)/shard_map/ppermute | solution.py:42
  23.3 0.2 collective-permute-done.7.rest_6_
  23.5 3.3 %correlate.1 = f32[64,2048]{1,0:T(8,128)} custom-call(f32[128,256]{1,0:T(8,128)S(1)} %get-tuple-element.19.rest_0_, f32[128,256]{1,0:T(8,128)S(1)} %collective-permute-done.2.rest_1_, f32[128,256]{1,0:T(8,128)S(1)} %collective-permute-done.3.rest_2_, f32[128,256]{1,0:T(8,128)S(1)} %collective-permute-done.4.rest_3_, ...), custom_call_target="tpu_custom_call" | custom-call | tf_op jit(solution)/shard_map/correlate/pallas_call | solution.py:292
Async XLA Ops:
  0.0 4.0 %copy-start = (s32[512]{0:T(512)S(1)}, s32[512]{0:T(512)}, u32[]{:S(2)}) copy-start(s32[512]{0:T(512)} %param.4) | copy-start | bytes 6148
  0.0 7.2 %collective-permute-start = (f32[128,1,256]{2,1,0:T(1,128)}, f32[128,1,256]{2,1,0:T(1,128)S(1)}, u32[]{:S(2)}, u32[]{:S(2)}) collective-permute-start(f32[128,1,256]{2,1,0:T(1,128)} %records_ref.1), channel_id=1, source_target_pairs={{0,16},{2,10},{4,20},{6,14},{8,24},{10,2},{12,28},{14,6},{16,0},{1... | collective-permute-start | bytes 393224 | tf_op jit(solution)/shard_map/ppermute | solution.py:56
  4.0 0.7 %copy-start.1 = (s32[64]{0:T(128)S(1)}, s32[64]{0:T(128)}, u32[]{:S(2)}) copy-start(s32[64]{0:T(128)} %param.5) | copy-start | bytes 772
  7.5 6.1 %collective-permute-start.1 = (f32[128,256]{1,0:T(8,128)S(1)}, f32[128,256]{1,0:T(8,128)S(1)}, u32[]{:S(2)}, u32[]{:S(2)}) collective-permute-start(f32[128,256]{1,0:T(8,128)S(1)} %get-tuple-element.18.sent_ref), channel_id=1, source_target_pairs={{0,8},{2,18},{4,12},{6,22},{8,0},{10,26},{12,4},{14,30},{16,24},{1... | collective-permute-start | bytes 393224 | tf_op jit(solution)/shard_map/ppermute | solution.py:56
  13.8 7.3 %collective-permute-start.6 = (f32[128,256]{1,0:T(8,128)S(1)}, f32[128,256]{1,0:T(8,128)S(1)}, u32[]{:S(2)}, u32[]{:S(2)}) collective-permute-start(f32[128,256]{1,0:T(8,128)S(1)} %get-tuple-element.20), channel_id=1, source_target_pairs={{0,5},{1,4},{2,7},{3,6},{4,1},{5,0},{6,3},{7,2},{8,13},{9,12},{10,... | collective-permute-start | bytes 393224 | tf_op jit(solution)/shard_map/ppermute | solution.py:42
  16.4 5.6 %collective-permute-start.2 = (f32[128,256]{1,0:T(8,128)S(1)}, f32[128,256]{1,0:T(8,128)S(1)}, u32[]{:S(2)}, u32[]{:S(2)}) collective-permute-start(f32[128,256]{1,0:T(8,128)S(1)} %get-tuple-element.20), channel_id=1, source_target_pairs={{0,1},{1,0},{2,3},{3,2},{4,5},{5,4},{6,7},{7,6},{8,9},{9,8},{10,11... | collective-permute-start | bytes 393224 | tf_op jit(solution)/shard_map/ppermute | solution.py:42
  16.9 5.1 %collective-permute-start.5 = (f32[128,256]{1,0:T(8,128)S(1)}, f32[128,256]{1,0:T(8,128)S(1)}, u32[]{:S(2)}, u32[]{:S(2)}) collective-permute-start(f32[128,256]{1,0:T(8,128)S(1)} %get-tuple-element.19.rest_0_), channel_id=1, source_target_pairs={{0,4},{1,5},{2,6},{3,7},{4,0},{5,1},{6,2},{7,3},{8,12},{9,13},{10,... | collective-permute-start | bytes 393224 | tf_op jit(solution)/shard_map/ppermute | solution.py:42
  17.3 5.1 %collective-permute-start.3 = (f32[128,256]{1,0:T(8,128)S(1)}, f32[128,256]{1,0:T(8,128)S(1)}, u32[]{:S(2)}, u32[]{:S(2)}) collective-permute-start(f32[128,256]{1,0:T(8,128)S(1)} %get-tuple-element.19.rest_0_), channel_id=1, source_target_pairs={{0,2},{1,3},{2,0},{3,1},{4,6},{5,7},{6,4},{7,5},{8,10},{9,11},{10,... | collective-permute-start | bytes 393224 | tf_op jit(solution)/shard_map/ppermute | solution.py:42
  21.1 1.3 %collective-permute-start.8 = (f32[128,256]{1,0:T(8,128)S(1)}, f32[128,256]{1,0:T(8,128)S(1)}, u32[]{:S(2)}, u32[]{:S(2)}) collective-permute-start(f32[128,256]{1,0:T(8,128)S(1)} %collective-permute-done.6.rest_5_), channel_id=1, source_target_pairs={{0,2},{1,3},{2,0},{3,1},{4,6},{5,7},{6,4},{7,5},{8,10},{9,11},{10,... | collective-permute-start | bytes 393224 | tf_op jit(solution)/shard_map/ppermute | solution.py:42
  21.9 1.3 %collective-permute-start.4 = (f32[128,256]{1,0:T(8,128)S(1)}, f32[128,256]{1,0:T(8,128)S(1)}, u32[]{:S(2)}, u32[]{:S(2)}) collective-permute-start(f32[128,256]{1,0:T(8,128)S(1)} %collective-permute-done.2.rest_1_), channel_id=1, source_target_pairs={{0,2},{1,3},{2,0},{3,1},{4,6},{5,7},{6,4},{7,5},{8,10},{9,11},{10,... | collective-permute-start | bytes 393224 | tf_op jit(solution)/shard_map/ppermute | solution.py:42
  21.9 1.5 %collective-permute-start.7 = (f32[128,256]{1,0:T(8,128)S(1)}, f32[128,256]{1,0:T(8,128)S(1)}, u32[]{:S(2)}, u32[]{:S(2)}) collective-permute-start(f32[128,256]{1,0:T(8,128)S(1)} %collective-permute-done.5.rest_4_), channel_id=1, source_target_pairs={{0,2},{1,3},{2,0},{3,1},{4,6},{5,7},{6,4},{7,5},{8,10},{9,11},{10,... | collective-permute-start | bytes 393224 | tf_op jit(solution)/shard_map/ppermute | solution.py:42
